TPU v7x, 32 devices: a whole 2x2x4 slice. The times are simulated.
32 devices in a mesh: rep: 4 (over x, core), shard: 8 (over z, y).
Axes of the slice: x: 2, y: 2, z: 4, core: 2. Of those that a mesh axis runs over, the one named last changes fastest.
Arguments:
- tokens: bfloat16 [8, 4, 1024, 768], P('shard', 'rep'), may hold values from -6 to 6
- cotangent: bfloat16 [8, 4, 1024, 768], P('shard', 'rep'), may hold values from -6 to 6
- teacher: bfloat16 [8, 4, 1024, 768], P('shard', 'rep'), may hold values from -20 to 20
- valid_mask: int32 [8, 4, 1024], P('shard', 'rep'), may hold values 0 or 1
- valid_count: int32 [], replicated, may hold values from 16384 to 32767
- query_weight: bfloat16 [768, 768], P('shard'), may hold values from -0.3125 to 0.3125
- query_bias: bfloat16 [768], P('shard'), may hold values from -0.8984375 to 0.8984375
- key_weight: bfloat16 [768, 768], P('shard'), may hold values from -0.21875 to 0.21875
- value_weight: bfloat16 [768, 768], P('shard'), may hold values from -0.21875 to 0.21875
- value_bias: bfloat16 [768], P('shard'), may hold values from -0.29882812 to 0.29882812
- attn_weight: bfloat16 [768, 768], P('shard'), may hold values from -2.5 to 2.5
- attn_bias: bfloat16 [768], P('shard'), may hold values from -0.59765625 to 0.59765625
- first_gain: bfloat16 [768], P('shard'), may hold values from 0.5 to 1.5
- first_shift: bfloat16 [768], P('shard'), may hold values from -0.59765625 to 0.59765625
- up_weight: bfloat16 [768, 3072], P('shard'), may hold values from -0.21875 to 0.21875
- up_bias: bfloat16 [3072], P('shard'), may hold values from -0.59765625 to 0.59765625
- down_weight: bfloat16 [3072, 768], P('shard'), may hold values from -0.109375 to 0.109375
- down_bias: bfloat16 [768], P('shard'), may hold values from -0.59765625 to 0.59765625
- second_gain: bfloat16 [768], P('shard'), may hold values from 0.5 to 1.5
- second_shift: bfloat16 [768], P('shard'), may hold values from -0.59765625 to 0.59765625
Outputs:
- layer_out: bfloat16 [8, 4, 1024, 768], P('shard', 'rep')
- loss_value: float32 [], replicated
- tokens_grad: bfloat16 [8, 4, 1024, 768], P('shard', 'rep')
- query_weight_grad: float32 [768, 768], P('shard')
- query_bias_grad: float32 [768], P('shard')
- key_weight_grad: float32 [768, 768], P('shard')
- value_weight_grad: float32 [768, 768], P('shard')
- value_bias_grad: float32 [768], P('shard')
- attn_weight_grad: float32 [768, 768], P('shard')
- attn_bias_grad: float32 [768], P('shard')
- first_gain_grad: float32 [768], P('shard')
- first_shift_grad: float32 [768], P('shard')
- up_weight_grad: float32 [768, 3072], P('shard')
- up_bias_grad: float32 [3072], P('shard')
- down_weight_grad: float32 [3072, 768], P('shard')
- down_bias_grad: float32 [768], P('shard')
- second_gain_grad: float32 [768], P('shard')
- second_shift_grad: float32 [768], P('shard')
All inputs are finite; a program needn't handle non-finite values. No bound on the sum of `valid_mask` on one device may be relied on, other than what follows from the above.
Results may differ from a plain program's by a relative error of at most 0.019.
Values may be sent and summed in bfloat16 or wider, within the bound.
A program may use at most 192 MiB of HBM per device.

v0:
```python
from functools import partial
import math

import jax
import jax.numpy as jnp
from jax import lax
from jax.sharding import PartitionSpec as P

HDIM = 64
PPIECE = 512
CLEN = 256
QBLK = 512


EPSILON = 1e-05
NEGATIVE = -1e30


def matmul(left_matrix, right_matrix):
    return jnp.dot(left_matrix, right_matrix, preferred_element_type=jnp.float32)


def inner_rows(left_matrix, right_matrix):
    return lax.dot_general(
        left_matrix, right_matrix, (((0,), (0,)), ((), ())), preferred_element_type=jnp.float32
    )


def times_transpose(left_matrix, right_matrix):
    return lax.dot_general(
        left_matrix, right_matrix, (((1,), (1,)), ((), ())), preferred_element_type=jnp.float32
    )


def column_sum(values):
    return jnp.sum(values.astype(jnp.float32), axis=0)


def layer_norm(values, norm_gain, norm_shift):
    centered = values - jnp.mean(values, axis=-1, keepdims=True)
    spread = lax.rsqrt(jnp.mean(centered * centered, axis=-1, keepdims=True) + EPSILON)
    normed = centered * spread
    return (normed, spread, normed * norm_gain.astype(jnp.float32) + norm_shift.astype(jnp.float32))


def norm_back(incoming, normed, spread, norm_gain):
    scaled = incoming * norm_gain.astype(jnp.float32)
    centered = scaled - jnp.mean(scaled, axis=-1, keepdims=True)
    return (centered - normed * jnp.mean(scaled * normed, axis=-1, keepdims=True)) * spread


def to_pairs(values, pair_count, pair_width):
    return values.reshape(values.shape[0], pair_count, pair_width).transpose(1, 0, 2)


def from_pairs(values):
    return values.transpose(1, 0, 2).reshape(values.shape[1], values.shape[0] * values.shape[2])


def pair_scores(query_block, key_pair, allowed_block, score_scale):
    heads_query = query_block.reshape(query_block.shape[0], 2, HDIM)
    heads_key = key_pair.reshape(key_pair.shape[0], 2, HDIM)
    raw_scores = (
        jnp.einsum("qhd,khd->hqk", heads_query, heads_key, preferred_element_type=jnp.float32)
        * score_scale
    )
    return jnp.where(allowed_block[None], raw_scores, NEGATIVE)


def local(
    tokens,
    cotangent,
    teacher,
    valid_mask,
    valid_count,
    query_weight,
    query_bias,
    key_weight,
    value_weight,
    value_bias,
    attn_weight,
    attn_bias,
    first_gain,
    first_shift,
    up_weight,
    up_bias,
    down_weight,
    down_bias,
    second_gain,
    second_shift,
):
    (
        query_full,
        query_bias_full,
        key_full,
        value_full,
        value_bias_full,
        attn_full,
        attn_bias_full,
        first_gain_full,
        first_shift_full,
        up_full,
        up_bias_full,
        down_full,
        down_bias_full,
        second_gain_full,
        second_shift_full,
    ) = (
        lax.all_gather(query_weight, "shard", axis=0, tiled=True),
        lax.all_gather(query_bias, "shard", axis=0, tiled=True),
        lax.all_gather(key_weight, "shard", axis=0, tiled=True),
        lax.all_gather(value_weight, "shard", axis=0, tiled=True),
        lax.all_gather(value_bias, "shard", axis=0, tiled=True),
        lax.all_gather(attn_weight, "shard", axis=0, tiled=True),
        lax.all_gather(attn_bias, "shard", axis=0, tiled=True),
        lax.all_gather(first_gain, "shard", axis=0, tiled=True),
        lax.all_gather(first_shift, "shard", axis=0, tiled=True),
        lax.all_gather(up_weight, "shard", axis=0, tiled=True),
        lax.all_gather(up_bias, "shard", axis=0, tiled=True),
        lax.all_gather(down_weight, "shard", axis=0, tiled=True),
        lax.all_gather(down_bias, "shard", axis=0, tiled=True),
        lax.all_gather(second_gain, "shard", axis=0, tiled=True),
        lax.all_gather(second_shift, "shard", axis=0, tiled=True),
    )
    row_total = tokens.shape[2]
    model_width = tokens.shape[3]
    member_count = lax.axis_size("rep")
    member_index = lax.axis_index("rep")
    piece_rows = PPIECE
    cont_length = CLEN
    cont_count = (row_total - piece_rows) // cont_length
    block_rows = QBLK
    pair_width = 2 * HDIM
    pair_count = model_width // pair_width
    block_count = row_total // block_rows
    prompt_rows = member_count * piece_rows
    key_total = prompt_rows + cont_count * cont_length
    score_scale = 1.0 / math.sqrt(HDIM)
    inputs = tokens.reshape(row_total, model_width)
    keep_mask = valid_mask.reshape(row_total)
    queries = (matmul(inputs, query_full) + query_bias_full.astype(jnp.float32)).astype(
        jnp.bfloat16
    )
    key_rows = matmul(inputs, key_full).astype(jnp.bfloat16)
    value_rows = (matmul(inputs, value_full) + value_bias_full.astype(jnp.float32)).astype(
        jnp.bfloat16
    )
    prompt_key, prompt_value, prompt_keep = (
        lax.all_gather(key_rows[:piece_rows], "rep", axis=0, tiled=True),
        lax.all_gather(value_rows[:piece_rows], "rep", axis=0, tiled=True),
        lax.all_gather(keep_mask[:piece_rows].astype(jnp.bfloat16), "rep", axis=0, tiled=True),
    )
    all_keys = jnp.concatenate([prompt_key, key_rows[piece_rows:]], axis=0)
    all_values = jnp.concatenate([prompt_value, value_rows[piece_rows:]], axis=0)
    key_keep = jnp.concatenate([prompt_keep > 0.5, keep_mask[piece_rows:] > 0])
    row_index = jnp.arange(row_total, dtype=jnp.int32)
    key_index = jnp.arange(key_total, dtype=jnp.int32)
    in_prompt = row_index < piece_rows
    row_cont = jnp.maximum(row_index - piece_rows, 0) // cont_length
    row_group = jnp.where(in_prompt, -1, row_cont)
    row_self = jnp.where(
        in_prompt, member_index * piece_rows + row_index, prompt_rows + row_index - piece_rows
    )
    key_is_prompt = key_index < prompt_rows
    key_group = jnp.where(key_is_prompt, -2, (key_index - prompt_rows) // cont_length)
    sees = key_is_prompt[None, :] | (row_group[:, None] == key_group[None, :])
    allowed = sees & (key_keep[None, :] | (row_self[:, None] == key_index[None, :]))
    allowed_blocks = allowed.reshape(block_count, block_rows, key_total)
    query_pairs = to_pairs(queries, pair_count, pair_width)
    key_pairs = to_pairs(all_keys, pair_count, pair_width)
    value_pairs = to_pairs(all_values, pair_count, pair_width)

    def pair_forward(pair_item):
        query_pair, key_pair, value_pair = pair_item
        heads_value = value_pair.reshape(key_total, 2, HDIM)

        def block_forward(block_item):
            query_block, allowed_block = block_item
            scores = pair_scores(query_block, key_pair, allowed_block, score_scale)
            row_max = jnp.max(scores, axis=-1, keepdims=True)
            exponent = jnp.exp(scores - row_max)
            row_sum = jnp.sum(exponent, axis=-1, keepdims=True)
            probs_low = (exponent / row_sum).astype(jnp.bfloat16)
            block_mixed = jnp.einsum(
                "hqk,khd->qhd", probs_low, heads_value, preferred_element_type=jnp.float32
            )
            return (
                block_mixed.reshape(block_rows, pair_width),
                row_max[..., 0] + jnp.log(row_sum[..., 0]),
            )

        block_mixed, block_logs = lax.map(
            block_forward, (query_pair.reshape(block_count, block_rows, pair_width), allowed_blocks)
        )
        return (block_mixed.reshape(row_total, pair_width), block_logs)

    mixed_pairs, log_totals = lax.map(pair_forward, (query_pairs, key_pairs, value_pairs))
    attn_mixed = from_pairs(mixed_pairs).astype(jnp.bfloat16)
    branch = matmul(attn_mixed, attn_full) + attn_bias_full.astype(jnp.float32)
    first_sum = inputs.astype(jnp.float32) + branch
    first_normed, first_inv, hidden = layer_norm(first_sum, first_gain_full, first_shift_full)
    hidden_low = hidden.astype(jnp.bfloat16)
    up_input = matmul(hidden_low, up_full) + up_bias_full.astype(jnp.float32)
    activation_full, gelu_pull = jax.vjp(partial(jax.nn.gelu, approximate=False), up_input)
    activation = activation_full.astype(jnp.bfloat16)
    second_sum = hidden + matmul(activation, down_full) + down_bias_full.astype(jnp.float32)
    second_normed, second_inv, layer_result = layer_norm(
        second_sum, second_gain_full, second_shift_full
    )
    target = teacher.reshape(row_total, model_width).astype(jnp.float32)
    keep_rows = keep_mask.astype(jnp.float32)[:, None]
    loss_denom = valid_count.astype(jnp.float32)
    errors = layer_result - target
    local_loss = jnp.sum(keep_rows * errors * errors) / loss_denom
    total_loss = lax.psum(local_loss, ("rep", "shard"))
    layer_grad = (
        cotangent.reshape(row_total, model_width).astype(jnp.float32)
        + 2.0 * keep_rows * errors / loss_denom
    )
    (
        layer_grad,
        query_held,
        key_held,
        value_held,
        attn_held,
        up_held,
        down_held,
        first_gain_held,
        second_gain_held,
    ) = lax.optimization_barrier(
        (
            layer_grad,
            query_weight,
            key_weight,
            value_weight,
            attn_weight,
            up_weight,
            down_weight,
            first_gain,
            second_gain,
        )
    )
    (
        query_back,
        key_back,
        value_back,
        attn_back,
        up_back,
        down_back,
        first_gain_back,
        second_gain_back,
    ) = (
        lax.all_gather(query_held, "shard", axis=0, tiled=True),
        lax.all_gather(key_held, "shard", axis=0, tiled=True),
        lax.all_gather(value_held, "shard", axis=0, tiled=True),
        lax.all_gather(attn_held, "shard", axis=0, tiled=True),
        lax.all_gather(up_held, "shard", axis=0, tiled=True),
        lax.all_gather(down_held, "shard", axis=0, tiled=True),
        lax.all_gather(first_gain_held, "shard", axis=0, tiled=True),
        lax.all_gather(second_gain_held, "shard", axis=0, tiled=True),
    )
    second_gain_grad = jnp.sum(layer_grad * second_normed, axis=0)
    second_shift_grad = jnp.sum(layer_grad, axis=0)
    second_grad = norm_back(layer_grad, second_normed, second_inv, second_gain_back)
    down_delta = second_grad.astype(jnp.bfloat16)
    down_weight_grad = inner_rows(activation, down_delta)
    down_bias_grad = column_sum(down_delta)
    up_delta = gelu_pull(times_transpose(down_delta, down_back))[0].astype(jnp.bfloat16)
    up_weight_grad = inner_rows(hidden_low, up_delta)
    up_bias_grad = column_sum(up_delta)
    hidden_grad = second_grad + times_transpose(up_delta, up_back)
    first_gain_grad = jnp.sum(hidden_grad * first_normed, axis=0)
    first_shift_grad = jnp.sum(hidden_grad, axis=0)
    first_grad = norm_back(hidden_grad, first_normed, first_inv, first_gain_back)
    attn_delta = first_grad.astype(jnp.bfloat16)
    attn_weight_grad = inner_rows(attn_mixed, attn_delta)
    attn_bias_grad = column_sum(attn_delta)
    mixed_delta = times_transpose(attn_delta, attn_back).astype(jnp.bfloat16)
    delta_pairs = to_pairs(mixed_delta, pair_count, pair_width)

    def pair_backward(pair_item):
        query_pair, key_pair, value_pair, delta_pair, log_pair = pair_item
        heads_key = key_pair.reshape(key_total, 2, HDIM)
        heads_value = value_pair.reshape(key_total, 2, HDIM)

        def block_backward(carried, block_item):
            key_grad, value_grad = carried
            query_block, delta_block, log_block, allowed_block = block_item
            scores = pair_scores(query_block, key_pair, allowed_block, score_scale)
            attn_probs = jnp.where(allowed_block[None], jnp.exp(scores - log_block[..., None]), 0.0)
            heads_delta = delta_block.reshape(block_rows, 2, HDIM)
            heads_query = query_block.reshape(block_rows, 2, HDIM)
            value_term = jnp.einsum(
                "hqk,qhd->khd",
                attn_probs.astype(jnp.bfloat16),
                heads_delta,
                preferred_element_type=jnp.float32,
            )
            prob_grad = jnp.einsum(
                "qhd,khd->hqk", heads_delta, heads_value, preferred_element_type=jnp.float32
            )
            inner_sum = jnp.sum(attn_probs * prob_grad, axis=-1, keepdims=True)
            score_delta = (attn_probs * (prob_grad - inner_sum)).astype(jnp.bfloat16)
            query_term = (
                jnp.einsum(
                    "hqk,khd->qhd", score_delta, heads_key, preferred_element_type=jnp.float32
                )
                * score_scale
            )
            key_term = (
                jnp.einsum(
                    "hqk,qhd->khd", score_delta, heads_query, preferred_element_type=jnp.float32
                )
                * score_scale
            )
            key_grad = key_grad + key_term.reshape(key_total, pair_width)
            value_grad = value_grad + value_term.reshape(key_total, pair_width)
            return ((key_grad, value_grad), query_term.reshape(block_rows, pair_width))

        zero_grads = jnp.zeros((key_total, pair_width), jnp.float32)
        block_items = (
            query_pair.reshape(block_count, block_rows, pair_width),
            delta_pair.reshape(block_count, block_rows, pair_width),
            log_pair,
            allowed_blocks,
        )
        (key_grad, value_grad), query_grad = lax.scan(
            block_backward, (zero_grads, zero_grads), block_items
        )
        return (query_grad.reshape(row_total, pair_width), key_grad, value_grad)

    query_grads, key_grads, value_grads = lax.map(
        pair_backward, (query_pairs, key_pairs, value_pairs, delta_pairs, log_totals)
    )
    query_delta = from_pairs(query_grads).astype(jnp.bfloat16)
    key_grad_all = from_pairs(key_grads)
    value_grad_all = from_pairs(value_grads)
    prompt_key_grad, prompt_value_grad = (
        lax.psum_scatter(
            key_grad_all[:prompt_rows].astype(jnp.bfloat16), "rep", scatter_dimension=0, tiled=True
        ).astype(jnp.float32),
        lax.psum_scatter(
            value_grad_all[:prompt_rows].astype(jnp.bfloat16),
            "rep",
            scatter_dimension=0,
            tiled=True,
        ).astype(jnp.float32),
    )
    key_delta = jnp.concatenate([prompt_key_grad, key_grad_all[prompt_rows:]], axis=0).astype(
        jnp.bfloat16
    )
    value_delta = jnp.concatenate([prompt_value_grad, value_grad_all[prompt_rows:]], axis=0).astype(
        jnp.bfloat16
    )
    query_weight_grad = inner_rows(inputs, query_delta)
    query_bias_grad = column_sum(query_delta)
    key_weight_grad = inner_rows(inputs, key_delta)
    value_weight_grad = inner_rows(inputs, value_delta)
    value_bias_grad = column_sum(value_delta)
    input_sum = (
        first_grad
        + times_transpose(query_delta, query_back)
        + times_transpose(key_delta, key_back)
        + times_transpose(value_delta, value_back)
    )
    tokens_grad = input_sum.astype(jnp.bfloat16).reshape(tokens.shape)
    (
        owned_query,
        owned_query_bias,
        owned_key,
        owned_value,
        owned_value_bias,
        owned_attn,
        owned_attn_bias,
        owned_first_gain,
        owned_first_shift,
        owned_up,
        owned_up_bias,
        owned_down,
        owned_down_bias,
        owned_second_gain,
        owned_second_shift,
    ) = (
        lax.psum_scatter(query_weight_grad, "shard", scatter_dimension=0, tiled=True),
        lax.psum_scatter(query_bias_grad, "shard", scatter_dimension=0, tiled=True),
        lax.psum_scatter(key_weight_grad, "shard", scatter_dimension=0, tiled=True),
        lax.psum_scatter(value_weight_grad, "shard", scatter_dimension=0, tiled=True),
        lax.psum_scatter(value_bias_grad, "shard", scatter_dimension=0, tiled=True),
        lax.psum_scatter(attn_weight_grad, "shard", scatter_dimension=0, tiled=True),
        lax.psum_scatter(attn_bias_grad, "shard", scatter_dimension=0, tiled=True),
        lax.psum_scatter(first_gain_grad, "shard", scatter_dimension=0, tiled=True),
        lax.psum_scatter(first_shift_grad, "shard", scatter_dimension=0, tiled=True),
        lax.psum_scatter(up_weight_grad, "shard", scatter_dimension=0, tiled=True),
        lax.psum_scatter(up_bias_grad, "shard", scatter_dimension=0, tiled=True),
        lax.psum_scatter(down_weight_grad, "shard", scatter_dimension=0, tiled=True),
        lax.psum_scatter(down_bias_grad, "shard", scatter_dimension=0, tiled=True),
        lax.psum_scatter(second_gain_grad, "shard", scatter_dimension=0, tiled=True),
        lax.psum_scatter(second_shift_grad, "shard", scatter_dimension=0, tiled=True),
    )
    summed_grads = (
        lax.psum(owned_query.astype(jnp.bfloat16), "rep").astype(jnp.float32),
        lax.psum(owned_query_bias.astype(jnp.bfloat16), "rep").astype(jnp.float32),
        lax.psum(owned_key.astype(jnp.bfloat16), "rep").astype(jnp.float32),
        lax.psum(owned_value.astype(jnp.bfloat16), "rep").astype(jnp.float32),
        lax.psum(owned_value_bias.astype(jnp.bfloat16), "rep").astype(jnp.float32),
        lax.psum(owned_attn.astype(jnp.bfloat16), "rep").astype(jnp.float32),
        lax.psum(owned_attn_bias.astype(jnp.bfloat16), "rep").astype(jnp.float32),
        lax.psum(owned_first_gain.astype(jnp.bfloat16), "rep").astype(jnp.float32),
        lax.psum(owned_first_shift.astype(jnp.bfloat16), "rep").astype(jnp.float32),
        lax.psum(owned_up.astype(jnp.bfloat16), "rep").astype(jnp.float32),
        lax.psum(owned_up_bias.astype(jnp.bfloat16), "rep").astype(jnp.float32),
        lax.psum(owned_down.astype(jnp.bfloat16), "rep").astype(jnp.float32),
        lax.psum(owned_down_bias.astype(jnp.bfloat16), "rep").astype(jnp.float32),
        lax.psum(owned_second_gain.astype(jnp.bfloat16), "rep").astype(jnp.float32),
        lax.psum(owned_second_shift.astype(jnp.bfloat16), "rep").astype(jnp.float32),
    )
    layer_out = layer_result.astype(jnp.bfloat16).reshape(tokens.shape)
    return (
        layer_out,
        total_loss,
        tokens_grad,
        summed_grads[0],
        summed_grads[1],
        summed_grads[2],
        summed_grads[3],
        summed_grads[4],
        summed_grads[5],
        summed_grads[6],
        summed_grads[7],
        summed_grads[8],
        summed_grads[9],
        summed_grads[10],
        summed_grads[11],
        summed_grads[12],
        summed_grads[13],
        summed_grads[14],
    )


def solution(mesh):
    return jax.shard_map(
        local,
        mesh=mesh,
        in_specs=(
            P("shard", "rep", None, None),
            P("shard", "rep", None, None),
            P("shard", "rep", None, None),
            P("shard", "rep", None),
            P(),
            P("shard", None),
            P("shard"),
            P("shard", None),
            P("shard", None),
            P("shard"),
            P("shard", None),
            P("shard"),
            P("shard"),
            P("shard"),
            P("shard", None),
            P("shard"),
            P("shard", None),
            P("shard"),
            P("shard"),
            P("shard"),
        ),
        out_specs=(
            P("shard", "rep", None, None),
            P(),
            P("shard", "rep", None, None),
            P("shard", None),
            P("shard"),
            P("shard", None),
            P("shard", None),
            P("shard"),
            P("shard", None),
            P("shard"),
            P("shard"),
            P("shard"),
            P("shard", None),
            P("shard"),
            P("shard", None),
            P("shard"),
            P("shard"),
            P("shard"),
        ),
        check_vma=False,
    )
```

profile of v0, /device:TPU:0, one launch (start us, length us, event | category | flops | bytes accessed | tf_op | source)
XLA Modules:
  0.0 1979.2 jit_solution(13383275892358202138)
XLA Ops:
  18.1 39.1 %all-reduce.21 = (bf16[768]{0:T(1024)(128)(2,1)S(1)}, bf16[768]{0:T(1024)(128)(2,1)S(1)}, bf16[768]{0:T(1024)(128)(2,1)S(1)}, bf16[768]{0:T(1024)(128)(2,1)S(1)}...) all-reduce(bf16[768]{0:T(1024)(128)(2,1)S(1)} %dynamic-update-slice, ...), channel_id=1, replica_groups=mesh['rep'=4,'shard'=8] {'shard'}, use_global_device_ids=true, to_apply=%add | all-reduce | flops 6144 | bytes 24576
  61.4 34.8 %all-gather.19.cloned.1.call-done = bf16[768,768]{1,0:T(8,128)(2,1)} async-done(((bf16[96,768]{1,0:T(8,128)(2,1)}), bf16[768,768]{1,0:T(8,128)(2,1)}) %all-gather.19.cloned.1.call-update) | async-done | bytes 1179664 | tf_op jit(solution)/shard_map/all_gather | solution.py:111
  111.8 26.2 %all-gather.1 = bf16[8,1,384]{2,1,0:T(2,128)(2,1)S(1)} all-gather(bf16[1,1,384]{2,1,0:T(2,128)(2,1)S(1)} %reshape.348), channel_id=1, replica_groups=mesh['rep'=4,'shard'=8] {'shard'}, dimensions={0}, use_global_device_ids=true | all-gather | bytes 6912 | tf_op jit(solution)/shard_map/all_gather | solution.py:119
  152.4 15.3 all-gather.25.cloned.1.call-done
  178.2 20.0 %all-gather.21.cloned.1.call-done = bf16[2048,768]{1,0:T(8,128)(2,1)} async-done(((bf16[512,768]{1,0:T(8,128)(2,1)}), bf16[2048,768]{1,0:T(8,128)(2,1)}) %all-gather.21.cloned.1.call-update) | async-done | bytes 3145744 | tf_op jit(solution)/shard_map/all_gather | solution.py:149
  210.0 182.3 %while.58 = (s32[]{:T(128)}, bf16[6,1024,128]{1,2,0:T(8,128)(2,1)}, f32[6,2,2,512]{3,2,1,0:T(2,128)}, bf16[6,1024,128]{2,1,0:T(8,128)(2,1)}, bf16[6,2560,128]{1,...) while((s32[]{:T(128)}, bf16[6,1024,128]{1,2,0:T(8,128)(2,1)}, ...), condition=%wide.region_5.6_spmd.clone, body=%wide.region_0.5_spmd.clone.sunk | while | flops 715652096 | bytes 47522108 | solution.py:197
  218.1 20.8 %while.61 = (s32[]{:T(128)}, bf16[2,512,128]{2,1,0:T(8,128)(2,1)S(1)}, f32[2,2,512]{2,1,0:T(2,128)S(1)}, pred[2,512,2560]{2,1,0:T(8,128)(4,1)}, bf16[2,512,128]{...) while((s32[]{:T(128)}, ...), condition=%wide.region_4.4_spmd, body=%wide.region_1.3_spmd.sunk | while | flops 702544896 | bytes 40665188 | solution.py:192
  248.5 20.9 %while.61 = (s32[]{:T(128)}, bf16[2,512,128]{2,1,0:T(8,128)(2,1)S(1)}, f32[2,2,512]{2,1,0:T(2,128)S(1)}, pred[2,512,2560]{2,1,0:T(8,128)(4,1)}, bf16[2,512,128]{...) while((s32[]{:T(128)}, ...), condition=%wide.region_4.4_spmd, body=%wide.region_1.3_spmd.sunk | while | flops 702544896 | bytes 40665188 | solution.py:192
  278.9 20.8 %while.61 = (s32[]{:T(128)}, bf16[2,512,128]{2,1,0:T(8,128)(2,1)S(1)}, f32[2,2,512]{2,1,0:T(2,128)S(1)}, pred[2,512,2560]{2,1,0:T(8,128)(4,1)}, bf16[2,512,128]{...) while((s32[]{:T(128)}, ...), condition=%wide.region_4.4_spmd, body=%wide.region_1.3_spmd.sunk | while | flops 702544896 | bytes 40665188 | solution.py:192
  309.3 20.8 %while.61 = (s32[]{:T(128)}, bf16[2,512,128]{2,1,0:T(8,128)(2,1)S(1)}, f32[2,2,512]{2,1,0:T(2,128)S(1)}, pred[2,512,2560]{2,1,0:T(8,128)(4,1)}, bf16[2,512,128]{...) while((s32[]{:T(128)}, ...), condition=%wide.region_4.4_spmd, body=%wide.region_1.3_spmd.sunk | while | flops 702544896 | bytes 40665188 | solution.py:192
  339.7 20.8 %while.61 = (s32[]{:T(128)}, bf16[2,512,128]{2,1,0:T(8,128)(2,1)S(1)}, f32[2,2,512]{2,1,0:T(2,128)S(1)}, pred[2,512,2560]{2,1,0:T(8,128)(4,1)}, bf16[2,512,128]{...) while((s32[]{:T(128)}, ...), condition=%wide.region_4.4_spmd, body=%wide.region_1.3_spmd.sunk | while | flops 702544896 | bytes 40665188 | solution.py:192
  370.0 20.8 %while.61 = (s32[]{:T(128)}, bf16[2,512,128]{2,1,0:T(8,128)(2,1)S(1)}, f32[2,2,512]{2,1,0:T(2,128)S(1)}, pred[2,512,2560]{2,1,0:T(8,128)(4,1)}, bf16[2,512,128]{...) while((s32[]{:T(128)}, ...), condition=%wide.region_4.4_spmd, body=%wide.region_1.3_spmd.sunk | while | flops 702544896 | bytes 40665188 | solution.py:192
  397.0 37.8 %multiply_convert_fusion.1 = (bf16[1024,3072]{1,0:T(8,128)(2,1)}, f32[1024,3072]{1,0:T(8,128)}, f32[1024,3072]{1,0:T(8,128)}) fusion(f32[3072]{0:T(1024)S(1)} %bitcast.266, bf16[768,3072]{1,0:T(8,128)(2,1)} %all-gather.29.cloned.1.call-done, f32[1024,768]{0,1:T(8,128)S(1)} %get-tuple-element.587, f32[768]{0:T(1024)S(1)} %copy-done.60, ...), kind=kOutput, calls=%fused_computation.51 | convolution fusion | flops 5043388416 | bytes 39348224 | tf_op jit(solution)/shard_map/dot_general | solution.py:20
  434.8 9.8 fusion.58
  450.5 21.9 %all-reduce.20 = (bf16[768]{0:T(1024)(128)(2,1)S(1)}, bf16[768]{0:T(1024)(128)(2,1)S(1)}) all-reduce(bf16[768]{0:T(1024)(128)(2,1)S(1)} %dynamic-update-slice.8, bf16[768]{0:T(1024)(128)(2,1)S(1)} %dynamic-update-slice.9), channel_id=1, replica_groups=mesh['rep'=4,'shard'=8] {'shard'}, use_global_device_ids=true, to_apply=%add.8 | all-reduce | flops 1536 | bytes 6144
  481.7 48.1 %all-gather.33.cloned.1.call-done = bf16[3072,768]{1,0:T(8,128)(2,1)} async-done(((bf16[384,768]{1,0:T(8,128)(2,1)}), bf16[3072,768]{1,0:T(8,128)(2,1)}) %all-gather.33.cloned.1.call-update) | async-done | bytes 4718608 | tf_op jit(solution)/shard_map/all_gather | solution.py:258
  529.8 20.0 %convert_reduce_fusion = (f32[3072]{0:T(1024)}, bf16[1024,3072]{1,0:T(8,128)(2,1)}) fusion(f32[1024,3072]{1,0:T(8,128)} %get-tuple-element.570, bf16[3072,768]{1,0:T(8,128)(2,1)} %all-gather.33.cloned.1.call-done, f32[1024,768]{0,1:T(8,128)} %get-tuple-element.566, f32[1024,3072]{1,0:T(8,128)} %get-tuple-element.588, f32[3072]{0:T(1024)S(1)} %bitcast.267), kind=kOutput, calls=%fused_computation.49 | convolution fusion | flops 4886098944 | bytes 39346176 | tf_op jit(solution)/shard_map/dot_general | solution.py:30
  549.8 60.1 %all-gather.35.cloned.1.call-done = bf16[768,3072]{1,0:T(8,128)(2,1)} async-done(((bf16[96,3072]{1,0:T(8,128)(2,1)}), bf16[768,3072]{1,0:T(8,128)(2,1)}) %all-gather.35.cloned.1.call-update) | async-done | bytes 4718608 | tf_op jit(solution)/shard_map/all_gather | solution.py:257
  609.9 10.6 multiply_reduce_fusion.2
  623.8 27.5 %all-gather.37.cloned.1.call-done = bf16[768,768]{1,0:T(8,128)(2,1)} async-done(((bf16[96,768]{1,0:T(8,128)(2,1)}), bf16[768,768]{1,0:T(8,128)(2,1)}) %all-gather.37.cloned.1.call-update) | async-done | bytes 1179664 | tf_op jit(solution)/shard_map/all_gather | solution.py:256
  657.9 426.9 %while.60 = (s32[]{:T(128)}, bf16[6,1024,128]{1,2,0:T(8,128)(2,1)}, bf16[6,2560,128]{1,2,0:T(8,128)(2,1)}, bf16[6,2560,128]{1,2,0:T(8,128)(2,1)}, bf16[6,1024,12...) while((s32[]{:T(128)}, bf16[6,1024,128]{1,2,0:T(8,128)(2,1)}, ...), condition=%wide.region_20.21_spmd.clone, body=%wide.region_16.20_spmd.clone.sunk | while | flops 1718811648 | bytes 210363728 | solution.py:332
  671.4 54.0 %while.62 = (s32[]{:T(128)}, f32[2560,128]{0,1:T(8,128)}, f32[2560,128]{0,1:T(8,128)}, bf16[2,512,128]{2,1,0:T(8,128)(2,1)}, bf16[2,512,128]{2,1,0:T(8,128)(2,1)...) while((s32[]{:T(128)}, f32[2560,128]{0,1:T(8,128)}, ...), condition=%wide.region_19.19_spmd.clone, body=%wide.region_17.18_spmd.clone.sunk | while | flops 1705704448 | bytes 195318672 | solution.py:327
  706.8 7.3 multiply_reduce_fusion.10
  742.5 54.0 %while.62 = (s32[]{:T(128)}, f32[2560,128]{0,1:T(8,128)}, f32[2560,128]{0,1:T(8,128)}, bf16[2,512,128]{2,1,0:T(8,128)(2,1)}, bf16[2,512,128]{2,1,0:T(8,128)(2,1)...) while((s32[]{:T(128)}, f32[2560,128]{0,1:T(8,128)}, ...), condition=%wide.region_19.19_spmd.clone, body=%wide.region_17.18_spmd.clone.sunk | while | flops 1705704448 | bytes 195318672 | solution.py:327
  777.9 7.3 multiply_reduce_fusion.10
  813.7 54.0 %while.62 = (s32[]{:T(128)}, f32[2560,128]{0,1:T(8,128)}, f32[2560,128]{0,1:T(8,128)}, bf16[2,512,128]{2,1,0:T(8,128)(2,1)}, bf16[2,512,128]{2,1,0:T(8,128)(2,1)...) while((s32[]{:T(128)}, f32[2560,128]{0,1:T(8,128)}, ...), condition=%wide.region_19.19_spmd.clone, body=%wide.region_17.18_spmd.clone.sunk | while | flops 1705704448 | bytes 195318672 | solution.py:327
  822.3 7.3 multiply_reduce_fusion.10
  849.1 7.3 multiply_reduce_fusion.10
  884.8 54.0 %while.62 = (s32[]{:T(128)}, f32[2560,128]{0,1:T(8,128)}, f32[2560,128]{0,1:T(8,128)}, bf16[2,512,128]{2,1,0:T(8,128)(2,1)}, bf16[2,512,128]{2,1,0:T(8,128)(2,1)...) while((s32[]{:T(128)}, f32[2560,128]{0,1:T(8,128)}, ...), condition=%wide.region_19.19_spmd.clone, body=%wide.region_17.18_spmd.clone.sunk | while | flops 1705704448 | bytes 195318672 | solution.py:327
  920.2 7.3 multiply_reduce_fusion.10
  955.9 54.0 %while.62 = (s32[]{:T(128)}, f32[2560,128]{0,1:T(8,128)}, f32[2560,128]{0,1:T(8,128)}, bf16[2,512,128]{2,1,0:T(8,128)(2,1)}, bf16[2,512,128]{2,1,0:T(8,128)(2,1)...) while((s32[]{:T(128)}, f32[2560,128]{0,1:T(8,128)}, ...), condition=%wide.region_19.19_spmd.clone, body=%wide.region_17.18_spmd.clone.sunk | while | flops 1705704448 | bytes 195318672 | solution.py:327
  991.3 7.3 multiply_reduce_fusion.10
  1027.0 54.0 %while.62 = (s32[]{:T(128)}, f32[2560,128]{0,1:T(8,128)}, f32[2560,128]{0,1:T(8,128)}, bf16[2,512,128]{2,1,0:T(8,128)(2,1)}, bf16[2,512,128]{2,1,0:T(8,128)(2,1)...) while((s32[]{:T(128)}, f32[2560,128]{0,1:T(8,128)}, ...), condition=%wide.region_19.19_spmd.clone, body=%wide.region_17.18_spmd.clone.sunk | while | flops 1705704448 | bytes 195318672 | solution.py:327
  1062.4 7.3 multiply_reduce_fusion.10
  1108.0 10.2 fusion.46
  1132.1 34.3 %reduce-scatter.15.cloned.1.call-done = bf16[512,768]{0,1:T(8,128)(2,1)} async-done(((bf16[2048,768]{0,1:T(8,128)(2,1)}), bf16[512,768]{0,1:T(8,128)(2,1)}) %reduce-scatter.15.cloned.1.call-update) | async-done | bytes 786448 | tf_op jit(solution)/shard_map/reduce_scatter | solution.py:339
  1173.7 10.5 fusion.49
  1187.8 39.8 %psum.112 = f32[]{:T(128)} all-reduce(f32[]{:T(128)S(6)} %div.71), channel_id=1, replica_groups=mesh['rep'=4,'shard'=8] {'rep','shard'}, use_global_device_ids=true, to_apply=%region_11.12 | all-reduce | flops 1 | bytes 8 | tf_op jit(solution)/shard_map/psum | solution.py:215
  1235.0 46.2 %reduce-scatter.19.cloned.1.call-done = f32[96,768]{1,0:T(8,128)} async-done(((f32[768,768]{1,0:T(8,128)}), f32[96,768]{1,0:T(8,128)}) %reduce-scatter.19.cloned.1.call-update) | async-done | bytes 294928 | tf_op jit(solution)/shard_map/reduce_scatter | solution.py:389
  1282.8 69.7 %reduce-scatter.25.cloned.1.call-done = f32[96,768]{1,0:T(8,128)} async-done(((f32[768,768]{1,0:T(8,128)}), f32[96,768]{1,0:T(8,128)}) %reduce-scatter.25.cloned.1.call-update) | async-done | bytes 294928
  1354.7 37.6 %all-reduce.19 = (bf16[768]{0:T(1024)(128)(2,1)S(1)}, bf16[768]{0:T(1024)(128)(2,1)S(1)}, bf16[768]{0:T(1024)(128)(2,1)S(1)}, bf16[768]{0:T(1024)(128)(2,1)S(1)}...) all-reduce(f32[768]{0:T(1024)S(1)} %bitcast.265, ...), channel_id=6, replica_groups=mesh['rep'=4,'shard'=8] {'shard'}, use_global_device_ids=true, to_apply=%region_26.27.clone | all-reduce | flops 9216 | bytes 55296
  1404.1 114.5 %reduce-scatter.23.cloned.1.call-done = f32[384,768]{1,0:T(8,128)} async-done(((f32[3072,768]{1,0:T(8,128)}), f32[384,768]{1,0:T(8,128)}) %reduce-scatter.23.cloned.1.call-update) | async-done | bytes 1179664 | tf_op jit(solution)/shard_map/reduce_scatter | solution.py:395
  1520.7 69.5 %reduce-scatter.29.cloned.1.call-done = f32[96,768]{1,0:T(8,128)} async-done(((f32[768,768]{1,0:T(8,128)}), f32[96,768]{1,0:T(8,128)}) %reduce-scatter.29.cloned.1.call-update) | async-done | bytes 294928
  1592.0 69.8 %reduce-scatter.27.cloned.1.call-done = f32[96,768]{1,0:T(8,128)} async-done(((f32[768,768]{1,0:T(8,128)}), f32[96,768]{1,0:T(8,128)}) %reduce-scatter.27.cloned.1.call-update) | async-done | bytes 294928
  1663.6 164.2 %reduce-scatter.21.cloned.1.call-done = f32[96,3072]{1,0:T(8,128)} async-done(((f32[768,3072]{1,0:T(8,128)}), f32[96,3072]{1,0:T(8,128)}) %reduce-scatter.21.cloned.1.call-update) | async-done | bytes 1179664 | tf_op jit(solution)/shard_map/reduce_scatter | solution.py:393
  1830.0 40.2 %all-gather.41.cloned.1.call-done = bf16[768,768]{1,0:T(8,128)(2,1)} async-done(((bf16[96,768]{1,0:T(8,128)(2,1)}), bf16[768,768]{1,0:T(8,128)(2,1)}) %all-gather.41.cloned.1.call-update) | async-done | bytes 1179664 | tf_op jit(solution)/shard_map/all_gather | solution.py:254
  1874.9 37.3 %all-gather.43.cloned.1.call-done = bf16[768,768]{1,0:T(8,128)(2,1)} async-done(((bf16[96,768]{1,0:T(8,128)(2,1)}), bf16[768,768]{1,0:T(8,128)(2,1)}) %all-gather.43.cloned.1.call-update) | async-done | bytes 1179664 | tf_op jit(solution)/shard_map/all_gather | solution.py:255
  1921.0 43.5 %all-reduce.26.cloned.1.call-done = (bf16[96,768]{0,1:T(8,128)(2,1)}, bf16[96,768]{0,1:T(8,128)(2,1)}, bf16[96,768]{0,1:T(8,128)(2,1)}, bf16[96,768]{1,0:T(8,128...) async-done(((bf16[96,768]{0,1:T(8,128)(2,1)}, bf16[96,768]{0,1:T(8,128)(2,1)}, bf16[96,768]{0,1:T(8,128)(2,1)}, bf16[96,768]{1,0:T(8,128)(2,1)}, ...) | async-done | bytes 1769488 | tf_op jit(solution)/shard_map/psum | solution.py:401
  (987 shorter events, 747.1 us)
Async XLA Ops:
  7.2 50.0 %all-gather.23.cloned.1.call-start = ((), (), s32[]{:S(2)}) async-start(), calls=%async_computation.11 | async-start | bytes 1327104 | tf_op jit(solution)/shard_map/all_gather | solution.py:112
  7.9 88.3 %all-gather.19.cloned.1.call-start = ((), (), s32[]{:S(2)}) async-start(), calls=%async_computation.9 | async-start | bytes 1327104 | tf_op jit(solution)/shard_map/all_gather | solution.py:111
  8.7 137.1 %all-gather.17.cloned.1.call-start = ((), (), s32[]{:S(2)}) async-start(), calls=%async_computation.8 | async-start | bytes 1327104 | tf_op jit(solution)/shard_map/all_gather | solution.py:109
  9.4 158.3 %all-gather.25.cloned.1.call-start = ((), (), s32[]{:S(2)}) async-start(), calls=%async_computation.12 | async-start | bytes 3932160 | tf_op jit(solution)/shard_map/all_gather | solution.py:150
  60.4 35.9 %copy-start.21 = (bf16[1,1,1024,768]{3,2,1,0:T(8,128)(2,1)S(1)}, bf16[1,1,1024,768]{3,2,1,0:T(8,128)(2,1)}, u32[]{:S(2)}) copy-start(bf16[1,1,1024,768]{3,2,1,0:T(8,128)(2,1)} %param.28) | copy-start | bytes 4718596
  61.4 136.8 %all-gather.21.cloned.1.call-start = ((), (), s32[]{:S(2)}) async-start(), calls=%async_computation.10 | async-start | bytes 3932160 | tf_op jit(solution)/shard_map/all_gather | solution.py:149
  99.9 11.8 copy-start.66
  99.9 40.4 %copy-start.20 = (bf16[1,1,1024,768]{3,2,1,0:T(8,128)(2,1)S(1)}, bf16[1,1,1024,768]{3,2,1,0:T(8,128)(2,1)}, u32[]{:S(2)}) copy-start(bf16[1,1,1024,768]{3,2,1,0:T(8,128)(2,1)} %param.30) | copy-start | bytes 4718596
  99.9 292.4 %all-gather.27.cloned.1.call-start = ((), (), s32[]{:S(2)}) async-start(), calls=%async_computation.13 | async-start | bytes 1327104 | tf_op jit(solution)/shard_map/all_gather | solution.py:114
  100.5 296.2 %all-gather.29.cloned.1.call-start = ((), (), s32[]{:S(2)}) async-start(), calls=%async_computation.14 | async-start | bytes 5308416 | tf_op jit(solution)/shard_map/all_gather | solution.py:118
  101.3 333.5 %all-gather.31.cloned.1.call-start = ((), (), s32[]{:S(2)}) async-start(), calls=%async_computation.15 | async-start | bytes 5308416 | tf_op jit(solution)/shard_map/all_gather | solution.py:120
  102.0 427.8 %all-gather.33.cloned.1.call-start = ((), (), s32[]{:S(2)}) async-start(), calls=%async_computation.16 | async-start | bytes 5308416 | tf_op jit(solution)/shard_map/all_gather | solution.py:258
  104.7 41.0 %copy-start.46 = (f32[1,1,1024]{2,1,0:T(1,128)}, f32[1,1,1024]{2,1,0:T(1,128)S(1)}, u32[]{:S(2)}) copy-start(f32[1,1,1024]{2,1,0:T(1,128)S(1)} %convert_element_type.269) | copy-start | bytes 12292
  210.0 182.4 %copy-start.63 = (f32[768]{0:T(1024)S(1)}, f32[768]{0:T(1024)}, u32[]{:S(2)}) copy-start(f32[768]{0:T(1024)} %convert_element_type.259) | copy-start | bytes 9220
  396.3 38.6 %copy-start.8 = (f32[1024,768]{0,1:T(8,128)}, f32[1024,768]{0,1:T(8,128)S(1)}, u32[]{:S(2)}) copy-start(f32[1024,768]{0,1:T(8,128)S(1)} %get-tuple-element.587) | copy-start | bytes 9437188
  396.3 224.2 %copy-start.42 = (f32[1024]{0:T(1024)}, f32[1024]{0:T(1024)S(1)}, u32[]{:S(2)}) copy-start(f32[1024]{0:T(1024)S(1)} %broadcast_multiply_fusion.6) | copy-start | bytes 12292
  396.7 223.8 %copy-start.48 = (f32[1024]{0:T(1024)}, f32[1024]{0:T(1024)S(1)}, u32[]{:S(2)}) copy-start(f32[1024]{0:T(1024)S(1)} %add_rsqrt_fusion.1) | copy-start | bytes 12292
  397.0 37.8 %copy-start.62 = (f32[768]{0:T(1024)S(1)}, f32[768]{0:T(1024)}, u32[]{:S(2)}) copy-start(f32[768]{0:T(1024)} %convert_element_type.265) | copy-start | bytes 9220
  446.6 25.9 %copy-start.47 = (f32[1,1,1024]{2,1,0:T(1,128)S(1)}, f32[1,1,1024]{2,1,0:T(1,128)}, u32[]{:S(2)}) copy-start(f32[1,1,1024]{2,1,0:T(1,128)} %copy-done.46) | copy-start | bytes 12292
  449.4 160.5 %all-gather.35.cloned.1.call-start = ((), (), s32[]{:S(2)}) async-start(), calls=%async_computation.17 | async-start | bytes 5308416 | tf_op jit(solution)/shard_map/all_gather | solution.py:257
  450.0 201.3 %all-gather.37.cloned.1.call-start = ((), (), s32[]{:S(2)}) async-start(), calls=%async_computation.18 | async-start | bytes 1327104 | tf_op jit(solution)/shard_map/all_gather | solution.py:256
  481.6 644.1 %reduce-scatter.17.cloned.1.call-start = ((), (), s32[]{:S(2)}) async-start(), calls=%async_computation.22 | async-start | bytes 3932160 | tf_op jit(solution)/shard_map/reduce_scatter | solution.py:342
  529.8 80.1 %copy-start.9 = (f32[1024,768]{0,1:T(8,128)S(1)}, f32[1024,768]{0,1:T(8,128)}, u32[]{:S(2)}) copy-start(f32[1024,768]{0,1:T(8,128)} %copy-done.8) | copy-start | bytes 9437188
  1088.9 77.6 %reduce-scatter.15.cloned.1.call-start = ((), (), s32[]{:S(2)}) async-start(), calls=%async_computation.20 | async-start | bytes 3932160 | tf_op jit(solution)/shard_map/reduce_scatter | solution.py:339
  1092.9 137.6 %all-gather.39.cloned.1.call-start = ((), (), s32[]{:S(2)}) async-start(), calls=%async_computation.19 | async-start | bytes 1327104 | tf_op jit(solution)/shard_map/all_gather | solution.py:253
  1093.5 187.7 %reduce-scatter.19.cloned.1.call-start = ((), (), s32[]{:S(2)}) async-start(), calls=%async_computation.24 | async-start | bytes 2654208 | tf_op jit(solution)/shard_map/reduce_scatter | solution.py:389
  1099.4 253.2 %reduce-scatter.25.cloned.1.call-start = ((), (), s32[]{:S(2)}) async-start(), calls=%async_computation.27 | async-start | bytes 2654208
  1108.0 410.6 %reduce-scatter.23.cloned.1.call-start = ((), (), s32[]{:S(2)}) async-start(), calls=%async_computation.26 | async-start | bytes 10616832 | tf_op jit(solution)/shard_map/reduce_scatter | solution.py:395
  1118.3 471.9 %reduce-scatter.29.cloned.1.call-start = ((), (), s32[]{:S(2)}) async-start(), calls=%async_computation.29 | async-start | bytes 2654208
  1119.5 9.2 copy-start.13
  1130.7 35.7 %copy-start.23 = (bf16[1,1,1024,768]{3,2,1,0:T(8,128)(2,1)S(1)}, bf16[1,1,1024,768]{3,2,1,0:T(8,128)(2,1)}, u32[]{:S(2)}) copy-start(bf16[1,1,1024,768]{3,2,1,0:T(8,128)(2,1)} %param.28) | copy-start | bytes 4718596
  1130.8 531.0 %reduce-scatter.27.cloned.1.call-start = ((), (), s32[]{:S(2)}) async-start(), calls=%async_computation.28 | async-start | bytes 2654208
  1132.1 34.3 %copy-start.27 = (bf16[512,6,128]{0,2,1:T(8,128)(2,1)}, bf16[512,6,128]{0,2,1:T(8,128)(2,1)S(1)}, u32[]{:S(2)}) copy-start(bf16[512,6,128]{0,2,1:T(8,128)(2,1)S(1)} %slice.63) | copy-start | bytes 2359300
  1173.6 654.2 %reduce-scatter.21.cloned.1.call-start = ((), (), s32[]{:S(2)}) async-start(), calls=%async_computation.25 | async-start | bytes 10616832 | tf_op jit(solution)/shard_map/reduce_scatter | solution.py:393
  1184.3 45.9 %copy-start.16 = (bf16[6,1024,128]{1,2,0:T(8,128)(2,1)S(1)}, bf16[6,1024,128]{1,2,0:T(8,128)(2,1)}, u32[]{:S(2)}) copy-start(bf16[6,1024,128]{1,2,0:T(8,128)(2,1)} %get-tuple-element.1222) | copy-start | bytes 4718596
  1184.3 685.9 %all-gather.41.cloned.1.call-start = ((), (), s32[]{:S(2)}) async-start(), calls=%async_computation.21 | async-start | bytes 1327104 | tf_op jit(solution)/shard_map/all_gather | solution.py:254
  1185.0 727.2 %all-gather.43.cloned.1.call-start = ((), (), s32[]{:S(2)}) async-start(), calls=%async_computation.23 | async-start | bytes 1327104 | tf_op jit(solution)/shard_map/all_gather | solution.py:255
  1185.8 778.7 %all-reduce.26.cloned.1.call-start = ((), (), s32[]{:S(2)}) async-start(), calls=%async_computation.30 | async-start | bytes 3833856 | tf_op jit(solution)/shard_map/psum | solution.py:401
  1230.4 123.9 %copy-start.14 = (bf16[512,6,128]{0,2,1:T(8,128)(2,1)S(1)}, bf16[512,6,128]{0,2,1:T(8,128)(2,1)}, u32[]{:S(2)}) copy-start(bf16[512,6,128]{0,2,1:T(8,128)(2,1)} %copy-done.13) | copy-start | bytes 2359300
  1230.4 123.9 %copy-start.19 = (bf16[512,768]{0,1:T(8,128)(2,1)S(1)}, bf16[512,768]{0,1:T(8,128)(2,1)}, u32[]{:S(2)}) copy-start(bf16[512,768]{0,1:T(8,128)(2,1)} %reduce-scatter.17.cloned.1.call-done) | copy-start | bytes 2359300
  1230.4 124.2 %copy-start.51 = (f32[768]{0:T(1024)S(1)}, f32[768]{0:T(1024)}, u32[]{:S(2)}) copy-start(f32[768]{0:T(1024)} %get-tuple-element.436) | copy-start | bytes 9220
  1230.5 124.2 %copy-start.52 = (f32[768]{0:T(1024)S(1)}, f32[768]{0:T(1024)}, u32[]{:S(2)}) copy-start(f32[768]{0:T(1024)} %get-tuple-element.443) | copy-start | bytes 9220
  1230.5 124.2 %copy-start.53 = (f32[768]{0:T(1024)S(1)}, f32[768]{0:T(1024)}, u32[]{:S(2)}) copy-start(f32[768]{0:T(1024)} %get-tuple-element.565) | copy-start | bytes 9220
  1230.5 124.2 %copy-start.54 = (f32[768]{0:T(1024)S(1)}, f32[768]{0:T(1024)}, u32[]{:S(2)}) copy-start(f32[768]{0:T(1024)} %get-tuple-element.567) | copy-start | bytes 9220
  1230.5 124.2 %copy-start.57 = (f32[3072]{0:T(1024)S(1)}, f32[3072]{0:T(1024)}, u32[]{:S(2)}) copy-start(f32[3072]{0:T(1024)} %get-tuple-element.592) | copy-start | bytes 36868
  1230.5 124.2 %copy-start.64 = (f32[768]{0:T(1024)S(1)}, f32[768]{0:T(1024)}, u32[]{:S(2)}) copy-start(f32[768]{0:T(1024)} %get-tuple-element.438) | copy-start | bytes 9220
  1230.5 124.2 %copy-start.65 = (f32[768]{0:T(1024)S(1)}, f32[768]{0:T(1024)}, u32[]{:S(2)}) copy-start(f32[768]{0:T(1024)} %get-tuple-element.444) | copy-start | bytes 9220
  1830.0 82.2 %copy-start.12 = (f32[1024,768]{0,1:T(8,128)S(1)}, f32[1024,768]{0,1:T(8,128)}, u32[]{:S(2)}) copy-start(f32[1024,768]{0,1:T(8,128)} %get-tuple-element.568) | copy-start | bytes 9437188
  (166 other events, 779.5 us)
Sparse Core Ops, SparseCore 0:
  10.2 43.8 all-gather.22
  56.2 39.9 all-gather.18
  98.4 39.8 all-gather.16
  140.3 27.2 all-gather.24
  169.6 28.5 all-gather.20
  200.3 41.0 all-gather.26
  243.5 78.6 all-gather.28
  324.4 78.0 all-gather.30
  449.5 80.2 all-gather.32
  531.8 78.0 all-gather.34
  612.1 39.1 all-gather.36
  1089.0 36.7 reduce-scatter.16
  1128.4 37.9 reduce-scatter.14
  1168.4 41.1 all-gather.38
  1213.0 68.1 reduce-scatter.18
  1284.5 67.9 reduce-scatter.24
  1356.0 162.4 reduce-scatter.22
  1521.9 68.2 reduce-scatter.28
  1593.7 68.0 reduce-scatter.26
  1665.2 162.4 reduce-scatter.20
  1830.0 40.1 all-gather.40
  1872.3 39.8 all-gather.42
  1916.1 48.2 all-reduce.25
where the time goes:
time: 1990 us; the launch traced here: 1980 us
  waiting for transfers between devices  908 us (46%)
  matrix products  415 us (21%)
  local copies, waits for them, and re-layouts  270 us (14%)
  other arithmetic  188 us (9%)
  blocking collectives  176 us (9%)
    unnamed x26, waiting for transfers between devices  216 us
    reduce_scatter x1, waiting for transfers between devices, local(): lax.psum_scatter(up_weight_grad, 'shard', scatter_dimension=0, tiled=True)  164 us
    dot_general x24, matrix products, pair_scores(): jnp.einsum('qhd,khd->hqk', heads_query, heads_key, preferred_element_type...  116 us
    reduce_scatter x1, waiting for transfers between devices, local(): lax.psum_scatter(down_weight_grad, 'shard', scatter_dimension=0, tiled=True)  114 us
    unnamed x3, blocking collectives  98.6 us
    dot_general x12, matrix products, block_backward(): jnp.einsum('qhd,khd->hqk', heads_delta, heads_value, preferred_element_ty...  67.2 us
    dot_general x6, matrix products, matmul(): jnp.dot(left_matrix, right_matrix, preferred_element_type=jnp.float32)  61.2 us
    all_gather x1, waiting for transfers between devices, local(): lax.all_gather(up_held, 'shard', axis=0, tiled=True)  60.1 us
  transfers between devices with their start and end apart: 23, of which 17 were waited for; matrix products, arithmetic and copies ran while one was open for 21% of the time, Pallas kernels for 0%

commit v1 on v0

v1 whole, which is shorter than its diff:
```python
import functools

import jax
import jax.numpy as jnp
from jax import lax
from jax.experimental import pallas as pl
from jax.experimental.pallas import tpu as pltpu
from jax.sharding import PartitionSpec as P

HDIM = 64
PPIECE = 512
CLEN = 256
EPSILON = 1e-05
NEGATIVE = -1e30
LOG2E = 1.4426950408889634
SCALE = 1.0 / 8.0
LIMIT = 100.0

f32 = jnp.float32
bf16 = jnp.bfloat16
NT = (((1,), (1,)), ((), ()))
NN = (((1,), (0,)), ((), ()))
TN = (((0,), (0,)), ((), ()))
ANY = pl.BlockSpec(memory_space=pl.ANY)
MESH = pl.DeviceIdType.MESH


def dot(left, right, dims):
    return lax.dot_general(left, right, dims, preferred_element_type=f32)


def params(mib=56, **more):
    return pltpu.CompilerParams(vmem_limit_bytes=mib * 2**20, **more)


def cost(gflop, mbytes):
    return pl.CostEstimate(
        flops=int(gflop * 1e9), bytes_accessed=int(mbytes * 1e6), transcendentals=0
    )


def lane_of(rows):
    return lax.broadcasted_iota(jnp.int32, (rows, 128), 1)


def split3(values):
    hi = values.astype(bf16).astype(f32)
    mid = (values - hi).astype(bf16).astype(f32)
    low = values - hi - mid
    return hi, mid, low


def side_lanes(first, values):
    lane = lane_of(values.shape[0])
    hi, mid, low = split3(values)
    out = jnp.where(lane == 1, -hi, jnp.where(lane == 2, -mid, jnp.where(lane == 3, -low, 0.0)))
    return jnp.where(lane == 0, first, out).astype(bf16)


def gather_kernel(
    wq, wk, wv, vec, tok, keep,
    fq, fk, fv, fvec, ptok, pkeep,
    local_sem, zrecv, yrecv, crecv, usend, dsend, ysend, csend, tsend, trecv,
):
    depth = 4
    rep = lax.axis_index("rep")
    shard = lax.axis_index("shard")
    core = rep % 2
    z = shard // 2
    y = shard % 2
    other_core = {"rep": rep + 1 - 2 * core}
    other_x = {"rep": (rep + 2) % 4}
    other_y = {"shard": z * 2 + 1 - y}
    up = {"shard": (shard + 2) % 8}
    down = {"shard": (shard + 6) % 8}

    barrier = pltpu.get_barrier_semaphore()
    for place in (other_core, other_x, other_y):
        pl.semaphore_signal(barrier, inc=1, device_id=place, device_id_type=MESH)

    @pl.when(z < depth - 1)
    def _():
        pl.semaphore_signal(barrier, inc=1, device_id=up, device_id_type=MESH)

    @pl.when(z > 0)
    def _():
        pl.semaphore_signal(barrier, inc=1, device_id=down, device_id_type=MESH)

    inner = jnp.where((z > 0) & (z < depth - 1), 5, 4)
    pl.semaphore_wait(barrier, inner)

    sources = (wq, wk, wv, vec)
    targets = (fq, fk, fv, fvec)

    def place_of(u, zz, yy, cc):
        if u == 3:
            return targets[u].at[zz * 2 + yy]
        return targets[u].at[(zz * 2 + yy) * 2 + cc]

    def own_of(u):
        return sources[u] if u == 3 else sources[u].at[core]

    def move(src, dst, send, recv, where):
        return pltpu.make_async_remote_copy(
            src_ref=src, dst_ref=dst, send_sem=send, recv_sem=recv,
            device_id=where, device_id_type=MESH,
        )

    def to_up(u, zz, src):
        return move(src, place_of(u, zz, y, core), usend.at[u, zz], zrecv.at[u, zz], up)

    def to_down(u, zz, src):
        return move(src, place_of(u, zz, y, core), dsend.at[u, zz], zrecv.at[u, zz], down)

    def to_y(u, zz, src):
        return move(src, place_of(u, zz, y, core), ysend.at[u, zz], yrecv.at[u, zz], other_y)

    def to_core(u, zz, yy):
        at = place_of(u, zz, yy, core)
        index = zz * 2 + yy
        return move(at, at, csend.at[u, index], crecv.at[u, index], other_core)

    for u in range(4):
        @pl.when(z < depth - 1)
        def _():
            to_up(u, z, own_of(u)).start()

        @pl.when(z > 0)
        def _():
            to_down(u, z, own_of(u)).start()

        to_y(u, z, own_of(u)).start()

    prompt = tok.at[pl.ds(0, PPIECE)]
    copies = [
        move(prompt, ptok.at[1], tsend.at[0], trecv.at[0], other_x),
        move(keep, pkeep.at[1], tsend.at[1], trecv.at[1], other_x),
        move(prompt, ptok.at[0], tsend.at[2], trecv.at[2], other_core),
        move(keep, pkeep.at[0], tsend.at[3], trecv.at[3], other_core),
    ]
    for copy in copies:
        copy.start()
    locals_ = []
    for u in range(4):
        if u == 3:
            dst = fvec.at[shard]
        else:
            dst = targets[u].at[pl.ds(shard * 2, 2)]
        locals_.append(pltpu.make_async_copy(sources[u], dst, local_sem.at[u]))
        locals_[-1].start()

    for step in range(1, depth + 1):
        for u in range(4):
            if step < depth:
                @pl.when(z - step >= 0)
                def _():
                    zz = z - step
                    at = place_of(u, zz, y, core)
                    to_up(u, zz, at).wait_recv()

                    @pl.when(z < depth - 1)
                    def _():
                        to_up(u, zz, at).start()

                    to_y(u, zz, at).start()
                    if u < 3:
                        to_core(u, zz, y).start()

                @pl.when(z + step < depth)
                def _():
                    zz = z + step
                    at = place_of(u, zz, y, core)
                    to_down(u, zz, at).wait_recv()

                    @pl.when(z > 0)
                    def _():
                        to_down(u, zz, at).start()

                    to_y(u, zz, at).start()
                    if u < 3:
                        to_core(u, zz, y).start()

        for u in range(4):
            def from_y(zz):
                at = targets[u].at[zz * 2 + 1 - y] if u == 3 else place_of(u, zz, 1 - y, core)
                move(at, at, ysend.at[u, zz], yrecv.at[u, zz], other_y).wait_recv()
                if u < 3:
                    to_core(u, zz, 1 - y).start()

            if step == 1:
                from_y(z)
            else:
                @pl.when(z - (step - 1) >= 0)
                def _():
                    from_y(z - (step - 1))

                @pl.when(z + (step - 1) < depth)
                def _():
                    from_y(z + (step - 1))

    copies[0].wait_recv()
    copies[1].wait_recv()
    forward = [
        move(ptok.at[1], ptok.at[2], tsend.at[4], trecv.at[4], other_core),
        move(pkeep.at[1], pkeep.at[2], tsend.at[5], trecv.at[5], other_core),
    ]
    for copy in forward:
        copy.start()

    def others(act):
        for zz in range(depth):
            for yy in range(2):
                @pl.when((zz != z) | (yy != y))
                def _():
                    act(zz, yy)

    for u in range(3):
        def arrived(zz, yy):
            at = place_of(u, zz, yy, 1 - core)
            index = zz * 2 + yy
            move(at, at, csend.at[u, index], crecv.at[u, index], other_core).wait_recv()

        others(arrived)
    copies[2].wait_recv()
    copies[3].wait_recv()
    for copy in forward:
        copy.wait_recv()

    for copy in copies + forward:
        copy.wait_send()
    for copy in locals_:
        copy.wait()
    for u in range(4):
        for zz in range(depth):
            at = place_of(u, zz, y, core)
            to_y(u, zz, at).wait_send()

            @pl.when((zz <= z) & (z < depth - 1))
            def _():
                to_up(u, zz, at).wait_send()

            @pl.when((zz >= z) & (z > 0))
            def _():
                to_down(u, zz, at).wait_send()

        if u < 3:
            others(lambda zz, yy: to_core(u, zz, yy).wait_send())


def first_gather(wq, wk, wv, vec, tok, keep):
    width = wq.shape[1]
    sem = pltpu.SemaphoreType.DMA
    halves = [w.reshape(2, 48, width) for w in (wq, wk, wv)]
    full = jax.ShapeDtypeStruct((16, 48, width), bf16)
    outs = pl.pallas_call(
        gather_kernel,
        in_specs=[ANY] * 6,
        out_specs=[ANY] * 6,
        out_shape=[
            full, full, full,
            jax.ShapeDtypeStruct((8, 16, 128), bf16),
            jax.ShapeDtypeStruct((3, PPIECE, width), bf16),
            jax.ShapeDtypeStruct((3, 8, 128), f32),
        ],
        scratch_shapes=[
            sem((4,)), sem((4, 4)), sem((4, 4)), sem((3, 8)), sem((4, 4)), sem((4, 4)),
            sem((4, 4)), sem((3, 8)), sem((6,)), sem((6,)),
        ],
        compiler_params=params(8, collective_id=1, has_side_effects=True),
        cost_estimate=cost(0, 20),
    )(*halves, vec, tok, keep)
    fq, fk, fv, fvec, ptok, pkeep = outs
    return (
        fq.reshape(width, width), fk.reshape(width, width), fv.reshape(width, width),
        fvec, ptok.reshape(3 * PPIECE, width), pkeep,
    )


def project_kernel(tok, oth, wq, wk, wv, qb, vb, q, k, v, qn, kn):
    step = pl.program_id(0)
    own = (step == 0) | (step == 4)
    width = wq.shape[0]
    row = lax.broadcasted_iota(jnp.int32, (width, 128), 0)
    lane = lax.broadcasted_iota(jnp.int32, (width, 128), 1)
    heads = jnp.where(row // HDIM == lane, 1.0, 0.0).astype(bf16)

    @pl.when(step == 0)
    def _():
        qn[...] = jnp.zeros_like(qn)
        kn[...] = jnp.zeros_like(kn)

    def norms(values):
        wide = values.astype(f32)
        sums = dot((wide * wide).astype(bf16), heads, NN)
        return jnp.broadcast_to(jnp.max(sums, axis=0, keepdims=True), (8, 128))

    def keys(rows):
        keys_low = dot(rows, wk[...], NN).astype(bf16)
        k[...] = keys_low
        kn[...] = jnp.maximum(kn[...], norms(keys_low))
        v[...] = (dot(rows, wv[...], NN) + vb[...].astype(f32)).astype(bf16)

    @pl.when(own)
    def _():
        rows = tok[...]
        keys(rows)
        low = (dot(rows, wq[...], NN) + qb[...].astype(f32)).astype(bf16)
        q[...] = low
        qn[...] = jnp.maximum(qn[...], norms(low))

    @pl.when(jnp.logical_not(own))
    def _():
        keys(oth[...])


def project(tok, oth, wq, wk, wv, qb, vb):
    width = tok.shape[1]
    block = (PPIECE, width)
    whole = pl.BlockSpec((width, width), lambda i: (0, 0))
    row = pl.BlockSpec((1, width), lambda i: (0, 0))
    small = pl.BlockSpec((8, 128), lambda i: (0, 0))
    return pl.pallas_call(
        project_kernel,
        grid=(5,),
        in_specs=[
            pl.BlockSpec(block, lambda i: (i // 4, 0)),
            pl.BlockSpec(block, lambda i: (jnp.clip(i - 1, 0, 2), 0)),
            whole, whole, whole, row, row,
        ],
        out_specs=[
            pl.BlockSpec(block, lambda i: (i // 4, 0)),
            pl.BlockSpec(block, lambda i: (i, 0)),
            pl.BlockSpec(block, lambda i: (i, 0)),
            small, small,
        ],
        out_shape=[
            jax.ShapeDtypeStruct((1024, width), bf16),
            jax.ShapeDtypeStruct((2560, width), bf16),
            jax.ShapeDtypeStruct((2560, width), bf16),
            jax.ShapeDtypeStruct((8, 128), f32),
            jax.ShapeDtypeStruct((8, 128), f32),
        ],
        compiler_params=params(),
        cost_estimate=cost(7.5, 20),
    )(tok, oth, wq, wk, wv, qb, vb)


def head_twice(values, head):
    wide = values.astype(f32)
    turned = pltpu.roll(wide, 64, 1)
    first = lane_of(values.shape[0]) < 64
    if head == 0:
        return jnp.where(first, wide, turned).astype(bf16)
    return jnp.where(first, turned, wide).astype(bf16)


def head_parts(values, head):
    wide = values.astype(f32) * (SCALE * LOG2E)
    hi = wide.astype(bf16).astype(f32)
    low = wide - hi
    first = lane_of(values.shape[0]) < 64
    if head == 0:
        return jnp.where(first, hi, pltpu.roll(low, 64, 1)).astype(bf16)
    return jnp.where(first, pltpu.roll(hi, 64, 1), low).astype(bf16)


def head_only(values, head):
    first = lane_of(values.shape[0]) < 64
    keep = first if head == 0 else jnp.logical_not(first)
    return jnp.where(keep, values, jnp.zeros_like(values))


def off_diagonal(size, bias):
    row = lax.broadcasted_iota(jnp.int32, (size, size), 0)
    col = lax.broadcasted_iota(jnp.int32, (size, size), 1)
    return jnp.where(row == col, 0.0, bias)


def attend_kernel(q, k, v, kb, brow, qn, kn, o, side, qx, qd, kx, vx, pm, pc, bown, bcont, top):
    @pl.when(pl.program_id(0) == 0)
    def _():
        for head in range(2):
            kx[head, :, 128:] = kb[...]
        vx[:, 128:] = jnp.ones((2560, 128), bf16)
        bown[...] = off_diagonal(512, brow[0:1, 0:512])
        for c in range(2):
            bcont[c] = off_diagonal(256, brow[0:1, 2048 + 256 * c : 2304 + 256 * c])

    far = jnp.max(qn[...] * kn[...]) * (SCALE * LOG2E) ** 2 * 1.1 > LIMIT * LIMIT
    near = jnp.logical_not(far)
    lane = lane_of(1024)
    vx[:, :128] = v[...]
    for head in range(2):
        parts = head_parts(q[...], head)
        qx[head, :, :128] = parts
        qd[head, :, :128] = parts
        kx[head, :, :128] = head_twice(k[...], head)
        qx[head, :, 128:] = jnp.where(lane == 0, 1.0, 0.0).astype(bf16)
        qd[head, :, 128:] = jnp.zeros((1024, 128), bf16)

    def own_scores(head):
        return dot(qd[head, :512], kx[head, :512], NT) + bown[...]

    def cont_scores(head, c):
        rows = slice(512 + 256 * c, 768 + 256 * c)
        keys = slice(2048 + 256 * c, 2304 + 256 * c)
        return dot(qd[head, rows], kx[head, keys], NT) + bcont[c]

    @pl.when(near)
    def _():
        top[...] = jnp.zeros_like(top)

    @pl.when(far)
    def _():
        def widest(scores):
            return jnp.broadcast_to(
                jnp.max(scores, axis=1, keepdims=True), (scores.shape[0], 128)
            )

        for head in range(2):
            def more(c, carry):
                found = widest(dot(qx[head], kx[head, pl.ds(512 + c * 256, 256)], NT))
                top[head] = jnp.maximum(top[head], found)
                return carry

            top[head] = jnp.full((1024, 128), -3e38, f32)
            lax.fori_loop(0, 6, more, 0)
            top[head, 0:512] = jnp.maximum(top[head, 0:512], widest(own_scores(head)))
            top[head, 512:1024] = jnp.maximum(
                top[head, 512:1024], widest(dot(qx[head, 512:], kx[head, :512], NT))
            )
            for c in range(2):
                rows = slice(512 + 256 * c, 768 + 256 * c)
                top[head, rows] = jnp.maximum(top[head, rows], widest(cont_scores(head, c)))
            qx[head, :, 128:] = side_lanes(1.0, top[head])
            qd[head, :, 128:] = side_lanes(0.0, top[head])

    outs = []
    for head in range(2):
        for c in range(3):
            keys = slice(512 + 512 * c, 1024 + 512 * c)
            pm[head, :, keys] = jnp.exp2(dot(qx[head], kx[head, keys], NT)).astype(bf16)
        pm[head, 512:, :512] = jnp.exp2(dot(qx[head, 512:], kx[head, :512], NT)).astype(bf16)
        pm[head, :512, :512] = jnp.exp2(own_scores(head)).astype(bf16)
        for c in range(2):
            pc[head, c] = jnp.exp2(cont_scores(head, c)).astype(bf16)
        total = dot(pm[head], vx[:2048], NN)
        extra = [dot(pc[head, c], vx[2048 + 256 * c : 2304 + 256 * c], NN) for c in range(2)]
        total = jnp.concatenate(
            [total[:512], total[512:768] + extra[0], total[768:] + extra[1]], axis=0
        )
        mass = total[:, 128:]
        outs.append(total[:, :128] / mass)
        side[head] = side_lanes(1.0, top[head] + jnp.log2(mass))
    o[...] = jnp.where(lane < 64, outs[0], outs[1]).astype(bf16)


def attend(q, k, v, kb, brow, qn, kn, first, count):
    def pair(rows):
        return pl.BlockSpec((rows, 128), lambda i: (0, i + first))

    def fixed(*shape):
        return pl.BlockSpec(shape, lambda i: (0,) * len(shape))

    return pl.pallas_call(
        attend_kernel,
        grid=(count,),
        in_specs=[
            pair(1024), pair(2560), pair(2560), fixed(2560, 128), fixed(8, 2560),
            fixed(8, 128), fixed(8, 128),
        ],
        out_specs=[
            pl.BlockSpec((1024, 128), lambda i: (0, i)),
            pl.BlockSpec((2, 1024, 128), lambda i: (i, 0, 0)),
        ],
        out_shape=[
            jax.ShapeDtypeStruct((1024, 128 * count), bf16),
            jax.ShapeDtypeStruct((2 * count, 1024, 128), bf16),
        ],
        scratch_shapes=[
            pltpu.VMEM((2, 1024, 256), bf16),
            pltpu.VMEM((2, 1024, 256), bf16),
            pltpu.VMEM((2, 2560, 256), bf16),
            pltpu.VMEM((2560, 256), bf16),
            pltpu.VMEM((2, 1024, 2048), bf16),
            pltpu.VMEM((2, 2, 256, 256), bf16),
            pltpu.VMEM((512, 512), f32),
            pltpu.VMEM((2, 256, 256), f32),
            pltpu.VMEM((2, 1024, 128), f32),
        ],
        compiler_params=params(),
        cost_estimate=cost(7.0 * count, 3 * count),
    )(q, k, v, kb, brow, qn, kn)


def attend_back_kernel(
    q, k, v, d, o, side, kb, dq, dkv, qx, qd, kx, vx, dx, qm, kt, pt, st, pc, sc, bown, bcont
):
    @pl.when(pl.program_id(0) == 0)
    def _():
        for head in range(2):
            kx[head, :, 128:] = kb[...]
        vx[:, 128:] = kb[...]
        column = kb[:, 0:1].astype(f32)
        bown[...] = off_diagonal(512, column[:512])
        for c in range(2):
            bcont[c] = off_diagonal(256, column[2048 + 256 * c : 2304 + 256 * c])

    lane = lane_of(1024)
    vx[:, :128] = v[...]
    kt[...] = jnp.transpose(k[...].astype(f32)).astype(bf16)
    product = d[...].astype(f32) * o[...].astype(f32)
    for head in range(2):
        parts = head_parts(q[...], head)
        qx[head, :, :128] = parts
        qd[head, :, :128] = parts
        tail = side[head]
        qx[head, :, 128:] = tail
        qd[head, :, 128:] = jnp.where(lane == 0, jnp.zeros_like(tail), tail)
        kx[head, :, :128] = head_twice(k[...], head)
        qm[head] = head_only(q[...], head)
        dx[head, :, :128] = head_only(d[...], head)
        inner = jnp.sum(head_only(product, head), axis=1, keepdims=True)
        dx[head, :, 128:] = side_lanes(0.0, jnp.broadcast_to(inner, (1024, 128)))

    dq_rows = []
    for head in range(2):
        def tile(keys, rows, queries, bias=None):
            scores = dot(kx[head, keys], queries[head, rows], NT)
            if bias is not None:
                scores = scores + bias
            probs = jnp.exp2(scores)
            return probs, probs * dot(vx[keys], dx[head, rows], NT)

        for c in range(3):
            keys = slice(512 + 512 * c, 1024 + 512 * c)
            probs, delta = tile(keys, slice(0, 1024), qx)
            pt[head, keys] = probs.astype(bf16)
            st[head, keys] = delta.astype(bf16)
        probs, delta = tile(slice(0, 512), slice(512, 1024), qx)
        pt[head, :512, 512:] = probs.astype(bf16)
        st[head, :512, 512:] = delta.astype(bf16)
        probs, delta = tile(slice(0, 512), slice(0, 512), qd, bown[...])
        pt[head, :512, :512] = probs.astype(bf16)
        st[head, :512, :512] = delta.astype(bf16)
        for c in range(2):
            keys = slice(2048 + 256 * c, 2304 + 256 * c)
            rows = slice(512 + 256 * c, 768 + 256 * c)
            probs, delta = tile(keys, rows, qd, bcont[c])
            pc[head, c] = probs.astype(bf16)
            sc[head, c] = delta.astype(bf16)
        kth = kt[64 * head : 64 * head + 64]
        main = dot(kth[:, :2048], st[head], NN)
        extra = [dot(kth[:, 2048 + 256 * c : 2304 + 256 * c], sc[head, c], NN) for c in range(2)]
        dq_rows.append(
            jnp.concatenate(
                [main[:, :512], main[:, 512:768] + extra[0], main[:, 768:] + extra[1]], axis=1
            )
        )
    dq[...] = jnp.transpose(jnp.concatenate(dq_rows, axis=0) * SCALE).astype(bf16)
    dkv[1, :2048] = (dot(pt[0], dx[0, :, :128], NN) + dot(pt[1], dx[1, :, :128], NN)).astype(bf16)
    dkv[0, :2048] = ((dot(st[0], qm[0], NN) + dot(st[1], qm[1], NN)) * SCALE).astype(bf16)
    for c in range(2):
        keys = slice(2048 + 256 * c, 2304 + 256 * c)
        rows = slice(512 + 256 * c, 768 + 256 * c)
        dkv[1, keys] = (
            dot(pc[0, c], dx[0, rows, :128], NN) + dot(pc[1, c], dx[1, rows, :128], NN)
        ).astype(bf16)
        dkv[0, keys] = (
            (dot(sc[0, c], qm[0, rows], NN) + dot(sc[1, c], qm[1, rows], NN)) * SCALE
        ).astype(bf16)


def attend_back(q, k, v, d, o, side, kb, first, count):
    def pair(rows):
        return pl.BlockSpec((rows, 128), lambda i: (0, i + first))

    return pl.pallas_call(
        attend_back_kernel,
        grid=(count,),
        in_specs=[
            pair(1024), pair(2560), pair(2560), pair(1024),
            pl.BlockSpec((1024, 128), lambda i: (0, i)),
            pl.BlockSpec((2, 1024, 128), lambda i: (i, 0, 0)),
            pl.BlockSpec((2560, 128), lambda i: (0, 0)),
        ],
        out_specs=[
            pl.BlockSpec((1024, 128), lambda i: (0, i)),
            pl.BlockSpec((2, 2560, 128), lambda i: (0, 0, i)),
        ],
        out_shape=[
            jax.ShapeDtypeStruct((1024, 128 * count), bf16),
            jax.ShapeDtypeStruct((2, 2560, 128 * count), bf16),
        ],
        scratch_shapes=[
            pltpu.VMEM((2, 1024, 256), bf16),
            pltpu.VMEM((2, 1024, 256), bf16),
            pltpu.VMEM((2, 2560, 256), bf16),
            pltpu.VMEM((2560, 256), bf16),
            pltpu.VMEM((2, 1024, 256), bf16),
            pltpu.VMEM((2, 1024, 128), bf16),
            pltpu.VMEM((128, 2560), bf16),
            pltpu.VMEM((2, 2048, 1024), bf16),
            pltpu.VMEM((2, 2048, 1024), bf16),
            pltpu.VMEM((2, 2, 256, 256), bf16),
            pltpu.VMEM((2, 2, 256, 256), bf16),
            pltpu.VMEM((512, 512), f32),
            pltpu.VMEM((2, 256, 256), f32),
        ],
        compiler_params=params(),
        cost_estimate=cost(14.0 * count, 5 * count),
    )(q, k, v, d, o, side, kb)


def gelu_parts(x):
    bell = jnp.exp2(x * x * (-0.5 * LOG2E))
    t = 1.0 / (1.0 + (0.3275911 * 0.7071067811865476) * jnp.abs(x))
    poly = 0.5 * 1.061405429
    for term in (-1.453152027, 1.421413741, -0.284496736, 0.254829592):
        poly = poly * t + 0.5 * term
    below = poly * t * bell
    phi = jnp.where(x >= 0.0, 1.0 - below, below)
    return x * phi, phi + x * bell * 0.3989422804014327


def normed_of(values):
    centered = values - jnp.mean(values, axis=-1, keepdims=True)
    spread = lax.rsqrt(jnp.mean(centered * centered, axis=-1, keepdims=True) + EPSILON)
    return centered * spread, spread


def norm_back(incoming, normed, spread, gain):
    scaled = incoming * gain
    centered = scaled - jnp.mean(scaled, axis=-1, keepdims=True)
    return (centered - normed * jnp.mean(scaled * normed, axis=-1, keepdims=True)) * spread


FCH = 768


def forward_back_kernel(
    order, m0, m1, m2, tok, cot, teach, keep, scale, vecs, upb,
    ua, ub, uc, ud, da, db, dc, dd,
    result, hid_o, act_o, ddel_o, udel_o, adel_o, mdel_o, sums,
    wa, wu, wd, slope, sems,
):
    step = pl.program_id(0)
    width = tok.shape[1]
    hidden_units = upb.shape[1]

    def arrivals(wait):
        for group, (up_part, down_part) in enumerate(((ua, da), (ub, db), (uc, dc), (ud, dd))):
            for j in range(4):
                place = order[group * 4 + j]
                at = pl.ds(pl.multiple_of(place * 48, 16), 48)
                far = pl.ds(pl.multiple_of(place * 192, 64), 192)
                for copy in (
                    pltpu.make_async_copy(
                        up_part.at[j, :, pl.ds(0, width)], wa.at[at], sems.at[0, group, j]
                    ),
                    pltpu.make_async_copy(
                        up_part.at[j, :, pl.ds(width, hidden_units)], wu.at[at],
                        sems.at[1, group, j],
                    ),
                    pltpu.make_async_copy(down_part.at[j], wd.at[far], sems.at[2, group, j]),
                ):
                    if wait:
                        copy.wait()
                    else:
                        copy.start()

    @pl.when(step == 0)
    def _():
        arrivals(False)
        sums[...] = jnp.zeros_like(sums)
        arrivals(True)

    def vector(index):
        return vecs[index : index + 1].astype(f32)

    attn_b, gain1, shift1, down_b, gain2, shift2 = [vector(i) for i in range(2, 8)]

    def add_sum(index, values):
        sums[index : index + 1] += jnp.sum(values, axis=0, keepdims=True)

    x = tok[...].astype(f32)
    branch = attn_b + x
    for g, part in enumerate((m0, m1, m2)):
        branch = branch + dot(part[...], wa[256 * g : 256 * g + 256], NN)
    normed1, inv1 = normed_of(branch)
    hidden = normed1 * gain1 + shift1
    hid_low = hidden.astype(bf16)
    hid_o[...] = hid_low
    for c in range(hidden_units // FCH):
        cols = slice(c * FCH, c * FCH + FCH)
        value, rise = gelu_parts(dot(hid_low, wu[:, cols], NN) + upb[:, cols].astype(f32))
        act_o[:, cols] = value.astype(bf16)
        slope[:, cols] = rise.astype(bf16)
    second = hidden + dot(act_o[...], wd[...], NN) + down_b
    normed2, inv2 = normed_of(second)
    final = normed2 * gain2 + shift2
    result[...] = final.astype(bf16)
    errors = final - teach[...].astype(f32)
    kept = errors * jnp.concatenate([keep[...]] * (width // 128), axis=1)
    add_sum(6, kept * errors)
    grad = cot[...].astype(f32) + kept * (2.0 * scale[...])
    add_sum(1, grad * normed2)
    add_sum(2, grad)
    grad2 = norm_back(grad, normed2, inv2, gain2)
    ddel = grad2.astype(bf16)
    ddel_o[...] = ddel
    add_sum(0, ddel.astype(f32))
    for c in range(hidden_units // FCH):
        cols = slice(c * FCH, c * FCH + FCH)
        delta = dot(ddel, wd[cols], NT) * slope[:, cols].astype(f32)
        low = delta.astype(bf16)
        udel_o[:, cols] = low
        add_sum(8 + c, low.astype(f32))
    hgrad = grad2 + dot(udel_o[...], wu[...], NT)
    add_sum(4, hgrad * normed1)
    add_sum(5, hgrad)
    grad1 = norm_back(hgrad, normed1, inv1, gain1)
    adel = grad1.astype(bf16)
    adel_o[...] = adel
    add_sum(3, adel.astype(f32))
    mdel_o[...] = dot(adel, wa[...], NT).astype(bf16)


def forward_back(order, mixed, tok, cot, teach, keep, scale, vecs, upb, ups, downs):
    rows, width = tok.shape
    hidden_units = upb.shape[1]
    half = 512

    def block(columns):
        return pl.BlockSpec((half, columns), lambda i, *_: (i, 0))

    def fixed(*shape):
        return pl.BlockSpec(shape, lambda i, *_: (0,) * len(shape))

    def out(columns):
        return jax.ShapeDtypeStruct((rows, columns), bf16)

    return pl.pallas_call(
        forward_back_kernel,
        grid_spec=pltpu.PrefetchScalarGridSpec(
            num_scalar_prefetch=1,
            grid=(rows // half,),
            in_specs=[
                block(256), block(256), block(256), block(width), block(width), block(width),
                block(128), fixed(1, 1), fixed(8, width), fixed(1, hidden_units),
            ] + [ANY] * 8,
            out_specs=[
                block(width), block(width), block(hidden_units), block(width),
                block(hidden_units), block(width), block(width), fixed(16, width),
            ],
            scratch_shapes=[
                pltpu.VMEM((width, width), bf16),
                pltpu.VMEM((width, hidden_units), bf16),
                pltpu.VMEM((hidden_units, width), bf16),
                pltpu.VMEM((half, hidden_units), bf16),
                pltpu.SemaphoreType.DMA((3, 4, 4)),
            ],
        ),
        out_shape=[
            out(width), out(width), out(hidden_units), out(width), out(hidden_units),
            out(width), out(width), jax.ShapeDtypeStruct((16, width), f32),
        ],
        compiler_params=params(60),
        cost_estimate=cost(32.6, 30),
    )(order, *mixed, tok, cot, teach, keep, scale, vecs, upb, *ups, *downs)


def store_pieces(order, source, mine, other, piece):
    for i in range(8):
        at = pl.multiple_of(order[i] * piece, 16)
        mine[i] = source[pl.ds(at, piece)]
        at = pl.multiple_of(order[i + 8] * piece, 16)
        other[i] = source[pl.ds(at, piece)]


def weight_grad_kernel(order, *refs, count, piece):
    lefts, right = refs[:count], refs[count]
    mine, other, whole = refs[count + 1 :]
    at = 0
    for left in lefts:
        size = left.shape[1]
        whole[at : at + size] = dot(left[...], right[...], TN).astype(bf16)
        at += size
    store_pieces(order, whole, mine, other, piece)


def weight_grad(order, lefts, right, chunk):
    rows, columns = right.shape
    total = sum(left.shape[1] for left in lefts)
    piece = total // 16
    shape = jax.ShapeDtypeStruct((8, piece, columns), bf16)
    out = pl.BlockSpec((8, piece, chunk), lambda i, *_: (0, 0, i))
    return pl.pallas_call(
        functools.partial(weight_grad_kernel, count=len(lefts), piece=piece),
        grid_spec=pltpu.PrefetchScalarGridSpec(
            num_scalar_prefetch=1,
            grid=(columns // chunk,),
            in_specs=[pl.BlockSpec(left.shape, lambda i, *_: (0, 0)) for left in lefts]
            + [pl.BlockSpec((rows, chunk), lambda i, *_: (0, i))],
            out_specs=[out, out],
            scratch_shapes=[pltpu.VMEM((total, chunk), bf16)],
        ),
        out_shape=[shape, shape],
        compiler_params=params(),
        cost_estimate=cost(2e-9 * rows * total * columns, 10),
    )(order, *lefts, right)


def project_grad_kernel(order, tok, oth, dq, dkv, mine, other, sums, whole):
    cols = dq.shape[1]
    whole[:, :cols] = dot(tok[...], dq[...], TN).astype(bf16)
    for j in range(2):
        total = dot(oth[...], dkv[j, 512:2048], TN)
        total = total + dot(tok[:512], dkv[j, :512], TN)
        total = total + dot(tok[512:], dkv[j, 2048:], TN)
        whole[:, cols * (j + 1) : cols * (j + 2)] = total.astype(bf16)
    store_pieces(order, whole, mine, other, 48)
    sums[...] = jnp.zeros_like(sums)
    sums[0:1] = jnp.sum(dq[...].astype(f32), axis=0, keepdims=True)
    sums[1:2] = jnp.sum(dkv[1].astype(f32), axis=0, keepdims=True)


def project_grad(order, tok, oth, dq, dkv):
    width = tok.shape[1]
    cols = dq.shape[1]

    def fixed(shape):
        return pl.BlockSpec(shape, lambda i, *_: (0,) * len(shape))

    piece = (8, 48, 3 * cols)
    return pl.pallas_call(
        project_grad_kernel,
        grid_spec=pltpu.PrefetchScalarGridSpec(
            num_scalar_prefetch=1,
            grid=(1,),
            in_specs=[fixed(tok.shape), fixed(oth.shape), fixed(dq.shape), fixed(dkv.shape)],
            out_specs=[fixed(piece), fixed(piece), fixed((8, cols))],
            scratch_shapes=[pltpu.VMEM((width, 3 * cols), bf16)],
        ),
        out_shape=[
            jax.ShapeDtypeStruct(piece, bf16), jax.ShapeDtypeStruct(piece, bf16),
            jax.ShapeDtypeStruct((8, cols), f32),
        ],
        compiler_params=params(),
        cost_estimate=cost(2.5, 12),
    )(order, tok, oth, dq, dkv)


def tokens_grad_kernel(adel, *refs):
    parts, (wq, wk, wv, out) = refs[:-4], refs[-4:]
    for half in range(2):
        rows = slice(512 * half, 512 * half + 512)
        total = adel[rows].astype(f32)
        for g in range(3):
            dq, own, cont = parts[3 * g : 3 * g + 3]
            cols = slice(256 * g, 256 * g + 256)
            low = own if half == 0 else cont
            total = total + dot(dq[rows], wq[:, cols], NT)
            total = total + dot(low[0], wk[:, cols], NT)
            total = total + dot(low[1], wv[:, cols], NT)
        out[rows] = total.astype(bf16)


def tokens_grad(adel, parts, wq, wk, wv):
    def fixed(shape):
        return pl.BlockSpec(shape, lambda i: (0,) * len(shape))

    specs, flat = [], []
    for dq, own, dkv in parts:
        specs += [
            fixed(dq.shape), fixed(own.shape),
            pl.BlockSpec((2, 512, dkv.shape[2]), lambda i: (0, 4, 0)),
        ]
        flat += [dq, own, dkv]
    return pl.pallas_call(
        tokens_grad_kernel,
        grid=(1,),
        in_specs=[fixed(adel.shape)] + specs + [fixed(wq.shape)] * 3,
        out_specs=fixed(adel.shape),
        out_shape=jax.ShapeDtypeStruct(adel.shape, bf16),
        compiler_params=params(),
        cost_estimate=cost(3.6, 12),
    )(adel, *flat, wq, wk, wv)


def swap(values, axis, bit):
    size = lax.axis_size(axis)
    return lax.ppermute(values, axis, [(i, i ^ bit) for i in range(size)])


def sum_all(values):
    for axis in ("rep", "shard"):
        bit = 1
        while bit < lax.axis_size(axis):
            values = values + swap(values, axis, bit)
            bit *= 2
    return values


def local(
    tokens, cotangent, teacher, valid_mask, valid_count,
    query_weight, query_bias, key_weight, value_weight, value_bias,
    attn_weight, attn_bias, first_gain, first_shift,
    up_weight, up_bias, down_weight, down_bias, second_gain, second_shift,
):
    rows, width = tokens.shape[2:]
    shards = lax.axis_size("shard")
    split = shards == 8
    rep = lax.axis_index("rep")
    shard = lax.axis_index("shard")
    core = rep % 2
    z, y = shard // 2, shard % 2
    tok = tokens.reshape(rows, width)
    keep = valid_mask.reshape(rows)
    if split:
        i = jnp.arange(16, dtype=jnp.int32)
        order = (((z ^ (i % 4)) * 2 + (y ^ (i // 4 % 2))) * 2 + (core ^ (i // 8))).astype(jnp.int32)
    else:
        order = jnp.arange(16, dtype=jnp.int32)

    small = [
        query_bias, value_bias, attn_bias, first_gain, first_shift, down_bias, second_gain,
        second_shift, up_bias,
    ]
    part = query_bias.shape[0]
    vec = jnp.concatenate(small)
    keep_low = keep[:PPIECE].astype(f32).reshape(4, 128)
    if split:
        keep_low = jnp.concatenate([keep_low, keep_low])
        vec = jnp.pad(vec, (0, 2048 - vec.shape[0])).reshape(16, 128)
        wq, wk, wv, vecs, oth, others_keep = first_gather(
            query_weight, key_weight, value_weight, vec, tok, keep_low
        )
        vecs = vecs.reshape(8, 2048)
    else:
        wq, wk, wv, vecs = [
            lax.all_gather(w, "shard", axis=0, tiled=True)
            for w in (query_weight, key_weight, value_weight, vec[None])
        ]
        prompt = tok[:PPIECE]
        oth = jnp.concatenate([swap(prompt, "rep", bit) for bit in (1, 2, 3)])
        others_keep = jnp.stack([swap(keep_low, "rep", bit) for bit in (1, 2, 3)])
    others_keep = others_keep[:, :4].reshape(3 * PPIECE)
    upb = vecs[:, 8 * part : 8 * part + up_bias.shape[0]].reshape(1, -1)
    vecs = vecs[:, : 8 * part].reshape(shards, 8, part).transpose(1, 0, 2).reshape(8, width)

    if split:
        up_half = jnp.concatenate(
            [attn_weight.reshape(2, 48, width), up_weight.reshape(2, 48, -1)], axis=2
        )
        down_half = down_weight.reshape(2, 192, width)
        up_half, down_half, wq = lax.optimization_barrier((up_half, down_half, wq))

        def gather(half):
            half = lax.dynamic_index_in_dim(half, core, 0, keepdims=False)
            near = jnp.stack([half] + [swap(half, "shard", 2 * d) for d in (1, 2, 3)])
            far = swap(near, "shard", 1)
            return near, far, swap(near, "rep", 1), swap(far, "rep", 1)

        ups, downs = gather(up_half), gather(down_half)
    else:
        full = jnp.concatenate(
            [
                lax.all_gather(w, "shard", axis=0, tiled=True)
                for w in (attn_weight, up_weight)
            ],
            axis=1,
        ).reshape(4, 4, 48, -1)
        ups = [full[j] for j in range(4)]
        full = lax.all_gather(down_weight, "shard", axis=0, tiled=True).reshape(4, 4, 192, width)
        downs = [full[j] for j in range(4)]

    q, k, v, qn, kn = project(tok, oth, wq, wk, wv, vecs[0:1], vecs[1:2])
    all_keep = jnp.concatenate(
        [keep[:PPIECE].astype(f32), others_keep, keep[PPIECE:].astype(f32)]
    )
    bias = jnp.where(all_keep > 0.5, 0.0, NEGATIVE)
    brow = jnp.broadcast_to(bias[None], (8, bias.shape[0]))
    lane = jnp.arange(128)[None]
    kb = jnp.where(lane == 0, bias[:, None], jnp.where(lane < 4, 1.0, 0.0)).astype(bf16)
    groups = 3
    pairs = width // 128 // groups
    mixed, sides = zip(
        *[attend(q, k, v, kb, brow, qn, kn, g * pairs, pairs) for g in range(groups)]
    )

    keep_wide = jnp.broadcast_to(keep.astype(f32)[:, None], (rows, 128))
    scale = (1.0 / valid_count.astype(f32)).reshape(1, 1)
    result, hid, act, ddel, udel, adel, mdel, sums = forward_back(
        order, mixed, tok, cotangent.reshape(rows, width), teacher.reshape(rows, width),
        keep_wide, scale, vecs, upb, ups, downs,
    )
    down_pieces = weight_grad(order, [act], ddel, 256)
    up_pieces = weight_grad(order, [hid], udel, 512)
    attn_pieces = weight_grad(order, mixed, adel, 256)

    def scatter(mine, other):
        if not split:
            piece, columns = mine.shape[1:]
            full = jnp.concatenate([mine, other]).reshape(16 * piece, columns)
            part = lax.psum_scatter(full, "shard", scatter_dimension=0, tiled=True)
            return lax.psum(part, "rep").astype(f32)
        got = mine.astype(f32) + swap(other, "rep", 1).astype(f32)
        got = got.astype(bf16)
        got = got[:4].astype(f32) + swap(got[4:], "shard", 1).astype(f32)
        got = got.astype(bf16)
        total = got[0].astype(f32)
        for d in (1, 2, 3):
            total = total + swap(got[d], "shard", 2 * d).astype(f32)
        total = total.astype(bf16)
        first, second, third = [swap(total, "rep", bit).astype(f32) for bit in (1, 2, 3)]
        own, twin = total.astype(f32) + second, first + third
        return jnp.where(
            core == 0, jnp.concatenate([own, twin]), jnp.concatenate([twin, own])
        )

    down_grad = scatter(*down_pieces)
    up_grad = scatter(*up_pieces)
    attn_grad = scatter(*attn_pieces)
    sums = sum_all(sums)

    parts, pieces, tails = [], [], []
    for g in range(groups):
        dq, dkv = attend_back(q, k, v, mdel, mixed[g], sides[g], kb, g * pairs, pairs)
        pieces_mine, pieces_other, tail = project_grad(order, tok, oth, dq, dkv)
        pieces.append(scatter(pieces_mine, pieces_other))
        tails.append(tail)
        near = swap(dkv[:, 512:1024], "rep", 1).astype(f32)
        turn = swap(dkv[:, 1536:2048], "rep", 1).astype(f32)
        turn = (turn + dkv[:, 1024:1536].astype(f32)).astype(bf16)
        turn = swap(turn, "rep", 2).astype(f32)
        own = (dkv[:, :512].astype(f32) + near + turn).astype(bf16)
        parts.append((dq, own, dkv))
    tails = sum_all(jnp.concatenate(tails, axis=1))
    token_grad = tokens_grad(adel, parts, wq, wk, wv)

    cols = width // groups
    query_grad, key_grad, value_grad = [
        jnp.concatenate([p[:, cols * j : cols * (j + 1)] for p in pieces], axis=1)
        for j in range(3)
    ]

    def owned(row):
        return lax.dynamic_slice(row, (shard * part,), (part,))

    up_part = up_bias.shape[0]
    loss = jnp.sum(sums[6]) / valid_count.astype(f32)
    return (
        result.reshape(tokens.shape),
        loss,
        token_grad.reshape(tokens.shape),
        query_grad,
        owned(tails[0]),
        key_grad,
        value_grad,
        owned(tails[1]),
        attn_grad,
        owned(sums[3]),
        owned(sums[4]),
        owned(sums[5]),
        up_grad,
        lax.dynamic_slice(sums[8:12].reshape(-1), (shard * up_part,), (up_part,)),
        down_grad,
        owned(sums[0]),
        owned(sums[1]),
        owned(sums[2]),
    )


def solution(mesh):
    wide = P("shard", "rep", None, None)
    matrix, vector = P("shard", None), P("shard")
    return jax.shard_map(
        local,
        mesh=mesh,
        in_specs=(
            wide, wide, wide, P("shard", "rep", None), P(),
            matrix, vector, matrix, matrix, vector, matrix, vector, vector, vector,
            matrix, vector, matrix, vector, vector, vector,
        ),
        out_specs=(
            wide, P(), wide,
            matrix, vector, matrix, matrix, vector, matrix, vector, vector, vector,
            matrix, vector, matrix, vector, vector, vector,
        ),
        check_vma=False,
    )
```

time: 1990 us -> 613 us (0.31)
  waiting for transfers between devices: 908 us -> 146 us
  matrix products: 415 us -> 0 us
  Pallas kernels: 0 us -> 294 us
  local copies, waits for them, and re-layouts: 270 us -> 29.9 us
  blocking collectives: 176 us -> 0 us
  other arithmetic: 188 us -> 26.5 us
  starting transfers between devices: 0.92 us -> 109 us
    dot_general x102 -> x0, matrix products: 415 us -> none  [the longest x24 116 us: pair_scores(): jnp.einsum('qhd,khd->hqk', heads_query, heads_key, preferred_element_type...]
    reduce_scatter x5 -> x0, waiting for transfers between devices: 365 us -> none  [the longest x1 164 us: local(): lax.psum_scatter(up_weight_grad, 'shard', scatter_dimension=0, tiled=True)]
    pallas_call x0 -> x16, Pallas kernels: none -> 294 us  [the longest x3 85.8 us: attend_back(): pl.pallas_call(attend_back_kernel, grid=(count,), in_specs=[pair(1024), p...]
    all_gather x14 -> x0, waiting for transfers between devices: 283 us -> none  [the longest x1 60.1 us: local(): lax.all_gather(up_held, 'shard', axis=0, tiled=True)]
    unnamed x26 -> x0, waiting for transfers between devices: 216 us -> none
    ppermute x0 -> x79, waiting for transfers between devices: none -> 146 us  [swap(): return lax.ppermute(values, axis, [(i, i ^ bit) for i in range(size)])]
    ppermute x0 -> x79, starting transfers between devices: none -> 109 us  [swap(): return lax.ppermute(values, axis, [(i, i ^ bit) for i in range(size)])]
    unnamed x3 -> x0, blocking collectives: 98.6 us -> none
  transfers between devices with their start and end apart: 23 -> 79, of which waited for: 17 -> 33; matrix products, arithmetic and copies ran while one was open for 21% -> 6% of each run, Pallas kernels for 0% -> 36%
where the time goes in v1:
time: 613 us; the launch traced here: 610 us
  Pallas kernels  294 us (48%)
  waiting for transfers between devices  146 us (24%)
  starting transfers between devices  109 us (18%)
  local copies, waits for them, and re-layouts  29.9 us (5%)
  other arithmetic  26.5 us (4%)
    ppermute x79, waiting for transfers between devices, swap(): return lax.ppermute(values, axis, [(i, i ^ bit) for i in range(size)])  146 us
    ppermute x79, starting transfers between devices, swap(): return lax.ppermute(values, axis, [(i, i ^ bit) for i in range(size)])  109 us
    pallas_call x3, Pallas kernels, attend_back(): pl.pallas_call(attend_back_kernel, grid=(count,), in_specs=[pair(1024), p...  85.8 us
    pallas_call x3, Pallas kernels, attend(): pl.pallas_call(attend_kernel, grid=(count,), in_specs=[pair(1024), pair(2...  58.8 us
    pallas_call x1, Pallas kernels, forward_back(): pl.pallas_call(forward_back_kernel, grid_spec=pltpu.PrefetchScalarGridSpe...  48 us
    pallas_call x3, Pallas kernels, weight_grad(): pl.pallas_call(functools.partial(weight_grad_kernel, count=len(lefts), pi...  27.8 us
    pallas_call x1, Pallas kernels, first_gather(): pl.pallas_call(gather_kernel, in_specs=[ANY] * 6, out_specs=[ANY] * 6, ou...  27.6 us
    pallas_call x3, Pallas kernels, project_grad(): pl.pallas_call(project_grad_kernel, grid_spec=pltpu.PrefetchScalarGridSpe...  22.5 us
  transfers between devices with their start and end apart: 79, of which 33 were waited for; matrix products, arithmetic and copies ran while one was open for 6% of the time, Pallas kernels for 36%

profile of v1, /device:TPU:0, one launch (start us, length us, event | category | flops | bytes accessed | tf_op | source)
XLA Modules:
  0.0 609.6 jit_solution(9282177736865357164)
XLA Ops:
  1.5 6.1 %concatenate.70 = bf16[1152]{0:T(1024)(128)(2,1)S(1)} concatenate(bf16[96]{0:T(256)(128)(2,1)} %param.26, bf16[96]{0:T(256)(128)(2,1)} %param.29, bf16[96]{0:T(256)(128)(2,1)} %param.31, bf16[96]{0:T(256)(128)(2,1)} %param.32, bf16[96]{0:T(256)(128)(2,1)} %param.33, bf16[96]{0:T(256)(128)(2,1)} %param.37, bf16[96]{0:T(256)(128)(2,1)} %param.38, bf16[96]{0:T(256)(128)(2,1)} %param.39, ...), dimensions={0} | concatenate | bytes 4608 | tf_op jit(solution)/shard_map/concatenate | solution.py:931
  10.2 27.6 %shard_map.331 = (bf16[16,48,768]{2,1,0:T(8,128)(2,1)S(1)}, bf16[16,48,768]{2,1,0:T(8,128)(2,1)S(1)}, bf16[16,48,768]{2,1,0:T(8,128)(2,1)S(1)}, bf16[8,16,128]{2...) custom-call(bf16[2,48,768]{2,1,0:T(8,128)(2,1)S(1)} %bitcast.141, ...), custom_call_target="tpu_custom_call" | custom-call | bytes 20000000 | tf_op jit(solution)/shard_map/pallas_call | solution.py:255
  48.1 3.5 collective-permute-start.2
  54.4 14.3 %shard_map.332 = (bf16[1024,768]{1,0:T(8,128)(2,1)}, bf16[2560,768]{1,0:T(8,128)(2,1)}, bf16[2560,768]{1,0:T(8,128)(2,1)}, f32[8,128]{1,0:T(8,128)}, f32[8,128]{1,0:T(8,128)}) custom-call(bf16[1024,768]{1,0:T(8,128)(2,1)} %bitcast.129, bf16[1536,768]{1,0:T(8,128)(2,1)} %bitcast.145, bf16[768,768]{1,0:T(8,128)(2,1)} %bitcast.135, bf16[768,768]{1,0:T(8,128)(2,1)} %bitcast.137, ...), custom_call_target="tpu_custom_call" | custom-call | flops 7500000256 | bytes 20000000 | tf_op jit(solution)/shard_map/pallas_call | solution.py:322
  69.4 19.5 %shard_map.335 = (bf16[1024,256]{1,0:T(8,128)(2,1)}, bf16[4,1024,128]{2,1,0:T(8,128)(2,1)}) custom-call(bf16[1024,768]{1,0:T(8,128)(2,1)} %get-tuple-element.73.q, bf16[2560,768]{1,0:T(8,128)(2,1)} %get-tuple-element.74.k, bf16[2560,768]{1,0:T(8,128)(2,1)} %get-tuple-element.75.v, bf16[2560,128]{1,0:T(8,128)(2,1)} %select_convert_fusion.kb, ...), custom_call_target="tpu_custom_call" | custom-call | flops 14000000000 | bytes 6000000 | tf_op jit(solution)/shard_map/pallas_call | solution.py:465
  88.9 12.9 %collective-permute-start.8 = (bf16[192,768]{1,0:T(8,128)(2,1)}, bf16[192,768]{1,0:T(8,128)(2,1)S(1)}, u32[]{:S(2)}, u32[]{:S(2)}) collective-permute-start(bf16[192,768]{1,0:T(8,128)(2,1)} %fusion.44), channel_id=1, source_target_pairs={{0,6},{1,7},{2,4},{3,5},{4,2},{5,3},{6,0},{7,1},{8,14},{9,15},{10,... | collective-permute-start | bytes 884744 | tf_op jit(solution)/shard_map/ppermute | solution.py:893
  102.1 4.6 collective-permute-done.8
  107.9 19.6 %shard_map.334 = (bf16[1024,256]{1,0:T(8,128)(2,1)}, bf16[4,1024,128]{2,1,0:T(8,128)(2,1)}) custom-call(bf16[1024,768]{1,0:T(8,128)(2,1)} %get-tuple-element.73.q, bf16[2560,768]{1,0:T(8,128)(2,1)} %get-tuple-element.74.k, bf16[2560,768]{1,0:T(8,128)(2,1)} %get-tuple-element.75.v, bf16[2560,128]{1,0:T(8,128)(2,1)} %select_convert_fusion.kb, ...), custom_call_target="tpu_custom_call" | custom-call | flops 14000000000 | bytes 6000000 | tf_op jit(solution)/shard_map/pallas_call | solution.py:465
  127.6 7.6 %collective-permute-done.3.ub = bf16[4,48,3840]{2,1,0:T(8,128)(2,1)} collective-permute-done((bf16[4,48,3840]{2,1,0:T(8,128)(2,1)S(1)}, bf16[4,48,3840]{2,1,0:T(8,128)(2,1)}, u32[]{:S(2)}, u32[]{:S(2)}) %collective-permute-start.3) | collective-permute-done | bytes 1474592 | tf_op jit(solution)/shard_map/ppermute | solution.py:893
  138.9 8.9 %collective-permute-done.9.db = bf16[4,192,768]{2,1,0:T(8,128)(2,1)} collective-permute-done((bf16[4,192,768]{2,1,0:T(8,128)(2,1)S(1)}, bf16[4,192,768]{2,1,0:T(8,128)(2,1)}, u32[]{:S(2)}, u32[]{:S(2)}) %collective-permute-start.9) | collective-permute-done | bytes 1179680 | tf_op jit(solution)/shard_map/ppermute | solution.py:893
  147.8 19.7 %shard_map.333 = (bf16[1024,256]{1,0:T(8,128)(2,1)}, bf16[4,1024,128]{2,1,0:T(8,128)(2,1)}) custom-call(bf16[1024,768]{1,0:T(8,128)(2,1)} %get-tuple-element.73.q, bf16[2560,768]{1,0:T(8,128)(2,1)} %get-tuple-element.74.k, bf16[2560,768]{1,0:T(8,128)(2,1)} %get-tuple-element.75.v, bf16[2560,128]{1,0:T(8,128)(2,1)} %select_convert_fusion.kb, ...), custom_call_target="tpu_custom_call" | custom-call | flops 14000000000 | bytes 6000000 | tf_op jit(solution)/shard_map/pallas_call | solution.py:465
  169.1 48.0 %shard_map.336 = (bf16[1024,768]{1,0:T(8,128)(2,1)}, bf16[1024,768]{1,0:T(8,128)(2,1)}, bf16[1024,3072]{1,0:T(8,128)(2,1)}, bf16[1024,768]{1,0:T(8,128)(2,1)}, b...) custom-call(s32[16]{0:T(128)} %fusion.20.order, ...), custom_call_target="tpu_custom_call" | custom-call | flops 32600000512 | bytes 30000000 | tf_op jit(solution)/shard_map/pallas_call | solution.py:743
  217.7 28.4 %shard_map.337 = (bf16[1024,256]{1,0:T(8,128)(2,1)}, bf16[2,2560,256]{2,1,0:T(8,128)(2,1)}) custom-call(bf16[1024,768]{1,0:T(8,128)(2,1)} %get-tuple-element.73.q, bf16[2560,768]{1,0:T(8,128)(2,1)} %get-tuple-element.74.k, bf16[2560,768]{1,0:T(8,128)(2,1)} %get-tuple-element.75.v, bf16[1024,768]{1,0:T(8,128)(2,1)} %get-tuple-element.87.d, ...), custom_call_target="tpu_custom_call" | custom-call | flops 28000000000 | bytes 10000000 | tf_op jit(solution)/shard_map/pallas_call | solution.py:578
  246.0 28.5 %shard_map.338 = (bf16[1024,256]{1,0:T(8,128)(2,1)}, bf16[2,2560,256]{2,1,0:T(8,128)(2,1)}) custom-call(bf16[1024,768]{1,0:T(8,128)(2,1)} %get-tuple-element.73.q, bf16[2560,768]{1,0:T(8,128)(2,1)} %get-tuple-element.74.k, bf16[2560,768]{1,0:T(8,128)(2,1)} %get-tuple-element.75.v, bf16[1024,768]{1,0:T(8,128)(2,1)} %get-tuple-element.87.d, ...), custom_call_target="tpu_custom_call" | custom-call | flops 28000000000 | bytes 10000000 | tf_op jit(solution)/shard_map/pallas_call | solution.py:578
  274.5 28.9 %shard_map.339 = (bf16[1024,256]{1,0:T(8,128)(2,1)}, bf16[2,2560,256]{2,1,0:T(8,128)(2,1)}) custom-call(bf16[1024,768]{1,0:T(8,128)(2,1)} %get-tuple-element.73.q, bf16[2560,768]{1,0:T(8,128)(2,1)} %get-tuple-element.74.k, bf16[2560,768]{1,0:T(8,128)(2,1)} %get-tuple-element.75.v, bf16[1024,768]{1,0:T(8,128)(2,1)} %get-tuple-element.87.d, ...), custom_call_target="tpu_custom_call" | custom-call | flops 28000000000 | bytes 10000000 | tf_op jit(solution)/shard_map/pallas_call | solution.py:578
  305.7 7.5 %shard_map.343 = (bf16[8,48,768]{2,1,0:T(8,128)(2,1)}, bf16[8,48,768]{2,1,0:T(8,128)(2,1)}, f32[8,256]{1,0:T(8,128)}) custom-call(s32[16]{0:T(128)} %fusion.20.order, bf16[1024,768]{1,0:T(8,128)(2,1)} %bitcast.131, bf16[1536,768]{1,0:T(8,128)(2,1)} %bitcast.146, bf16[1024,256]{1,0:T(8,128)(2,1)} %get-tuple-element.95.refs_6_.dq, ...), custom_call_target="tpu_custom_call" | custom-call | flops 2500000000 | bytes 12000000 | tf_op jit(solution)/shard_map/pallas_call | solution.py:836
  313.2 7.5 %shard_map.341 = (bf16[8,48,768]{2,1,0:T(8,128)(2,1)}, bf16[8,48,768]{2,1,0:T(8,128)(2,1)}, f32[8,256]{1,0:T(8,128)}) custom-call(s32[16]{0:T(128)} %fusion.20.order, bf16[1024,768]{1,0:T(8,128)(2,1)} %bitcast.132, bf16[1536,768]{1,0:T(8,128)(2,1)} %bitcast.147, bf16[1024,256]{1,0:T(8,128)(2,1)} %get-tuple-element.89.refs_0_.dq, ...), custom_call_target="tpu_custom_call" | custom-call | flops 2500000000 | bytes 12000000 | tf_op jit(solution)/shard_map/pallas_call | solution.py:836
  321.3 7.6 %shard_map.342 = (bf16[8,48,768]{2,1,0:T(8,128)(2,1)}, bf16[8,48,768]{2,1,0:T(8,128)(2,1)}, f32[8,256]{1,0:T(8,128)}) custom-call(s32[16]{0:T(128)} %fusion.20.order, bf16[1024,768]{1,0:T(8,128)(2,1)} %bitcast.133, bf16[1536,768]{1,0:T(8,128)(2,1)} %bitcast.148, bf16[1024,256]{1,0:T(8,128)(2,1)} %get-tuple-element.92.refs_3_.dq, ...), custom_call_target="tpu_custom_call" | custom-call | flops 2500000000 | bytes 12000000 | tf_op jit(solution)/shard_map/pallas_call | solution.py:836
  329.7 11.4 %shard_map.346 = (bf16[8,192,768]{2,1,0:T(8,128)(2,1)}, bf16[8,192,768]{2,1,0:T(8,128)(2,1)}) custom-call(s32[16]{0:T(128)} %fusion.20.order, bf16[1024,3072]{1,0:T(8,128)(2,1)} %get-tuple-element.112.refs_0_, bf16[1024,768]{1,0:T(8,128)(2,1)} %get-tuple-element.113.refs_1_), custom_call_target="tpu_custom_call" | custom-call | flops 4831838208 | bytes 10000000 | tf_op jit(solution)/shard_map/pallas_call | solution.py:798
  341.0 3.6 collective-permute-start.51
  350.8 22.0 %collective-permute-start.53 = (f32[8,768]{1,0:T(8,128)S(1)}, f32[8,768]{1,0:T(8,128)S(1)}, u32[]{:S(2)}, u32[]{:S(2)}) collective-permute-start(f32[8,768]{1,0:T(8,128)S(1)} %add.274), channel_id=1, source_target_pairs={{0,2},{1,3},{2,0},{3,1},{4,6},{5,7},{6,4},{7,5},{8,10},{9,11},{10,... | collective-permute-start | bytes 73736 | tf_op jit(solution)/shard_map/ppermute | solution.py:893
  372.8 10.7 %shard_map.345 = (bf16[8,48,3072]{2,1,0:T(8,128)(2,1)}, bf16[8,48,3072]{2,1,0:T(8,128)(2,1)}) custom-call(s32[16]{0:T(128)} %fusion.20.order, bf16[1024,768]{1,0:T(8,128)(2,1)} %get-tuple-element.108.refs_0_, bf16[1024,3072]{1,0:T(8,128)(2,1)} %get-tuple-element.109.refs_1_), custom_call_target="tpu_custom_call" | custom-call | flops 4831838208 | bytes 10000000 | tf_op jit(solution)/shard_map/pallas_call | solution.py:798
  384.8 5.7 shard_map.344
  391.2 4.1 collective-permute-done.15
  395.3 3.0 collective-permute-start.16
  413.3 6.0 collective-permute-done.56
  420.6 5.1 collective-permute-done.27
  425.8 6.2 %collective-permute-done.35 = bf16[4,48,768]{2,1,0:T(8,128)(2,1)S(1)} collective-permute-done((bf16[4,48,768]{2,1,0:T(8,128)(2,1)S(1)}, bf16[4,48,768]{2,1,0:T(8,128)(2,1)S(1)}, u32[]{:S(2)}, u32[]{:S(2)}) %collective-permute-start.35) | collective-permute-done | bytes 294944 | tf_op jit(solution)/shard_map/ppermute | solution.py:893
  432.0 2.9 collective-permute-start.58
  435.0 2.7 collective-permute-done.43
  444.2 2.8 collective-permute-start.30
  450.5 2.7 collective-permute-start.38
  467.3 2.8 collective-permute-done.31
  471.6 3.4 collective-permute-done.39
  476.5 2.8 collective-permute-done.47
  481.1 2.7 collective-permute-done.62
  489.2 3.2 collective-permute-done.41
  493.7 2.9 collective-permute-done.49
  505.2 6.2 %collective-permute-done.25 = bf16[2,512,256]{2,1,0:T(8,128)(2,1)S(1)} collective-permute-done((bf16[2,512,256]{2,1,0:T(8,128)(2,1)S(1)}, bf16[2,512,256]{2,1,0:T(8,128)(2,1)S(1)}, u32[]{:S(2)}, u32[]{:S(2)}) %collective-permute-start.25) | collective-permute-done | bytes 524320 | tf_op jit(solution)/shard_map/ppermute | solution.py:893
  514.9 7.8 %collective-permute-done.22 = bf16[2,512,256]{2,1,0:T(8,128)(2,1)S(1)} collective-permute-done((bf16[2,512,256]{2,1,0:T(8,128)(2,1)S(1)}, bf16[2,512,256]{2,1,0:T(8,128)(2,1)S(1)}, u32[]{:S(2)}, u32[]{:S(2)}) %collective-permute-start.22) | collective-permute-done | bytes 524320 | tf_op jit(solution)/shard_map/ppermute | solution.py:893
  524.8 8.2 %collective-permute-done.19 = bf16[2,512,256]{2,1,0:T(8,128)(2,1)S(1)} collective-permute-done((bf16[2,512,256]{2,1,0:T(8,128)(2,1)S(1)}, bf16[2,512,256]{2,1,0:T(8,128)(2,1)S(1)}, u32[]{:S(2)}, u32[]{:S(2)}) %collective-permute-start.19) | collective-permute-done | bytes 524320 | tf_op jit(solution)/shard_map/ppermute | solution.py:893
  539.5 3.3 collective-permute-start.66
  542.8 20.8 %collective-permute-done.72 = bf16[4,192,768]{2,1,0:T(8,128)(2,1)S(1)} collective-permute-done((bf16[4,192,768]{2,1,0:T(8,128)(2,1)S(1)}, bf16[4,192,768]{2,1,0:T(8,128)(2,1)S(1)}, u32[]{:S(2)}, u32[]{:S(2)}) %collective-permute-start.72) | collective-permute-done | bytes 1179680 | tf_op jit(solution)/shard_map/ppermute | solution.py:893
  565.3 3.3 collective-permute-start.74
  569.8 8.9 %shard_map.340 = bf16[1024,768]{1,0:T(8,128)(2,1)} custom-call(bf16[1024,768]{1,0:T(8,128)(2,1)} %get-tuple-element.86.adel.refs_3_, bf16[1024,256]{1,0:T(8,128)(2,1)} %get-tuple-element.89.refs_0_.dq, bf16[2,512,256]{2,1,0:T(8,128)(2,1)} %add_convert_fusion.12.refs_1_, bf16[2,2560,256]{2,1,0:T(8,128)(2,1)} %get-tuple-element.90.refs_2_.dkv, ...), custom_call_target="tpu_custom_call" | custom-call | flops 3600000000 | bytes 12000000 | tf_op jit(solution)/shard_map/pallas_call | solution.py:880
  578.6 10.5 %collective-permute-done.74 = bf16[192,768]{1,0:T(8,128)(2,1)S(1)} collective-permute-done((bf16[192,768]{1,0:T(8,128)(2,1)S(1)}, bf16[192,768]{1,0:T(8,128)(2,1)S(1)}, u32[]{:S(2)}, u32[]{:S(2)}) %collective-permute-start.74) | collective-permute-done | bytes 294944 | tf_op jit(solution)/shard_map/ppermute | solution.py:893
  592.5 6.4 %collective-permute-done.76 = bf16[192,768]{1,0:T(8,128)(2,1)S(1)} collective-permute-done((bf16[192,768]{1,0:T(8,128)(2,1)S(1)}, bf16[192,768]{1,0:T(8,128)(2,1)S(1)}, u32[]{:S(2)}, u32[]{:S(2)}) %collective-permute-start.76) | collective-permute-done | bytes 294944 | tf_op jit(solution)/shard_map/ppermute | solution.py:893
  599.0 4.4 collective-permute-done.78
  (303 shorter events, 118.5 us)
Async XLA Ops:
  43.0 59.0 %collective-permute-start.6 = (bf16[192,768]{1,0:T(8,128)(2,1)}, bf16[192,768]{1,0:T(8,128)(2,1)S(1)}, u32[]{:S(2)}, u32[]{:S(2)}) collective-permute-start(bf16[192,768]{1,0:T(8,128)(2,1)} %fusion.44), channel_id=1, source_target_pairs={{0,2},{1,3},{2,0},{3,1},{4,6},{5,7},{6,4},{7,5},{8,10},{9,11},{10,... | collective-permute-start | bytes 884744 | tf_op jit(solution)/shard_map/ppermute | solution.py:893
  44.6 57.4 %collective-permute-start.7 = (bf16[192,768]{1,0:T(8,128)(2,1)}, bf16[192,768]{1,0:T(8,128)(2,1)}, u32[]{:S(2)}, u32[]{:S(2)}) collective-permute-start(bf16[192,768]{1,0:T(8,128)(2,1)} %fusion.44), channel_id=1, source_target_pairs={{0,4},{1,5},{2,6},{3,7},{4,0},{5,1},{6,2},{7,3},{8,12},{9,13},{10,... | collective-permute-start | bytes 884744 | tf_op jit(solution)/shard_map/ppermute | solution.py:893
  47.2 41.7 %collective-permute-start = (bf16[48,3840]{1,0:T(8,128)(2,1)S(1)}, bf16[48,3840]{1,0:T(8,128)(2,1)S(1)}, u32[]{:S(2)}, u32[]{:S(2)}) collective-permute-start(bf16[48,3840]{1,0:T(8,128)(2,1)S(1)} %fusion.45), channel_id=1, source_target_pairs={{0,2},{1,3},{2,0},{3,1},{4,6},{5,7},{6,4},{7,5},{8,10},{9,11},{10,... | collective-permute-start | bytes 1105928 | tf_op jit(solution)/shard_map/ppermute | solution.py:893
  47.8 54.0 %collective-permute-start.1 = (bf16[48,3840]{1,0:T(8,128)(2,1)S(1)}, bf16[48,3840]{1,0:T(8,128)(2,1)S(1)}, u32[]{:S(2)}, u32[]{:S(2)}) collective-permute-start(bf16[48,3840]{1,0:T(8,128)(2,1)S(1)} %fusion.45), channel_id=1, source_target_pairs={{0,4},{1,5},{2,6},{3,7},{4,0},{5,1},{6,2},{7,3},{8,12},{9,13},{10,... | collective-permute-start | bytes 1105928 | tf_op jit(solution)/shard_map/ppermute | solution.py:893
  48.1 53.6 %collective-permute-start.2 = (bf16[48,3840]{1,0:T(8,128)(2,1)S(1)}, bf16[48,3840]{1,0:T(8,128)(2,1)S(1)}, u32[]{:S(2)}, u32[]{:S(2)}) collective-permute-start(bf16[48,3840]{1,0:T(8,128)(2,1)S(1)} %fusion.45), channel_id=1, source_target_pairs={{0,6},{1,7},{2,4},{3,5},{4,2},{5,3},{6,0},{7,1},{8,14},{9,15},{10,... | collective-permute-start | bytes 1105928 | tf_op jit(solution)/shard_map/ppermute | solution.py:893
  88.9 17.8 %collective-permute-start.8 = (bf16[192,768]{1,0:T(8,128)(2,1)}, bf16[192,768]{1,0:T(8,128)(2,1)S(1)}, u32[]{:S(2)}, u32[]{:S(2)}) collective-permute-start(bf16[192,768]{1,0:T(8,128)(2,1)} %fusion.44), channel_id=1, source_target_pairs={{0,6},{1,7},{2,4},{3,5},{4,2},{5,3},{6,0},{7,1},{8,14},{9,15},{10,... | collective-permute-start | bytes 884744 | tf_op jit(solution)/shard_map/ppermute | solution.py:893
  101.9 33.2 %collective-permute-start.3 = (bf16[4,48,3840]{2,1,0:T(8,128)(2,1)S(1)}, bf16[4,48,3840]{2,1,0:T(8,128)(2,1)}, u32[]{:S(2)}, u32[]{:S(2)}) collective-permute-start(bf16[4,48,3840]{2,1,0:T(8,128)(2,1)S(1)} %pad_maximum_fusion.ua), channel_id=1, source_target_pairs={{0,1},{1,0},{2,3},{3,2},{4,5},{5,4},{6,7},{7,6},{8,9},{9,8},{10,11... | collective-permute-start | bytes 4423688 | tf_op jit(solution)/shard_map/ppermute | solution.py:893
  107.8 40.0 %collective-permute-start.9 = (bf16[4,192,768]{2,1,0:T(8,128)(2,1)S(1)}, bf16[4,192,768]{2,1,0:T(8,128)(2,1)}, u32[]{:S(2)}, u32[]{:S(2)}) collective-permute-start(bf16[4,192,768]{2,1,0:T(8,128)(2,1)S(1)} %pad_maximum_fusion.1.da), channel_id=1, source_target_pairs={{0,1},{1,0},{2,3},{3,2},{4,5},{5,4},{6,7},{7,6},{8,9},{9,8},{10,11... | collective-permute-start | bytes 3538952 | tf_op jit(solution)/shard_map/ppermute | solution.py:893
  127.5 40.0 %collective-permute-start.4 = (bf16[4,48,3840]{2,1,0:T(8,128)(2,1)S(1)}, bf16[4,48,3840]{2,1,0:T(8,128)(2,1)}, u32[]{:S(2)}, u32[]{:S(2)}) collective-permute-start(bf16[4,48,3840]{2,1,0:T(8,128)(2,1)S(1)} %pad_maximum_fusion.ua), channel_id=1, source_target_pairs={{0,8},{8,0},{16,24},{24,16},{1,9},{9,1},{17,25},{25,17},{2,10},{10... | collective-permute-start | bytes 4423688 | tf_op jit(solution)/shard_map/ppermute | solution.py:893
  135.1 32.4 %collective-permute-start.5 = (bf16[4,48,3840]{2,1,0:T(8,128)(2,1)}, bf16[4,48,3840]{2,1,0:T(8,128)(2,1)}, u32[]{:S(2)}, u32[]{:S(2)}) collective-permute-start(bf16[4,48,3840]{2,1,0:T(8,128)(2,1)} %collective-permute-done.3.ub), channel_id=1, source_target_pairs={{0,8},{8,0},{16,24},{24,16},{1,9},{9,1},{17,25},{25,17},{2,10},{10... | collective-permute-start | bytes 4423688 | tf_op jit(solution)/shard_map/ppermute | solution.py:893
  138.4 29.1 %collective-permute-start.10 = (bf16[4,192,768]{2,1,0:T(8,128)(2,1)S(1)}, bf16[4,192,768]{2,1,0:T(8,128)(2,1)S(1)}, u32[]{:S(2)}, u32[]{:S(2)}) collective-permute-start(bf16[4,192,768]{2,1,0:T(8,128)(2,1)S(1)} %pad_maximum_fusion.1.da), channel_id=1, source_target_pairs={{0,8},{8,0},{16,24},{24,16},{1,9},{9,1},{17,25},{25,17},{2,10},{10... | collective-permute-start | bytes 3538952 | tf_op jit(solution)/shard_map/ppermute | solution.py:893
  147.8 19.8 %collective-permute-start.11 = (bf16[4,192,768]{2,1,0:T(8,128)(2,1)}, bf16[4,192,768]{2,1,0:T(8,128)(2,1)S(1)}, u32[]{:S(2)}, u32[]{:S(2)}) collective-permute-start(bf16[4,192,768]{2,1,0:T(8,128)(2,1)} %collective-permute-done.9.db), channel_id=1, source_target_pairs={{0,8},{8,0},{16,24},{24,16},{1,9},{9,1},{17,25},{25,17},{2,10},{10... | collective-permute-start | bytes 3538952 | tf_op jit(solution)/shard_map/ppermute | solution.py:893
  217.1 131.4 %collective-permute-start.12 = (f32[16,768]{1,0:T(8,128)}, f32[16,768]{1,0:T(8,128)S(1)}, u32[]{:S(2)}, u32[]{:S(2)}) collective-permute-start(f32[16,768]{1,0:T(8,128)} %get-tuple-element.85), channel_id=1, source_target_pairs={{0,8},{8,0},{16,24},{24,16},{1,9},{9,1},{17,25},{25,17},{2,10},{10... | collective-permute-start | bytes 147464 | tf_op jit(solution)/shard_map/ppermute | solution.py:893
  329.6 11.4 %collective-permute-start.50 = (f32[8,768]{1,0:T(8,128)S(1)}, f32[8,768]{1,0:T(8,128)S(1)}, u32[]{:S(2)}, u32[]{:S(2)}) collective-permute-start(f32[8,768]{1,0:T(8,128)S(1)} %constant_dynamic-update-slice_fusion), channel_id=1, source_target_pairs={{0,8},{8,0},{16,24},{24,16},{1,9},{9,1},{17,25},{25,17},{2,10},{10... | collective-permute-start | bytes 73736 | tf_op jit(solution)/shard_map/ppermute | solution.py:893
  348.5 185.5 %collective-permute-start.71 = (bf16[8,192,768]{2,1,0:T(8,128)(2,1)}, bf16[8,192,768]{2,1,0:T(8,128)(2,1)}, u32[]{:S(2)}, u32[]{:S(2)}) collective-permute-start(bf16[8,192,768]{2,1,0:T(8,128)(2,1)} %get-tuple-element.115), channel_id=1, source_target_pairs={{0,8},{8,0},{16,24},{24,16},{1,9},{9,1},{17,25},{25,17},{2,10},{10... | collective-permute-start | bytes 7077896 | tf_op jit(solution)/shard_map/ppermute | solution.py:893
  348.6 35.0 %collective-permute-start.13 = (f32[16,768]{1,0:T(8,128)S(1)}, f32[16,768]{1,0:T(8,128)S(1)}, u32[]{:S(2)}, u32[]{:S(2)}) collective-permute-start(f32[16,768]{1,0:T(8,128)S(1)} %add.237), channel_id=1, source_target_pairs={{0,16},{8,24},{16,0},{24,8},{1,17},{9,25},{17,1},{25,9},{2,18},{10... | collective-permute-start | bytes 147464 | tf_op jit(solution)/shard_map/ppermute | solution.py:893
  350.8 33.9 %collective-permute-start.53 = (f32[8,768]{1,0:T(8,128)S(1)}, f32[8,768]{1,0:T(8,128)S(1)}, u32[]{:S(2)}, u32[]{:S(2)}) collective-permute-start(f32[8,768]{1,0:T(8,128)S(1)} %add.274), channel_id=1, source_target_pairs={{0,2},{1,3},{2,0},{3,1},{4,6},{5,7},{6,4},{7,5},{8,10},{9,11},{10,... | collective-permute-start | bytes 73736 | tf_op jit(solution)/shard_map/ppermute | solution.py:893
  383.6 115.9 %collective-permute-start.63 = (bf16[8,48,3072]{2,1,0:T(8,128)(2,1)}, bf16[8,48,3072]{2,1,0:T(8,128)(2,1)}, u32[]{:S(2)}, u32[]{:S(2)}) collective-permute-start(bf16[8,48,3072]{2,1,0:T(8,128)(2,1)} %get-tuple-element.111), channel_id=1, source_target_pairs={{0,8},{8,0},{16,24},{24,16},{1,9},{9,1},{17,25},{25,17},{2,10},{10... | collective-permute-start | bytes 7077896 | tf_op jit(solution)/shard_map/ppermute | solution.py:893
  390.5 17.4 %collective-permute-start.55 = (bf16[8,48,768]{2,1,0:T(8,128)(2,1)}, bf16[8,48,768]{2,1,0:T(8,128)(2,1)}, u32[]{:S(2)}, u32[]{:S(2)}) collective-permute-start(bf16[8,48,768]{2,1,0:T(8,128)(2,1)} %get-tuple-element.107), channel_id=1, source_target_pairs={{0,8},{8,0},{16,24},{24,16},{1,9},{9,1},{17,25},{25,17},{2,10},{10... | collective-permute-start | bytes 1769480 | tf_op jit(solution)/shard_map/ppermute | solution.py:893
  390.8 13.3 %collective-permute-start.24 = (bf16[2,512,256]{2,1,0:T(8,128)(2,1)}, bf16[2,512,256]{2,1,0:T(8,128)(2,1)S(1)}, u32[]{:S(2)}, u32[]{:S(2)}) collective-permute-start(bf16[2,512,256]{2,1,0:T(8,128)(2,1)} %get-tuple-element.117), channel_id=1, source_target_pairs={{0,8},{8,0},{16,24},{24,16},{1,9},{9,1},{17,25},{25,17},{2,10},{10... | collective-permute-start | bytes 1572872 | tf_op jit(solution)/shard_map/ppermute | solution.py:893
  409.4 9.9 %collective-permute-start.56 = (bf16[4,48,768]{2,1,0:T(8,128)(2,1)S(1)}, bf16[4,48,768]{2,1,0:T(8,128)(2,1)S(1)}, u32[]{:S(2)}, u32[]{:S(2)}) collective-permute-start(bf16[4,48,768]{2,1,0:T(8,128)(2,1)S(1)} %slice.342), channel_id=1, source_target_pairs={{0,1},{1,0},{2,3},{3,2},{4,5},{5,4},{6,7},{7,6},{8,9},{9,8},{10,11... | collective-permute-start | bytes 884744 | tf_op jit(solution)/shard_map/ppermute | solution.py:893
  410.8 14.8 %collective-permute-start.27 = (bf16[4,48,768]{2,1,0:T(8,128)(2,1)S(1)}, bf16[4,48,768]{2,1,0:T(8,128)(2,1)S(1)}, u32[]{:S(2)}, u32[]{:S(2)}) collective-permute-start(bf16[4,48,768]{2,1,0:T(8,128)(2,1)S(1)} %slice.313), channel_id=1, source_target_pairs={{0,1},{1,0},{2,3},{3,2},{4,5},{5,4},{6,7},{7,6},{8,9},{9,8},{10,11... | collective-permute-start | bytes 884744 | tf_op jit(solution)/shard_map/ppermute | solution.py:893
  412.0 20.0 %collective-permute-start.35 = (bf16[4,48,768]{2,1,0:T(8,128)(2,1)S(1)}, bf16[4,48,768]{2,1,0:T(8,128)(2,1)S(1)}, u32[]{:S(2)}, u32[]{:S(2)}) collective-permute-start(bf16[4,48,768]{2,1,0:T(8,128)(2,1)S(1)} %slice.320), channel_id=1, source_target_pairs={{0,1},{1,0},{2,3},{3,2},{4,5},{5,4},{6,7},{7,6},{8,9},{9,8},{10,11... | collective-permute-start | bytes 884744 | tf_op jit(solution)/shard_map/ppermute | solution.py:893
  419.3 18.4 %collective-permute-start.43 = (bf16[4,48,768]{2,1,0:T(8,128)(2,1)S(1)}, bf16[4,48,768]{2,1,0:T(8,128)(2,1)S(1)}, u32[]{:S(2)}, u32[]{:S(2)}) collective-permute-start(bf16[4,48,768]{2,1,0:T(8,128)(2,1)S(1)} %slice.327), channel_id=1, source_target_pairs={{0,1},{1,0},{2,3},{3,2},{4,5},{5,4},{6,7},{7,6},{8,9},{9,8},{10,11... | collective-permute-start | bytes 884744 | tf_op jit(solution)/shard_map/ppermute | solution.py:893
  425.7 14.5 %collective-permute-start.57 = (bf16[48,768]{1,0:T(8,128)(2,1)S(1)}, bf16[48,768]{1,0:T(8,128)(2,1)S(1)}, u32[]{:S(2)}, u32[]{:S(2)}) collective-permute-start(bf16[48,768]{1,0:T(8,128)(2,1)S(1)} %get-tuple-element.128), channel_id=1, source_target_pairs={{0,2},{1,3},{2,0},{3,1},{4,6},{5,7},{6,4},{7,5},{8,10},{9,11},{10,... | collective-permute-start | bytes 221192 | tf_op jit(solution)/shard_map/ppermute | solution.py:893
  432.0 9.4 %collective-permute-start.58 = (bf16[48,768]{1,0:T(8,128)(2,1)S(1)}, bf16[48,768]{1,0:T(8,128)(2,1)S(1)}, u32[]{:S(2)}, u32[]{:S(2)}) collective-permute-start(bf16[48,768]{1,0:T(8,128)(2,1)S(1)} %get-tuple-element.130), channel_id=1, source_target_pairs={{0,4},{1,5},{2,6},{3,7},{4,0},{5,1},{6,2},{7,3},{8,12},{9,13},{10,... | collective-permute-start | bytes 221192 | tf_op jit(solution)/shard_map/ppermute | solution.py:893
  441.4 7.6 %collective-permute-start.29 = (bf16[48,768]{1,0:T(8,128)(2,1)S(1)}, bf16[48,768]{1,0:T(8,128)(2,1)S(1)}, u32[]{:S(2)}, u32[]{:S(2)}) collective-permute-start(bf16[48,768]{1,0:T(8,128)(2,1)S(1)} %get-tuple-element.142), channel_id=1, source_target_pairs={{0,4},{1,5},{2,6},{3,7},{4,0},{5,1},{6,2},{7,3},{8,12},{9,13},{10,... | collective-permute-start | bytes 221192 | tf_op jit(solution)/shard_map/ppermute | solution.py:893
  459.9 43.3 %collective-permute-start.23 = (bf16[2,512,256]{2,1,0:T(8,128)(2,1)S(1)}, bf16[2,512,256]{2,1,0:T(8,128)(2,1)S(1)}, u32[]{:S(2)}, u32[]{:S(2)}) collective-permute-start(bf16[2,512,256]{2,1,0:T(8,128)(2,1)S(1)} %copy-done.19), channel_id=1, source_target_pairs={{0,8},{8,0},{16,24},{24,16},{1,9},{9,1},{17,25},{25,17},{2,10},{10... | collective-permute-start | bytes 1572872 | tf_op jit(solution)/shard_map/ppermute | solution.py:893
  463.8 15.6 %collective-permute-start.61 = (bf16[48,768]{1,0:T(8,128)(2,1)S(1)}, bf16[48,768]{1,0:T(8,128)(2,1)S(1)}, u32[]{:S(2)}, u32[]{:S(2)}) collective-permute-start(bf16[48,768]{1,0:T(8,128)(2,1)S(1)} %fusion.8), channel_id=1, source_target_pairs={{0,8},{8,0},{16,24},{24,16},{1,9},{9,1},{17,25},{25,17},{2,10},{10... | collective-permute-start | bytes 221192 | tf_op jit(solution)/shard_map/ppermute | solution.py:893
  493.3 10.8 %collective-permute-start.20 = (bf16[2,512,256]{2,1,0:T(8,128)(2,1)S(1)}, bf16[2,512,256]{2,1,0:T(8,128)(2,1)S(1)}, u32[]{:S(2)}, u32[]{:S(2)}) collective-permute-start(bf16[2,512,256]{2,1,0:T(8,128)(2,1)S(1)} %copy-done.21), channel_id=1, source_target_pairs={{0,8},{8,0},{16,24},{24,16},{1,9},{9,1},{17,25},{25,17},{2,10},{10... | collective-permute-start | bytes 1572872 | tf_op jit(solution)/shard_map/ppermute | solution.py:893
  496.6 14.8 %collective-permute-start.25 = (bf16[2,512,256]{2,1,0:T(8,128)(2,1)S(1)}, bf16[2,512,256]{2,1,0:T(8,128)(2,1)S(1)}, u32[]{:S(2)}, u32[]{:S(2)}) collective-permute-start(bf16[2,512,256]{2,1,0:T(8,128)(2,1)S(1)} %add_convert_fusion.9), channel_id=1, source_target_pairs={{0,16},{8,24},{16,0},{24,8},{1,17},{9,25},{17,1},{25,9},{2,18},{10... | collective-permute-start | bytes 1572872 | tf_op jit(solution)/shard_map/ppermute | solution.py:893
  499.5 23.1 %collective-permute-start.22 = (bf16[2,512,256]{2,1,0:T(8,128)(2,1)S(1)}, bf16[2,512,256]{2,1,0:T(8,128)(2,1)S(1)}, u32[]{:S(2)}, u32[]{:S(2)}) collective-permute-start(bf16[2,512,256]{2,1,0:T(8,128)(2,1)S(1)} %add_convert_fusion.11), channel_id=1, source_target_pairs={{0,16},{8,24},{16,0},{24,8},{1,17},{9,25},{17,1},{25,9},{2,18},{10... | collective-permute-start | bytes 1572872 | tf_op jit(solution)/shard_map/ppermute | solution.py:893
  504.1 20.8 %collective-permute-start.17 = (bf16[2,512,256]{2,1,0:T(8,128)(2,1)S(1)}, bf16[2,512,256]{2,1,0:T(8,128)(2,1)S(1)}, u32[]{:S(2)}, u32[]{:S(2)}) collective-permute-start(bf16[2,512,256]{2,1,0:T(8,128)(2,1)S(1)} %copy-done.20), channel_id=1, source_target_pairs={{0,8},{8,0},{16,24},{24,16},{1,9},{9,1},{17,25},{25,17},{2,10},{10... | collective-permute-start | bytes 1572872 | tf_op jit(solution)/shard_map/ppermute | solution.py:893
  504.1 29.0 %collective-permute-start.19 = (bf16[2,512,256]{2,1,0:T(8,128)(2,1)S(1)}, bf16[2,512,256]{2,1,0:T(8,128)(2,1)S(1)}, u32[]{:S(2)}, u32[]{:S(2)}) collective-permute-start(bf16[2,512,256]{2,1,0:T(8,128)(2,1)S(1)} %add_convert_fusion.13), channel_id=1, source_target_pairs={{0,16},{8,24},{16,0},{24,8},{1,17},{9,25},{17,1},{25,9},{2,18},{10... | collective-permute-start | bytes 1572872 | tf_op jit(solution)/shard_map/ppermute | solution.py:893
  511.4 26.5 %collective-permute-start.64 = (bf16[4,48,3072]{2,1,0:T(8,128)(2,1)S(1)}, bf16[4,48,3072]{2,1,0:T(8,128)(2,1)S(1)}, u32[]{:S(2)}, u32[]{:S(2)}) collective-permute-start(bf16[4,48,3072]{2,1,0:T(8,128)(2,1)S(1)} %slice.351), channel_id=1, source_target_pairs={{0,1},{1,0},{2,3},{3,2},{4,5},{5,4},{6,7},{7,6},{8,9},{9,8},{10,11... | collective-permute-start | bytes 3538952 | tf_op jit(solution)/shard_map/ppermute | solution.py:893
  536.4 27.2 %collective-permute-start.72 = (bf16[4,192,768]{2,1,0:T(8,128)(2,1)S(1)}, bf16[4,192,768]{2,1,0:T(8,128)(2,1)S(1)}, u32[]{:S(2)}, u32[]{:S(2)}) collective-permute-start(bf16[4,192,768]{2,1,0:T(8,128)(2,1)S(1)} %slice.358), channel_id=1, source_target_pairs={{0,1},{1,0},{2,3},{3,2},{4,5},{5,4},{6,7},{7,6},{8,9},{9,8},{10,11... | collective-permute-start | bytes 3538952 | tf_op jit(solution)/shard_map/ppermute | solution.py:893
  538.3 30.2 %collective-permute-start.65 = (bf16[48,3072]{1,0:T(8,128)(2,1)S(1)}, bf16[48,3072]{1,0:T(8,128)(2,1)S(1)}, u32[]{:S(2)}, u32[]{:S(2)}) collective-permute-start(bf16[48,3072]{1,0:T(8,128)(2,1)S(1)} %get-tuple-element.125), channel_id=1, source_target_pairs={{0,2},{1,3},{2,0},{3,1},{4,6},{5,7},{6,4},{7,5},{8,10},{9,11},{10,... | collective-permute-start | bytes 884744 | tf_op jit(solution)/shard_map/ppermute | solution.py:893
  539.5 29.0 %collective-permute-start.66 = (bf16[48,3072]{1,0:T(8,128)(2,1)S(1)}, bf16[48,3072]{1,0:T(8,128)(2,1)S(1)}, u32[]{:S(2)}, u32[]{:S(2)}) collective-permute-start(bf16[48,3072]{1,0:T(8,128)(2,1)S(1)} %get-tuple-element.127), channel_id=1, source_target_pairs={{0,4},{1,5},{2,6},{3,7},{4,0},{5,1},{6,2},{7,3},{8,12},{9,13},{10,... | collective-permute-start | bytes 884744 | tf_op jit(solution)/shard_map/ppermute | solution.py:893
  542.8 25.8 %collective-permute-start.67 = (bf16[48,3072]{1,0:T(8,128)(2,1)S(1)}, bf16[48,3072]{1,0:T(8,128)(2,1)S(1)}, u32[]{:S(2)}, u32[]{:S(2)}) collective-permute-start(bf16[48,3072]{1,0:T(8,128)(2,1)S(1)} %get-tuple-element.126), channel_id=1, source_target_pairs={{0,6},{1,7},{2,4},{3,5},{4,2},{5,3},{6,0},{7,1},{8,14},{9,15},{10,... | collective-permute-start | bytes 884744 | tf_op jit(solution)/shard_map/ppermute | solution.py:893
  563.9 14.7 %collective-permute-start.73 = (bf16[192,768]{1,0:T(8,128)(2,1)S(1)}, bf16[192,768]{1,0:T(8,128)(2,1)S(1)}, u32[]{:S(2)}, u32[]{:S(2)}) collective-permute-start(bf16[192,768]{1,0:T(8,128)(2,1)S(1)} %get-tuple-element.122), channel_id=1, source_target_pairs={{0,2},{1,3},{2,0},{3,1},{4,6},{5,7},{6,4},{7,5},{8,10},{9,11},{10,... | collective-permute-start | bytes 884744 | tf_op jit(solution)/shard_map/ppermute | solution.py:893
  565.3 23.8 %collective-permute-start.74 = (bf16[192,768]{1,0:T(8,128)(2,1)S(1)}, bf16[192,768]{1,0:T(8,128)(2,1)S(1)}, u32[]{:S(2)}, u32[]{:S(2)}) collective-permute-start(bf16[192,768]{1,0:T(8,128)(2,1)S(1)} %get-tuple-element.124), channel_id=1, source_target_pairs={{0,4},{1,5},{2,6},{3,7},{4,0},{5,1},{6,2},{7,3},{8,12},{9,13},{10,... | collective-permute-start | bytes 884744 | tf_op jit(solution)/shard_map/ppermute | solution.py:893
  568.5 20.6 %collective-permute-start.75 = (bf16[192,768]{1,0:T(8,128)(2,1)S(1)}, bf16[192,768]{1,0:T(8,128)(2,1)S(1)}, u32[]{:S(2)}, u32[]{:S(2)}) collective-permute-start(bf16[192,768]{1,0:T(8,128)(2,1)S(1)} %get-tuple-element.123), channel_id=1, source_target_pairs={{0,6},{1,7},{2,4},{3,5},{4,2},{5,3},{6,0},{7,1},{8,14},{9,15},{10,... | collective-permute-start | bytes 884744 | tf_op jit(solution)/shard_map/ppermute | solution.py:893
  568.7 22.7 %collective-permute-start.68 = (bf16[48,3072]{1,0:T(8,128)(2,1)S(1)}, bf16[48,3072]{1,0:T(8,128)(2,1)S(1)}, u32[]{:S(2)}, u32[]{:S(2)}) collective-permute-start(bf16[48,3072]{1,0:T(8,128)(2,1)S(1)} %fusion.5), channel_id=1, source_target_pairs={{0,16},{8,24},{16,0},{24,8},{1,17},{9,25},{17,1},{25,9},{2,18},{10... | collective-permute-start | bytes 884744 | tf_op jit(solution)/shard_map/ppermute | solution.py:893
  589.2 9.6 %collective-permute-start.76 = (bf16[192,768]{1,0:T(8,128)(2,1)S(1)}, bf16[192,768]{1,0:T(8,128)(2,1)S(1)}, u32[]{:S(2)}, u32[]{:S(2)}) collective-permute-start(bf16[192,768]{1,0:T(8,128)(2,1)S(1)} %fusion.2), channel_id=1, source_target_pairs={{0,16},{8,24},{16,0},{24,8},{1,17},{9,25},{17,1},{25,9},{2,18},{10... | collective-permute-start | bytes 884744 | tf_op jit(solution)/shard_map/ppermute | solution.py:893
  590.2 8.8 %collective-permute-start.77 = (bf16[192,768]{1,0:T(8,128)(2,1)S(1)}, bf16[192,768]{1,0:T(8,128)(2,1)S(1)}, u32[]{:S(2)}, u32[]{:S(2)}) collective-permute-start(bf16[192,768]{1,0:T(8,128)(2,1)S(1)} %fusion.2), channel_id=1, source_target_pairs={{0,8},{8,0},{16,24},{24,16},{1,9},{9,1},{17,25},{25,17},{2,10},{10... | collective-permute-start | bytes 884744 | tf_op jit(solution)/shard_map/ppermute | solution.py:893
  590.2 13.2 %collective-permute-start.78 = (bf16[192,768]{1,0:T(8,128)(2,1)S(1)}, bf16[192,768]{1,0:T(8,128)(2,1)S(1)}, u32[]{:S(2)}, u32[]{:S(2)}) collective-permute-start(bf16[192,768]{1,0:T(8,128)(2,1)S(1)} %fusion.2), channel_id=1, source_target_pairs={{0,24},{8,16},{16,8},{24,0},{1,25},{9,17},{17,9},{25,1},{2,26},{10... | collective-permute-start | bytes 884744 | tf_op jit(solution)/shard_map/ppermute | solution.py:893
  591.5 13.1 %collective-permute-start.69 = (bf16[48,3072]{1,0:T(8,128)(2,1)S(1)}, bf16[48,3072]{1,0:T(8,128)(2,1)S(1)}, u32[]{:S(2)}, u32[]{:S(2)}) collective-permute-start(bf16[48,3072]{1,0:T(8,128)(2,1)S(1)} %fusion.5), channel_id=1, source_target_pairs={{0,8},{8,0},{16,24},{24,16},{1,9},{9,1},{17,25},{25,17},{2,10},{10... | collective-permute-start | bytes 884744 | tf_op jit(solution)/shard_map/ppermute | solution.py:893
  591.5 15.6 %collective-permute-start.70 = (bf16[48,3072]{1,0:T(8,128)(2,1)S(1)}, bf16[48,3072]{1,0:T(8,128)(2,1)S(1)}, u32[]{:S(2)}, u32[]{:S(2)}) collective-permute-start(bf16[48,3072]{1,0:T(8,128)(2,1)S(1)} %fusion.5), channel_id=1, source_target_pairs={{0,24},{8,16},{16,8},{24,0},{1,25},{9,17},{17,9},{25,1},{2,26},{10... | collective-permute-start | bytes 884744 | tf_op jit(solution)/shard_map/ppermute | solution.py:893
  (62 other events, 440.7 us)

commit v2 on v1

--- a/solution.py
+++ b/solution.py
@@ -276,7 +276,7 @@
     )
 
 
-def project_kernel(tok, oth, wq, wk, wv, qb, vb, q, k, v, qn, kn):
+def project_kernel(tok, oth, wq, wk, wv, qb, vb, q, k, v, xt, qn, kn):
     step = pl.program_id(0)
     own = (step == 0) | (step == 4)
     width = wq.shape[0]
@@ -299,6 +299,7 @@
         k[...] = keys_low
         kn[...] = jnp.maximum(kn[...], norms(keys_low))
         v[...] = (dot(rows, wv[...], NN) + vb[...].astype(f32)).astype(bf16)
+        xt[...] = jnp.transpose(rows)
 
     @pl.when(own)
     def _():
@@ -331,12 +332,14 @@
             pl.BlockSpec(block, lambda i: (i // 4, 0)),
             pl.BlockSpec(block, lambda i: (i, 0)),
             pl.BlockSpec(block, lambda i: (i, 0)),
+            pl.BlockSpec((width, PPIECE), lambda i: (0, i)),
             small, small,
         ],
         out_shape=[
             jax.ShapeDtypeStruct((1024, width), bf16),
             jax.ShapeDtypeStruct((2560, width), bf16),
             jax.ShapeDtypeStruct((2560, width), bf16),
+            jax.ShapeDtypeStruct((width, 2560), bf16),
             jax.ShapeDtypeStruct((8, 128), f32),
             jax.ShapeDtypeStruct((8, 128), f32),
         ],
@@ -376,7 +379,7 @@
     return jnp.where(row == col, 0.0, bias)
 
 
-def attend_kernel(q, k, v, kb, brow, qn, kn, o, side, qx, qd, kx, vx, pm, pc, bown, bcont, top):
+def attend_kernel(q, k, v, kb, brow, qn, kn, o_in, side_in, o, side, qx, qd, kx, vx, pm, pc, bown, bcont, top):
     @pl.when(pl.program_id(0) == 0)
     def _():
         for head in range(2):
@@ -455,27 +458,29 @@
     o[...] = jnp.where(lane < 64, outs[0], outs[1]).astype(bf16)
 
 
-def attend(q, k, v, kb, brow, qn, kn, first, count):
+def attend(q, k, v, kb, brow, qn, kn, outs, first, count):
     def pair(rows):
         return pl.BlockSpec((rows, 128), lambda i: (0, i + first))
 
     def fixed(*shape):
         return pl.BlockSpec(shape, lambda i: (0,) * len(shape))
 
+    kernel = attend_kernel if outs else functools.partial(fresh, attend_kernel)
+    width = q.shape[1]
     return pl.pallas_call(
-        attend_kernel,
+        kernel,
         grid=(count,),
         in_specs=[
             pair(1024), pair(2560), pair(2560), fixed(2560, 128), fixed(8, 2560),
             fixed(8, 128), fixed(8, 128),
-        ],
+        ] + [ANY] * len(outs),
         out_specs=[
-            pl.BlockSpec((1024, 128), lambda i: (0, i)),
-            pl.BlockSpec((2, 1024, 128), lambda i: (i, 0, 0)),
+            pair(1024),
+            pl.BlockSpec((2, 1024, 128), lambda i: (i + first, 0, 0)),
         ],
         out_shape=[
-            jax.ShapeDtypeStruct((1024, 128 * count), bf16),
-            jax.ShapeDtypeStruct((2 * count, 1024, 128), bf16),
+            jax.ShapeDtypeStruct((1024, width), bf16),
+            jax.ShapeDtypeStruct((width // HDIM, 1024, 128), bf16),
         ],
         scratch_shapes=[
             pltpu.VMEM((2, 1024, 256), bf16),
@@ -488,23 +493,27 @@
             pltpu.VMEM((2, 256, 256), f32),
             pltpu.VMEM((2, 1024, 128), f32),
         ],
+        input_output_aliases={7: 0, 8: 1} if outs else {},
         compiler_params=params(),
         cost_estimate=cost(7.0 * count, 3 * count),
-    )(q, k, v, kb, brow, qn, kn)
-
-
-def attend_back_kernel(
-    q, k, v, d, o, side, kb, dq, dkv, qx, qd, kx, vx, dx, qm, kt, pt, st, pc, sc, bown, bcont
-):
+    )(q, k, v, kb, brow, qn, kn, *outs)
+
+
+def fresh(kernel, *refs):
+    return kernel(*refs[:7], None, None, *refs[7:])
+
+
+def back_fill(q, k, v, d, o, side, kb, qx, qd, kx, vx, dx, qm, kt, bown, bcont):
     @pl.when(pl.program_id(0) == 0)
     def _():
         for head in range(2):
             kx[head, :, 128:] = kb[...]
         vx[:, 128:] = kb[...]
         column = kb[:, 0:1].astype(f32)
-        bown[...] = off_diagonal(512, column[:512])
+        bown[...] = off_diagonal(512, column[:512]).astype(bf16)
         for c in range(2):
-            bcont[c] = off_diagonal(256, column[2048 + 256 * c : 2304 + 256 * c])
+            keys = slice(2048 + 256 * c, 2304 + 256 * c)
+            bcont[c] = off_diagonal(256, column[keys]).astype(bf16)
 
     lane = lane_of(1024)
     vx[:, :128] = v[...]
@@ -523,93 +532,443 @@
         inner = jnp.sum(head_only(product, head), axis=1, keepdims=True)
         dx[head, :, 128:] = side_lanes(0.0, jnp.broadcast_to(inner, (1024, 128)))
 
-    dq_rows = []
-    for head in range(2):
-        def tile(keys, rows, queries, bias=None):
-            scores = dot(kx[head, keys], queries[head, rows], NT)
-            if bias is not None:
-                scores = scores + bias
-            probs = jnp.exp2(scores)
-            return probs, probs * dot(vx[keys], dx[head, rows], NT)
-
-        for c in range(3):
-            keys = slice(512 + 512 * c, 1024 + 512 * c)
-            probs, delta = tile(keys, slice(0, 1024), qx)
-            pt[head, keys] = probs.astype(bf16)
-            st[head, keys] = delta.astype(bf16)
-        probs, delta = tile(slice(0, 512), slice(512, 1024), qx)
-        pt[head, :512, 512:] = probs.astype(bf16)
-        st[head, :512, 512:] = delta.astype(bf16)
-        probs, delta = tile(slice(0, 512), slice(0, 512), qd, bown[...])
-        pt[head, :512, :512] = probs.astype(bf16)
-        st[head, :512, :512] = delta.astype(bf16)
-        for c in range(2):
-            keys = slice(2048 + 256 * c, 2304 + 256 * c)
-            rows = slice(512 + 256 * c, 768 + 256 * c)
-            probs, delta = tile(keys, rows, qd, bcont[c])
-            pc[head, c] = probs.astype(bf16)
-            sc[head, c] = delta.astype(bf16)
-        kth = kt[64 * head : 64 * head + 64]
-        main = dot(kth[:, :2048], st[head], NN)
-        extra = [dot(kth[:, 2048 + 256 * c : 2304 + 256 * c], sc[head, c], NN) for c in range(2)]
-        dq_rows.append(
-            jnp.concatenate(
-                [main[:, :512], main[:, 512:768] + extra[0], main[:, 768:] + extra[1]], axis=1
-            )
-        )
-    dq[...] = jnp.transpose(jnp.concatenate(dq_rows, axis=0) * SCALE).astype(bf16)
-    dkv[1, :2048] = (dot(pt[0], dx[0, :, :128], NN) + dot(pt[1], dx[1, :, :128], NN)).astype(bf16)
-    dkv[0, :2048] = ((dot(st[0], qm[0], NN) + dot(st[1], qm[1], NN)) * SCALE).astype(bf16)
+
+def back_head(head, qx, qd, kx, vx, dx, qm, kt, pt, st, pc, sc, bown, bcont):
+    def tile(keys, rows, queries, bias=None):
+        scores = dot(kx[head, keys], queries[head, rows], NT)
+        if bias is not None:
+            scores = scores + bias.astype(f32)
+        probs = jnp.exp2(scores)
+        return probs.astype(bf16), (probs * dot(vx[keys], dx[head, rows], NT)).astype(bf16)
+
+    for c in range(3):
+        keys = slice(512 + 512 * c, 1024 + 512 * c)
+        pt[keys], st[keys] = tile(keys, slice(0, 1024), qx)
+    pt[:512, 512:], st[:512, 512:] = tile(slice(0, 512), slice(512, 1024), qx)
+    pt[:512, :512], st[:512, :512] = tile(slice(0, 512), slice(0, 512), qd, bown[...])
+    for c in range(2):
+        keys = slice(2048 + 256 * c, 2304 + 256 * c)
+        pc[c], sc[c] = tile(keys, slice(512 + 256 * c, 768 + 256 * c), qd, bcont[c])
+    kth = kt[64 * head : 64 * head + 64]
+    main = dot(kth[:, :2048], st[...], NN)
+    extra = [dot(kth[:, 2048 + 256 * c : 2304 + 256 * c], sc[c], NN) for c in range(2)]
+    rows = jnp.concatenate(
+        [main[:, :512], main[:, 512:768] + extra[0], main[:, 768:] + extra[1]], axis=1
+    )
+    return rows
+
+
+def back_keys(head, dx, qm, pt, st, pc, sc, acc):
+    def put(keys, cols, value):
+        if head == 0:
+            acc[keys, cols] = value
+        else:
+            acc[keys, cols] += value
+
+    left, right = slice(0, 128), slice(128, 256)
+    put(slice(0, 2048), left, dot(st[...], qm[head], NN) * SCALE)
+    put(slice(0, 2048), right, dot(pt[...], dx[head, :, :128], NN))
     for c in range(2):
         keys = slice(2048 + 256 * c, 2304 + 256 * c)
         rows = slice(512 + 256 * c, 768 + 256 * c)
-        dkv[1, keys] = (
-            dot(pc[0, c], dx[0, rows, :128], NN) + dot(pc[1, c], dx[1, rows, :128], NN)
-        ).astype(bf16)
-        dkv[0, keys] = (
-            (dot(sc[0, c], qm[0, rows], NN) + dot(sc[1, c], qm[1, rows], NN)) * SCALE
-        ).astype(bf16)
-
-
-def attend_back(q, k, v, d, o, side, kb, first, count):
+        put(keys, left, dot(sc[c], qm[head, rows], NN) * SCALE)
+        put(keys, right, dot(pc[c], dx[head, rows, :128], NN))
+
+
+BACK_SCRATCH = [
+    pltpu.VMEM((2, 1024, 256), bf16),
+    pltpu.VMEM((2, 1024, 256), bf16),
+    pltpu.VMEM((2, 2560, 256), bf16),
+    pltpu.VMEM((2560, 256), bf16),
+    pltpu.VMEM((2, 1024, 256), bf16),
+    pltpu.VMEM((2, 1024, 128), bf16),
+    pltpu.VMEM((128, 2560), bf16),
+    pltpu.VMEM((2048, 1024), bf16),
+    pltpu.VMEM((2048, 1024), bf16),
+    pltpu.VMEM((2, 256, 256), bf16),
+    pltpu.VMEM((2, 256, 256), bf16),
+    pltpu.VMEM((512, 512), bf16),
+    pltpu.VMEM((2, 256, 256), bf16),
+    pltpu.VMEM((2560, 256), f32),
+]
+
+
+def back_specs():
     def pair(rows):
-        return pl.BlockSpec((rows, 128), lambda i: (0, i + first))
-
+        return pl.BlockSpec((rows, 128), lambda i: (0, i))
+
+    def once(*shape):
+        return pl.BlockSpec(shape, lambda i: (0,) * len(shape), pipeline_mode=pl.Buffered(1))
+
+    return [
+        pair(1024), pair(2560), pair(2560), pair(1024), pair(1024),
+        pl.BlockSpec((2, 1024, 128), lambda i: (i, 0, 0)),
+        once(2560, 128), once(768, 2560),
+    ]
+
+
+def back_alone_kernel(q, k, v, d, o, side, kb, xt, dq, cont, partial_rows, whole, *scratch):
+    (qx, qd, kx, vx, dx, qm, kt, pt, st, pc, sc, bown, bcont, acc) = scratch
+    back_fill(q, k, v, d, o, side, kb, qx, qd, kx, vx, dx, qm, kt, bown, bcont)
+    rows = []
+    for head in range(2):
+        rows.append(back_head(head, qx, qd, kx, vx, dx, qm, kt, pt, st, pc, sc, bown, bcont))
+        back_keys(head, dx, qm, pt, st, pc, sc, acc)
+    delta = jnp.transpose(jnp.concatenate(rows, axis=0) * SCALE).astype(bf16)
+    dq[...] = delta
+    low = acc[...].astype(bf16)
+    partial_rows[...] = low[:2048]
+    cont[...] = low[2048:]
+    grad = dot(xt[:, :512], delta[:512], NN) + dot(xt[:, 2048:], delta[512:], NN)
+    whole[:, :128] = grad.astype(bf16)
+    whole[:, 128:] = dot(xt[...], low, NN).astype(bf16)
+
+
+def attend_back_alone(q, k, v, d, o, side, kb, xt):
+    width = q.shape[1]
+    count = width // 128
     return pl.pallas_call(
-        attend_back_kernel,
+        back_alone_kernel,
         grid=(count,),
-        in_specs=[
-            pair(1024), pair(2560), pair(2560), pair(1024),
-            pl.BlockSpec((1024, 128), lambda i: (0, i)),
-            pl.BlockSpec((2, 1024, 128), lambda i: (i, 0, 0)),
-            pl.BlockSpec((2560, 128), lambda i: (0, 0)),
-        ],
+        in_specs=back_specs(),
         out_specs=[
             pl.BlockSpec((1024, 128), lambda i: (0, i)),
-            pl.BlockSpec((2, 2560, 128), lambda i: (0, 0, i)),
+            pl.BlockSpec((512, 256), lambda i: (0, i)),
+            pl.BlockSpec((2048, 256), lambda i: (0, i)),
+            pl.BlockSpec((width, 384), lambda i: (0, i)),
         ],
         out_shape=[
-            jax.ShapeDtypeStruct((1024, 128 * count), bf16),
-            jax.ShapeDtypeStruct((2, 2560, 128 * count), bf16),
+            jax.ShapeDtypeStruct((1024, width), bf16),
+            jax.ShapeDtypeStruct((512, 2 * width), bf16),
+            jax.ShapeDtypeStruct((2048, 2 * width), bf16),
+            jax.ShapeDtypeStruct((width, 3 * width), bf16),
         ],
-        scratch_shapes=[
-            pltpu.VMEM((2, 1024, 256), bf16),
-            pltpu.VMEM((2, 1024, 256), bf16),
-            pltpu.VMEM((2, 2560, 256), bf16),
-            pltpu.VMEM((2560, 256), bf16),
-            pltpu.VMEM((2, 1024, 256), bf16),
-            pltpu.VMEM((2, 1024, 128), bf16),
-            pltpu.VMEM((128, 2560), bf16),
-            pltpu.VMEM((2, 2048, 1024), bf16),
-            pltpu.VMEM((2, 2048, 1024), bf16),
-            pltpu.VMEM((2, 2, 256, 256), bf16),
-            pltpu.VMEM((2, 2, 256, 256), bf16),
-            pltpu.VMEM((512, 512), f32),
-            pltpu.VMEM((2, 256, 256), f32),
+        scratch_shapes=BACK_SCRATCH,
+        compiler_params=params(60),
+        cost_estimate=cost(100, 40),
+    )(q, k, v, d, o, side, kb, xt)
+
+
+PAIRS = 6
+HALF_UP = 1920
+AB_COPIES = 15
+PAIR_COPIES = 11
+
+
+def back_linked_kernel(
+    q, k, v, d, o, side, kb, xt, xa, xb,
+    dq, cont, own, gq, gk, gv, qrow, ga, gb,
+    qx, qd, kx, vx, dx, qm, kt, pt, st, pc, sc, bown, bcont, acc,
+    a_mine, a_x, a_y, a_z, a_q, b_mine, b_y, b_z, b_r,
+    p_mine, p_other, c_in, y_in, z_in, r_in, keys_low, k_in, k_far, k_x, dw,
+    lsem, ab_send, ab_recv, p_send, p_recv,
+):
+    step = pl.program_id(0)
+    rep = lax.axis_index("rep")
+    shard = lax.axis_index("shard")
+    core = rep % 2
+    x = rep // 2
+    z = shard // 2
+    y = shard % 2
+    rep1 = rep + 1 - 2 * core
+    to_rep = [None, {"rep": rep1}, {"rep": (rep + 2) % 4}, {"rep": (rep1 + 2) % 4}]
+    to_y = {"shard": z * 2 + 1 - y}
+    zs = [z, z + 1 - 2 * (z % 2), (z + 2) % 4, 3 - z]
+    to_z = [None] + [{"shard": zs[j] * 2 + y} for j in range(1, 4)]
+
+    def move(src, dst, send, recv, where):
+        return pltpu.make_async_remote_copy(
+            src_ref=src, dst_ref=dst, send_sem=send, recv_sem=recv,
+            device_id=where, device_id_type=MESH,
+        )
+
+    def ab(index, src, dst, where):
+        return move(src, dst, ab_send.at[index], ab_recv.at[index], where)
+
+    def columns(which):
+        return pl.ds(pl.multiple_of(which * HALF_UP, 128), HALF_UP)
+
+    def copy_ax():
+        return ab(0, xa.at[:, :, columns(1 - x)], a_x, to_rep[2])
+
+    def copy_ay():
+        return ab(1, a_mine.at[pl.ds(4, 4)], a_y, to_y)
+
+    def copy_az(j):
+        return ab(1 + j, a_mine.at[j], a_z.at[j - 1], to_z[j])
+
+    def copy_aq(j):
+        return ab(4 + j, a_q.at[0], a_q.at[j], to_rep[j])
+
+    def copy_by():
+        return ab(8, xb.at[pl.ds(4, 4)], b_y, to_y)
+
+    def copy_bz(j):
+        return ab(8 + j, b_mine.at[j], b_z.at[j - 1], to_z[j])
+
+    def copy_br(j):
+        return ab(11 + j, b_r.at[0], b_r.at[j], to_rep[j])
+
+    def pair_copy(p, index, src, dst, where):
+        return move(src, dst, p_send.at[p, index], p_recv.at[p, index], where)
+
+    def copy_core(p):
+        return pair_copy(p, 0, p_other, c_in.at[p], to_rep[1])
+
+    def copy_y(p):
+        return pair_copy(p, 1, p_mine.at[p % 2, pl.ds(4, 4)], y_in.at[p], to_y)
+
+    def copy_z(p, j):
+        return pair_copy(p, 1 + j, p_mine.at[p % 2, j], z_in.at[p, j - 1], to_z[j])
+
+    def copy_rep(p, j):
+        return pair_copy(p, 4 + j, r_in.at[p, 0], r_in.at[p, j], to_rep[j])
+
+    def copy_near(p):
+        return pair_copy(p, 8, keys_low.at[p % 2, pl.ds(512, 512)], k_in.at[p], to_rep[1])
+
+    def copy_far(p):
+        return pair_copy(p, 9, keys_low.at[p % 2, pl.ds(1536, 512)], k_far.at[p], to_rep[1])
+
+    def copy_turn(p):
+        return pair_copy(p, 10, keys_low.at[p % 2, pl.ds(1024, 512)], k_x.at[p], to_rep[2])
+
+    def add(left, right):
+        return (left.astype(f32) + right.astype(f32)).astype(bf16)
+
+    def after_core(p):
+        slot = p % 2
+        copy_core(p).wait()
+        for i in range(8):
+            p_mine[slot, i] = add(p_mine[slot, i], c_in[p, i])
+        copy_y(p).start()
+        copy_near(p).wait()
+        copy_far(p).wait()
+        keys_low[slot, 1024:1536] = add(keys_low[slot, 1024:1536], k_far[p])
+        copy_turn(p).start()
+
+    def after_y(p):
+        slot = p % 2
+        copy_y(p).wait()
+        for i in range(4):
+            p_mine[slot, i] = add(p_mine[slot, i], y_in[p, i])
+        for j in range(1, 4):
+            copy_z(p, j).start()
+        copy_turn(p).wait()
+        total = keys_low[slot, :512].astype(f32) + k_in[p].astype(f32) + k_x[p].astype(f32)
+        own[:, pl.ds(pl.multiple_of(p * 256, 256), 256)] = total.astype(bf16)
+
+    def after_z(p):
+        slot = p % 2
+        for j in range(1, 4):
+            copy_z(p, j).wait()
+        total = p_mine[slot, 0].astype(f32)
+        for j in range(3):
+            total = total + z_in[p, j].astype(f32)
+        r_in[p, 0] = total.astype(bf16)
+        for j in range(1, 4):
+            copy_rep(p, j).start()
+
+    def after_rep(p):
+        for j in range(1, 4):
+            copy_rep(p, j).wait()
+        at = pl.ds(pl.multiple_of(p * 128, 128), 128)
+        for half, (one, two) in enumerate(((0, 2), (1, 3))):
+            total = add(r_in[p, one], r_in[p, two])
+            rows = core if half == 0 else 1 - core
+            rows = pl.ds(pl.multiple_of(rows * 48, 16), 48)
+            for j, out in enumerate((gq, gk, gv)):
+                out[rows, at] = total[:48, 128 * j : 128 * j + 128]
+            if half == 0:
+                qrow[:, at] = total[48:64, :128]
+
+    @pl.when(step == 0)
+    def _():
+        barrier = pltpu.get_barrier_semaphore()
+        for place in to_rep[1:] + [to_y] + to_z[1:]:
+            pl.semaphore_signal(barrier, inc=1, device_id=place, device_id_type=MESH)
+        pl.semaphore_wait(barrier, 7)
+        copy_by().start()
+        copy_ax().start()
+        for copy in (
+            pltpu.make_async_copy(xa.at[:, :, columns(x)], a_mine, lsem.at[0]),
+            pltpu.make_async_copy(xb.at[pl.ds(0, 4)], b_mine, lsem.at[1]),
+        ):
+            copy.start()
+
+    back_fill(q, k, v, d, o, side, kb, qx, qd, kx, vx, dx, qm, kt, bown, bcont)
+    turned = []
+    turned.append(back_head(0, qx, qd, kx, vx, dx, qm, kt, pt, st, pc, sc, bown, bcont))
+    back_keys(0, dx, qm, pt, st, pc, sc, acc)
+
+    @pl.when(step > 0)
+    def _():
+        after_core(step - 1)
+
+    @pl.when(step > 1)
+    def _():
+        after_z(step - 2)
+
+    @pl.when(step == 2)
+    def _():
+        copy_ax().wait()
+        pltpu.make_async_copy(xa.at[:, :, columns(x)], a_mine, lsem.at[0]).wait()
+
+        def sum_piece(i, carry):
+            a_mine[i] = add(a_mine[i], a_x[i])
+            return carry
+
+        lax.fori_loop(0, 8, sum_piece, 0)
+        copy_ay().start()
+
+    @pl.when(step == 3)
+    def _():
+        copy_ay().wait()
+
+        def sum_piece(i, carry):
+            a_mine[i] = add(a_mine[i], a_y[i])
+            return carry
+
+        lax.fori_loop(0, 4, sum_piece, 0)
+        for j in range(1, 4):
+            copy_az(j).start()
+
+    turned.append(back_head(1, qx, qd, kx, vx, dx, qm, kt, pt, st, pc, sc, bown, bcont))
+    back_keys(1, dx, qm, pt, st, pc, sc, acc)
+
+    @pl.when(step > 0)
+    def _():
+        after_y(step - 1)
+
+    @pl.when(step > 1)
+    def _():
+        after_rep(step - 2)
+
+    @pl.when(step == 1)
+    def _():
+        copy_by().wait()
+        pltpu.make_async_copy(xb.at[pl.ds(0, 4)], b_mine, lsem.at[1]).wait()
+
+        def sum_piece(i, carry):
+            b_mine[i] = add(b_mine[i], b_y[i])
+            return carry
+
+        lax.fori_loop(0, 4, sum_piece, 0)
+        for j in range(1, 4):
+            copy_bz(j).start()
+
+    @pl.when(step == 3)
+    def _():
+        for j in range(1, 4):
+            copy_bz(j).wait()
+        total = b_mine[0].astype(f32)
+        for j in range(3):
+            total = total + b_z[j].astype(f32)
+        b_r[0] = total.astype(bf16)
+        for j in range(1, 4):
+            copy_br(j).start()
+
+    @pl.when(step == 4)
+    def _():
+        for j in range(1, 4):
+            copy_br(j).wait()
+        gb[core] = add(b_r[0], b_r[2])
+        gb[1 - core] = add(b_r[1], b_r[3])
+        for j in range(1, 4):
+            copy_az(j).wait()
+        total = a_mine[0].astype(f32)
+        for j in range(3):
+            total = total + a_z[j].astype(f32)
+        a_q[0] = total.astype(bf16)
+        for j in range(1, 4):
+            copy_aq(j).start()
+
+    delta = jnp.transpose(jnp.concatenate(turned, axis=0) * SCALE)
+    low = delta.astype(bf16)
+    dq[...] = low
+    slot = step % 2
+    keys_low[slot] = acc[:2048].astype(bf16)
+    tail = acc[2048:].astype(bf16)
+    cont[...] = tail
+    copy_near(step).start()
+    copy_far(step).start()
+    grad = dot(xt[:, :512], low[:512], NN) + dot(xt[:, 2048:], low[512:], NN)
+    dw[:, :128] = grad.astype(bf16)
+    dw[:, 128:] = (dot(xt[:, :2048], keys_low[slot], NN) + dot(xt[:, 2048:], tail, NN)).astype(bf16)
+    extra = jnp.sum(low.astype(f32), axis=0, keepdims=True)
+    extra = jnp.concatenate([jnp.broadcast_to(extra, (16, 128)), jnp.zeros((16, 256), f32)], axis=1)
+    extra = extra.astype(bf16)
+    for i in range(8):
+        place = (zs[i % 4] * 2 + (y if i < 4 else 1 - y)) * 2
+        at = pl.multiple_of((place + core) * 48, 16)
+        p_mine[slot, i, :48] = dw[pl.ds(at, 48)]
+        p_mine[slot, i, 48:] = extra
+        at = pl.multiple_of((place + 1 - core) * 48, 16)
+        p_other[i, :48] = dw[pl.ds(at, 48)]
+        p_other[i, 48:] = extra
+    copy_core(step).start()
+
+    @pl.when(step == PAIRS - 1)
+    def _():
+        after_z(PAIRS - 2)
+        after_core(PAIRS - 1)
+        for j in range(1, 4):
+            copy_aq(j).wait()
+        for j, (rows, which) in enumerate(
+            ((core, x), (1 - core, x), (core, 1 - x), (1 - core, 1 - x))
+        ):
+            rows = pl.ds(pl.multiple_of(rows * 48, 16), 48)
+            ga[rows, columns(which)] = a_q[j]
+        after_y(PAIRS - 1)
+        after_rep(PAIRS - 2)
+        after_z(PAIRS - 1)
+        after_rep(PAIRS - 1)
+
+
+def attend_back(q, k, v, d, o, side, kb, xt, xa, xb):
+    width = q.shape[1]
+    count = width // 128
+    full = xa.shape[2]
+
+    def held(*shape):
+        return pl.BlockSpec(shape, lambda i: (0,) * len(shape), pipeline_mode=pl.Buffered(1))
+
+    def vm(*shape):
+        return pltpu.VMEM(shape, bf16)
+
+    def out(*shape):
+        return jax.ShapeDtypeStruct(shape, bf16)
+
+    sem = pltpu.SemaphoreType.DMA
+    piece = (64, 384)
+    return pl.pallas_call(
+        back_linked_kernel,
+        grid=(count,),
+        in_specs=back_specs() + [ANY, ANY],
+        out_specs=[
+            pl.BlockSpec((1024, 128), lambda i: (0, i)),
+            pl.BlockSpec((512, 256), lambda i: (0, i)),
+            held(512, 2 * width), held(96, width), held(96, width), held(96, width),
+            held(16, width), held(96, full), held(2, 208, width),
         ],
-        compiler_params=params(),
-        cost_estimate=cost(14.0 * count, 5 * count),
-    )(q, k, v, d, o, side, kb)
+        out_shape=[
+            out(1024, width), out(512, 2 * width), out(512, 2 * width), out(96, width),
+            out(96, width), out(96, width), out(16, width), out(96, full), out(2, 208, width),
+        ],
+        scratch_shapes=BACK_SCRATCH
+        + [
+            vm(8, 48, HALF_UP), vm(8, 48, HALF_UP), vm(4, 48, HALF_UP), vm(3, 48, HALF_UP),
+            vm(4, 48, HALF_UP), vm(4, 208, width), vm(4, 208, width), vm(3, 208, width),
+            vm(4, 208, width),
+            vm(2, 8, *piece), vm(8, *piece), vm(PAIRS, 8, *piece), vm(PAIRS, 4, *piece),
+            vm(PAIRS, 3, *piece), vm(PAIRS, 4, *piece), vm(2, 2048, 256), vm(PAIRS, 512, 256),
+            vm(PAIRS, 512, 256), vm(PAIRS, 512, 256), vm(width, 384),
+            sem((2,)), sem((AB_COPIES,)), sem((AB_COPIES,)), sem((PAIRS, PAIR_COPIES)),
+            sem((PAIRS, PAIR_COPIES)),
+        ],
+        compiler_params=params(62, collective_id=2, has_side_effects=True),
+        cost_estimate=cost(100, 40),
+    )(q, k, v, d, o, side, kb, xt, xa, xb)
 
 
 def gelu_parts(x):
@@ -639,7 +998,7 @@
 
 
 def forward_back_kernel(
-    order, m0, m1, m2, tok, cot, teach, keep, scale, vecs, upb,
+    order, mixed, tok, cot, teach, keep, scale, vecs, upb,
     ua, ub, uc, ud, da, db, dc, dd,
     result, hid_o, act_o, ddel_o, udel_o, adel_o, mdel_o, sums,
     wa, wu, wd, slope, sems,
@@ -684,9 +1043,7 @@
         sums[index : index + 1] += jnp.sum(values, axis=0, keepdims=True)
 
     x = tok[...].astype(f32)
-    branch = attn_b + x
-    for g, part in enumerate((m0, m1, m2)):
-        branch = branch + dot(part[...], wa[256 * g : 256 * g + 256], NN)
+    branch = attn_b + x + dot(mixed[...], wa[...], NN)
     normed1, inv1 = normed_of(branch)
     hidden = normed1 * gain1 + shift1
     hid_low = hidden.astype(bf16)
@@ -723,7 +1080,9 @@
     adel = grad1.astype(bf16)
     adel_o[...] = adel
     add_sum(3, adel.astype(f32))
-    mdel_o[...] = dot(adel, wa[...], NT).astype(bf16)
+    mdel = dot(adel, wa[...], NT).astype(bf16)
+    mdel_o[...] = mdel
+    add_sum(7, mdel.astype(f32))
 
 
 def forward_back(order, mixed, tok, cot, teach, keep, scale, vecs, upb, ups, downs):
@@ -746,7 +1105,7 @@
             num_scalar_prefetch=1,
             grid=(rows // half,),
             in_specs=[
-                block(256), block(256), block(256), block(width), block(width), block(width),
+                block(width), block(width), block(width), block(width),
                 block(128), fixed(1, 1), fixed(8, width), fixed(1, hidden_units),
             ] + [ANY] * 8,
             out_specs=[
@@ -767,139 +1126,116 @@
         ],
         compiler_params=params(60),
         cost_estimate=cost(32.6, 30),
-    )(order, *mixed, tok, cot, teach, keep, scale, vecs, upb, *ups, *downs)
+    )(order, mixed, tok, cot, teach, keep, scale, vecs, upb, *ups, *downs)
+
+
+def up_grad_kernel(order, mixed, adel, hid, udel, mine, other, whole):
+    step = pl.program_id(0)
+
+    @pl.when(step == 0)
+    def _():
+        whole[...] = dot(mixed[...], adel[...], TN).astype(bf16)
+
+    @pl.when(step > 0)
+    def _():
+        whole[...] = dot(hid[...], udel[...], TN).astype(bf16)
+
+    store_pieces(order, whole, mine, other, 48)
 
 
 def store_pieces(order, source, mine, other, piece):
     for i in range(8):
         at = pl.multiple_of(order[i] * piece, 16)
-        mine[i] = source[pl.ds(at, piece)]
+        mine[i, :piece] = source[pl.ds(at, piece)]
         at = pl.multiple_of(order[i + 8] * piece, 16)
-        other[i] = source[pl.ds(at, piece)]
-
-
-def weight_grad_kernel(order, *refs, count, piece):
-    lefts, right = refs[:count], refs[count]
-    mine, other, whole = refs[count + 1 :]
-    at = 0
-    for left in lefts:
-        size = left.shape[1]
-        whole[at : at + size] = dot(left[...], right[...], TN).astype(bf16)
-        at += size
-    store_pieces(order, whole, mine, other, piece)
-
-
-def weight_grad(order, lefts, right, chunk):
-    rows, columns = right.shape
-    total = sum(left.shape[1] for left in lefts)
-    piece = total // 16
-    shape = jax.ShapeDtypeStruct((8, piece, columns), bf16)
-    out = pl.BlockSpec((8, piece, chunk), lambda i, *_: (0, 0, i))
+        other[i, :piece] = source[pl.ds(at, piece)]
+
+
+def up_grad(order, mixed, adel, hid, udel):
+    rows, width = adel.shape
+    columns = udel.shape[1]
+    shape = jax.ShapeDtypeStruct((8, 48, width + columns), bf16)
+    out = pl.BlockSpec((8, 48, width), lambda i, *_: (0, 0, i))
+    full = pl.BlockSpec((rows, width), lambda i, *_: (0, 0))
     return pl.pallas_call(
-        functools.partial(weight_grad_kernel, count=len(lefts), piece=piece),
+        up_grad_kernel,
+        grid_spec=pltpu.PrefetchScalarGridSpec(
+            num_scalar_prefetch=1,
+            grid=(1 + columns // width,),
+            in_specs=[
+                full, full, full,
+                pl.BlockSpec((rows, width), lambda i, *_: (0, jnp.maximum(i - 1, 0))),
+            ],
+            out_specs=[out, out],
+            scratch_shapes=[pltpu.VMEM((width, width), bf16)],
+        ),
+        out_shape=[shape, shape],
+        compiler_params=params(),
+        cost_estimate=cost(6, 20),
+    )(order, mixed, adel, hid, udel)
+
+
+def down_grad_kernel(order, act, ddel, sums, mine, other, whole):
+    whole[...] = dot(act[...], ddel[...], TN).astype(bf16)
+    store_pieces(order, whole, mine, other, 192)
+    low = sums[...].astype(bf16)
+    for i in range(8):
+        mine[i, 192:] = low
+        other[i, 192:] = low
+
+
+def down_grad(order, act, ddel, sums):
+    rows, columns = ddel.shape
+    total = act.shape[1]
+    chunk = 256
+    shape = jax.ShapeDtypeStruct((8, 208, columns), bf16)
+    out = pl.BlockSpec((8, 208, chunk), lambda i, *_: (0, 0, i))
+    return pl.pallas_call(
+        down_grad_kernel,
         grid_spec=pltpu.PrefetchScalarGridSpec(
             num_scalar_prefetch=1,
             grid=(columns // chunk,),
-            in_specs=[pl.BlockSpec(left.shape, lambda i, *_: (0, 0)) for left in lefts]
-            + [pl.BlockSpec((rows, chunk), lambda i, *_: (0, i))],
+            in_specs=[
+                pl.BlockSpec(act.shape, lambda i, *_: (0, 0)),
+                pl.BlockSpec((rows, chunk), lambda i, *_: (0, i)),
+                pl.BlockSpec((16, chunk), lambda i, *_: (0, i)),
+            ],
             out_specs=[out, out],
             scratch_shapes=[pltpu.VMEM((total, chunk), bf16)],
         ),
         out_shape=[shape, shape],
         compiler_params=params(),
-        cost_estimate=cost(2e-9 * rows * total * columns, 10),
-    )(order, *lefts, right)
-
-
-def project_grad_kernel(order, tok, oth, dq, dkv, mine, other, sums, whole):
-    cols = dq.shape[1]
-    whole[:, :cols] = dot(tok[...], dq[...], TN).astype(bf16)
-    for j in range(2):
-        total = dot(oth[...], dkv[j, 512:2048], TN)
-        total = total + dot(tok[:512], dkv[j, :512], TN)
-        total = total + dot(tok[512:], dkv[j, 2048:], TN)
-        whole[:, cols * (j + 1) : cols * (j + 2)] = total.astype(bf16)
-    store_pieces(order, whole, mine, other, 48)
-    sums[...] = jnp.zeros_like(sums)
-    sums[0:1] = jnp.sum(dq[...].astype(f32), axis=0, keepdims=True)
-    sums[1:2] = jnp.sum(dkv[1].astype(f32), axis=0, keepdims=True)
-
-
-def project_grad(order, tok, oth, dq, dkv):
-    width = tok.shape[1]
-    cols = dq.shape[1]
-
-    def fixed(shape):
-        return pl.BlockSpec(shape, lambda i, *_: (0,) * len(shape))
-
-    piece = (8, 48, 3 * cols)
-    return pl.pallas_call(
-        project_grad_kernel,
-        grid_spec=pltpu.PrefetchScalarGridSpec(
-            num_scalar_prefetch=1,
-            grid=(1,),
-            in_specs=[fixed(tok.shape), fixed(oth.shape), fixed(dq.shape), fixed(dkv.shape)],
-            out_specs=[fixed(piece), fixed(piece), fixed((8, cols))],
-            scratch_shapes=[pltpu.VMEM((width, 3 * cols), bf16)],
-        ),
-        out_shape=[
-            jax.ShapeDtypeStruct(piece, bf16), jax.ShapeDtypeStruct(piece, bf16),
-            jax.ShapeDtypeStruct((8, cols), f32),
-        ],
-        compiler_params=params(),
-        cost_estimate=cost(2.5, 12),
-    )(order, tok, oth, dq, dkv)
-
-
-def tokens_grad_kernel(adel, *refs):
-    parts, (wq, wk, wv, out) = refs[:-4], refs[-4:]
-    for half in range(2):
+        cost_estimate=cost(5, 20),
+    )(order, act, ddel, sums)
+
+
+def tokens_grad_kernel(adel, dq, own, cont, wq, wk, wv, out):
+    for half, low in enumerate((own, cont)):
         rows = slice(512 * half, 512 * half + 512)
-        total = adel[rows].astype(f32)
-        for g in range(3):
-            dq, own, cont = parts[3 * g : 3 * g + 3]
-            cols = slice(256 * g, 256 * g + 256)
-            low = own if half == 0 else cont
-            total = total + dot(dq[rows], wq[:, cols], NT)
-            total = total + dot(low[0], wk[:, cols], NT)
-            total = total + dot(low[1], wv[:, cols], NT)
+        total = adel[rows].astype(f32) + dot(dq[rows], wq[...], NT)
+        for p in range(wq.shape[1] // 128):
+            cols = slice(128 * p, 128 * p + 128)
+            both = jnp.concatenate([wk[:, cols], wv[:, cols]], axis=1)
+            total = total + dot(low[:, 256 * p : 256 * p + 256], both, NT)
         out[rows] = total.astype(bf16)
 
 
-def tokens_grad(adel, parts, wq, wk, wv):
-    def fixed(shape):
-        return pl.BlockSpec(shape, lambda i: (0,) * len(shape))
-
-    specs, flat = [], []
-    for dq, own, dkv in parts:
-        specs += [
-            fixed(dq.shape), fixed(own.shape),
-            pl.BlockSpec((2, 512, dkv.shape[2]), lambda i: (0, 4, 0)),
-        ]
-        flat += [dq, own, dkv]
+def tokens_grad(adel, dq, own, cont, wq, wk, wv):
+    args = (adel, dq, own, cont, wq, wk, wv)
     return pl.pallas_call(
         tokens_grad_kernel,
         grid=(1,),
-        in_specs=[fixed(adel.shape)] + specs + [fixed(wq.shape)] * 3,
-        out_specs=fixed(adel.shape),
+        in_specs=[pl.BlockSpec(a.shape, lambda i: (0, 0)) for a in args],
+        out_specs=pl.BlockSpec(adel.shape, lambda i: (0, 0)),
         out_shape=jax.ShapeDtypeStruct(adel.shape, bf16),
         compiler_params=params(),
         cost_estimate=cost(3.6, 12),
-    )(adel, *flat, wq, wk, wv)
+    )(*args)
 
 
 def swap(values, axis, bit):
     size = lax.axis_size(axis)
     return lax.ppermute(values, axis, [(i, i ^ bit) for i in range(size)])
-
-
-def sum_all(values):
-    for axis in ("rep", "shard"):
-        bit = 1
-        while bit < lax.axis_size(axis):
-            values = values + swap(values, axis, bit)
-            bit *= 2
-    return values
 
 
 def local(
@@ -928,7 +1264,7 @@
         second_shift, up_bias,
     ]
     part = query_bias.shape[0]
-    vec = jnp.concatenate(small)
+    vec = jnp.concatenate([v[None] for v in small], axis=1)[0]
     keep_low = keep[:PPIECE].astype(f32).reshape(4, 128)
     if split:
         keep_low = jnp.concatenate([keep_low, keep_low])
@@ -975,7 +1311,7 @@
         full = lax.all_gather(down_weight, "shard", axis=0, tiled=True).reshape(4, 4, 192, width)
         downs = [full[j] for j in range(4)]
 
-    q, k, v, qn, kn = project(tok, oth, wq, wk, wv, vecs[0:1], vecs[1:2])
+    q, k, v, xt, qn, kn = project(tok, oth, wq, wk, wv, vecs[0:1], vecs[1:2])
     all_keep = jnp.concatenate(
         [keep[:PPIECE].astype(f32), others_keep, keep[PPIECE:].astype(f32)]
     )
@@ -985,9 +1321,10 @@
     kb = jnp.where(lane == 0, bias[:, None], jnp.where(lane < 4, 1.0, 0.0)).astype(bf16)
     groups = 3
     pairs = width // 128 // groups
-    mixed, sides = zip(
-        *[attend(q, k, v, kb, brow, qn, kn, g * pairs, pairs) for g in range(groups)]
-    )
+    outs = ()
+    for g in range(groups):
+        outs = attend(q, k, v, kb, brow, qn, kn, outs, g * pairs, pairs)
+    mixed, sides = outs
 
     keep_wide = jnp.broadcast_to(keep.astype(f32)[:, None], (rows, 128))
     scale = (1.0 / valid_count.astype(f32)).reshape(1, 1)
@@ -995,55 +1332,42 @@
         order, mixed, tok, cotangent.reshape(rows, width), teacher.reshape(rows, width),
         keep_wide, scale, vecs, upb, ups, downs,
     )
-    down_pieces = weight_grad(order, [act], ddel, 256)
-    up_pieces = weight_grad(order, [hid], udel, 512)
-    attn_pieces = weight_grad(order, mixed, adel, 256)
-
-    def scatter(mine, other):
-        if not split:
-            piece, columns = mine.shape[1:]
-            full = jnp.concatenate([mine, other]).reshape(16 * piece, columns)
-            part = lax.psum_scatter(full, "shard", scatter_dimension=0, tiled=True)
+    down_mine, down_other = down_grad(order, act, ddel, sums)
+    up_mine, up_other = up_grad(order, mixed, adel, hid, udel)
+    if split:
+        down_sum = (down_mine.astype(f32) + swap(down_other, "rep", 1).astype(f32)).astype(bf16)
+        up_sum = (up_mine.astype(f32) + swap(up_other, "rep", 1).astype(f32)).astype(bf16)
+        dq, cont, own, query_low, key_low, value_low, qrow, up_low, down_low = attend_back(
+            q, k, v, mdel, mixed, sides, kb, xt, up_sum, down_sum
+        )
+        query_grad, key_grad, value_grad = [g.astype(f32) for g in (query_low, key_low, value_low)]
+        up_all = up_low.astype(f32)
+        down_all = down_low[:, :192].astype(f32).reshape(-1, width)
+        sums = down_low[0, 192:].astype(f32)
+        query_row = qrow[0].astype(f32)
+    else:
+        dq, cont, partial_rows, whole = attend_back_alone(q, k, v, mdel, mixed, sides, kb, xt)
+
+        def scatter(part):
+            part = lax.psum_scatter(part, "shard", scatter_dimension=0, tiled=True)
             return lax.psum(part, "rep").astype(f32)
-        got = mine.astype(f32) + swap(other, "rep", 1).astype(f32)
-        got = got.astype(bf16)
-        got = got[:4].astype(f32) + swap(got[4:], "shard", 1).astype(f32)
-        got = got.astype(bf16)
-        total = got[0].astype(f32)
-        for d in (1, 2, 3):
-            total = total + swap(got[d], "shard", 2 * d).astype(f32)
-        total = total.astype(bf16)
-        first, second, third = [swap(total, "rep", bit).astype(f32) for bit in (1, 2, 3)]
-        own, twin = total.astype(f32) + second, first + third
-        return jnp.where(
-            core == 0, jnp.concatenate([own, twin]), jnp.concatenate([twin, own])
+
+        def joined(mine, other, piece):
+            return jnp.concatenate([mine, other])[:, :piece].reshape(16 * piece, -1)
+
+        turned = partial_rows.reshape(2, 2, PPIECE, -1)
+        turned = jnp.where(core == 1, turned[:, ::-1], turned)
+        turned = jnp.where(rep // 2 == 1, turned[::-1], turned)
+        own = lax.psum_scatter(
+            turned.reshape(4 * PPIECE, -1), "rep", scatter_dimension=0, tiled=True
         )
-
-    down_grad = scatter(*down_pieces)
-    up_grad = scatter(*up_pieces)
-    attn_grad = scatter(*attn_pieces)
-    sums = sum_all(sums)
-
-    parts, pieces, tails = [], [], []
-    for g in range(groups):
-        dq, dkv = attend_back(q, k, v, mdel, mixed[g], sides[g], kb, g * pairs, pairs)
-        pieces_mine, pieces_other, tail = project_grad(order, tok, oth, dq, dkv)
-        pieces.append(scatter(pieces_mine, pieces_other))
-        tails.append(tail)
-        near = swap(dkv[:, 512:1024], "rep", 1).astype(f32)
-        turn = swap(dkv[:, 1536:2048], "rep", 1).astype(f32)
-        turn = (turn + dkv[:, 1024:1536].astype(f32)).astype(bf16)
-        turn = swap(turn, "rep", 2).astype(f32)
-        own = (dkv[:, :512].astype(f32) + near + turn).astype(bf16)
-        parts.append((dq, own, dkv))
-    tails = sum_all(jnp.concatenate(tails, axis=1))
-    token_grad = tokens_grad(adel, parts, wq, wk, wv)
-
-    cols = width // groups
-    query_grad, key_grad, value_grad = [
-        jnp.concatenate([p[:, cols * j : cols * (j + 1)] for p in pieces], axis=1)
-        for j in range(3)
-    ]
+        whole = scatter(whole).reshape(part, width // 128, 3, 128)
+        query_grad, key_grad, value_grad = [whole[:, :, j].reshape(part, width) for j in range(3)]
+        up_all = scatter(joined(up_mine, up_other, 48))
+        down_all = scatter(joined(down_mine, down_other, 192))
+        sums = lax.psum(sums, ("rep", "shard"))
+        query_row = lax.psum(jnp.sum(dq.astype(f32), axis=0), ("rep", "shard"))
+    token_grad = tokens_grad(adel, dq, own, cont, wq, wk, wv)
 
     def owned(row):
         return lax.dynamic_slice(row, (shard * part,), (part,))
@@ -1055,17 +1379,17 @@
         loss,
         token_grad.reshape(tokens.shape),
         query_grad,
-        owned(tails[0]),
+        owned(query_row),
         key_grad,
         value_grad,
-        owned(tails[1]),
-        attn_grad,
+        owned(sums[7]),
+        up_all[:, :width],
         owned(sums[3]),
         owned(sums[4]),
         owned(sums[5]),
-        up_grad,
+        up_all[:, width:],
         lax.dynamic_slice(sums[8:12].reshape(-1), (shard * up_part,), (up_part,)),
-        down_grad,
+        down_all,
         owned(sums[0]),
         owned(sums[1]),
         owned(sums[2]),

time: 613 us -> 449 us (0.73)
  waiting for transfers between devices: 146 us -> 19.3 us
  starting transfers between devices: 109 us -> 12.4 us
  Pallas kernels: 294 us -> 370 us
  local copies, waits for them, and re-layouts: 29.9 us -> 20.6 us
  other arithmetic: 26.5 us -> 17.5 us
    ppermute x79 -> x14, waiting for transfers between devices: 146 us -> 19.3 us  [swap(): return lax.ppermute(values, axis, [(i, i ^ bit) for i in range(size)])]
    ppermute x79 -> x14, starting transfers between devices: 109 us -> 12.4 us  [swap(): return lax.ppermute(values, axis, [(i, i ^ bit) for i in range(size)])]
    pallas_call x13 -> x7, Pallas kernels: 204 us -> 281 us  [the longest x1 151 us: attend_back(): pl.pallas_call(back_linked_kernel, grid=(count,), in_specs=back_specs() +...]
    convert_element_type x24 -> x6, other arithmetic: 15.8 us -> 10.1 us  [the longest x1 4.8 us: local(): (down_mine.astype(f32) + swap(down_other, 'rep', 1).astype(f32)).astype(b...]
  transfers between devices with their start and end apart: 79 -> 14, of which waited for: 33 -> 3; matrix products, arithmetic and copies ran while one was open for 6% -> 3% of each run, Pallas kernels for 36% -> 28%
where the time goes in v2:
time: 449 us; the launch traced here: 444 us
  Pallas kernels  370 us (82%)
  local copies, waits for them, and re-layouts  20.6 us (5%)
  waiting for transfers between devices  19.3 us (4%)
  other arithmetic  17.5 us (4%)
  starting transfers between devices  12.4 us (3%)
    pallas_call x1, Pallas kernels, attend_back(): pl.pallas_call(back_linked_kernel, grid=(count,), in_specs=back_specs() +...  151 us
    pallas_call x3, Pallas kernels, attend(): pl.pallas_call(kernel, grid=(count,), in_specs=[pair(1024), pair(2560), p...  96.3 us
    pallas_call x1, Pallas kernels, forward_back(): pl.pallas_call(forward_back_kernel, grid_spec=pltpu.PrefetchScalarGridSpe...  47.1 us
    pallas_call x1, Pallas kernels, first_gather(): pl.pallas_call(gather_kernel, in_specs=[ANY] * 6, out_specs=[ANY] * 6, ou...  27.6 us
    ppermute x14, waiting for transfers between devices, swap(): return lax.ppermute(values, axis, [(i, i ^ bit) for i in range(size)])  19.3 us
    pallas_call x1, Pallas kernels, project(): pl.pallas_call(project_kernel, grid=(5,), in_specs=[pl.BlockSpec(block, l...  14.7 us
    pallas_call x1, Pallas kernels, up_grad(): pl.pallas_call(up_grad_kernel, grid_spec=pltpu.PrefetchScalarGridSpec(num...  12.9 us
    ppermute x14, starting transfers between devices, swap(): return lax.ppermute(values, axis, [(i, i ^ bit) for i in range(size)])  12.4 us
  transfers between devices with their start and end apart: 14, of which 3 were waited for; matrix products, arithmetic and copies ran while one was open for 3% of the time, Pallas kernels for 28%

profile of v2, /device:TPU:0, one launch (start us, length us, event | category | flops | bytes accessed | tf_op | source)
XLA Modules:
  0.0 443.7 jit_solution(7908003153104698171)
XLA Ops:
  0.7 0.8 slice_convert_fusion.1
  1.5 0.7 broadcast_in_dim.89
  2.2 0.9 concatenate.22
  3.1 1.1 pad_maximum_fusion.2
  4.3 1.4 copy-done.2
  5.7 27.6 %shard_map.331 = (bf16[16,48,768]{2,1,0:T(8,128)(2,1)S(1)}, bf16[16,48,768]{2,1,0:T(8,128)(2,1)S(1)}, bf16[16,48,768]{2,1,0:T(8,128)(2,1)S(1)}, bf16[8,16,128]{2...) custom-call(bf16[2,48,768]{2,1,0:T(8,128)(2,1)S(1)} %bitcast.77, ...), custom_call_target="tpu_custom_call" | custom-call | bytes 20000000 | tf_op jit(solution)/shard_map/pallas_call | solution.py:255
  33.3 1.4 copy-done.6
  34.7 1.0 copy-done.7
  35.7 1.0 copy-done.8
  36.8 1.0 copy-done.9
  37.8 1.7 collective-permute-start
  39.5 2.5 collective-permute-start.1
  42.3 0.7 fusion.20
  43.0 0.7 collective-permute-start.6
  43.7 3.4 collective-permute-start.7
  47.3 0.7 slice.84.qb
  47.9 0.7 slice.86.vb
  48.6 1.3 select_convert_fusion.refs_3_.kb
  49.9 14.7 %shard_map.332 = (bf16[1024,768]{1,0:T(8,128)(2,1)}, bf16[2560,768]{1,0:T(8,128)(2,1)}, bf16[2560,768]{1,0:T(8,128)(2,1)}, bf16[768,2560]{1,0:T(8,128)(2,1)}, f32[8,128]{1,0:T(8,128)}, /*index=5*/f32[8,128]{1,0:T(8,128)}) custom-call(bf16[1024,768]{1,0:T(8,128)(2,1)} %bitcast.74, bf16[1536,768]{1,0:T(8,128)(2,1)} %bitcast.81, bf16[768,768]{1,0:T(8,128)(2,1)} %bitcast.82, ...), custom_call_target="tpu_custom_call" | custom-call | flops 7500000256 | bytes 20000000 | tf_op jit(solution)/shard_map/pallas_call | solution.py:323
  64.6 0.6 broadcast_in_dim.97.refs_4_.brow
  65.3 32.0 %shard_map.333 = (bf16[1024,768]{1,0:T(8,128)(2,1)}, bf16[12,1024,128]{2,1,0:T(8,128)(2,1)}) custom-call(bf16[1024,768]{1,0:T(8,128)(2,1)} %get-tuple-element.66.refs_0_.q, bf16[2560,768]{1,0:T(8,128)(2,1)} %get-tuple-element.67.refs_1_.k, bf16[2560,768]{1,0:T(8,128)(2,1)} %get-tuple-element.68.refs_2_.v, bf16[2560,128]{1,0:T(8,128)(2,1)} %select_convert_fusion.refs_3_.kb, ...), custom_call_target="tpu_custom_call" | custom-call | flops 14000000000 | bytes 6000000 | tf_op jit(solution)/shard_map/pallas_call | solution.py:470
  98.5 7.7 %collective-permute-done.8 = bf16[192,768]{1,0:T(8,128)(2,1)S(1)} collective-permute-done((bf16[192,768]{1,0:T(8,128)(2,1)}, bf16[192,768]{1,0:T(8,128)(2,1)S(1)}, u32[]{:S(2)}, u32[]{:S(2)}) %collective-permute-start.8) | collective-permute-done | bytes 294944 | tf_op jit(solution)/shard_map/ppermute | solution.py:1238
  106.2 1.1 pad_maximum_fusion.1.da
  107.3 1.7 collective-permute-start.9
  109.1 32.1 %shard_map.334 = (bf16[1024,768]{1,0:T(8,128)(2,1)}, bf16[12,1024,128]{2,1,0:T(8,128)(2,1)}) custom-call(bf16[1024,768]{1,0:T(8,128)(2,1)} %get-tuple-element.66.refs_0_.q, bf16[2560,768]{1,0:T(8,128)(2,1)} %get-tuple-element.67.refs_1_.k, bf16[2560,768]{1,0:T(8,128)(2,1)} %get-tuple-element.68.refs_2_.v, ...), custom_call_target="tpu_custom_call", output_to_operand_aliasing={{0}: (7, {}), {1}: (8, {})} | custom-call | flops 14000000000 | bytes 6000000 | tf_op jit(solution)/shard_map/pallas_call | solution.py:470
  141.7 0.7 slice_bitcast_fusion
  142.4 0.7 reshape.236.vecs
  145.1 11.1 %collective-permute-done.9.db = bf16[4,192,768]{2,1,0:T(8,128)(2,1)} collective-permute-done((bf16[4,192,768]{2,1,0:T(8,128)(2,1)S(1)}, bf16[4,192,768]{2,1,0:T(8,128)(2,1)}, u32[]{:S(2)}, u32[]{:S(2)}) %collective-permute-start.9) | collective-permute-done | bytes 1179680 | tf_op jit(solution)/shard_map/ppermute | solution.py:1238
  156.2 32.2 %shard_map.335 = (bf16[1024,768]{1,0:T(8,128)(2,1)}, bf16[12,1024,128]{2,1,0:T(8,128)(2,1)}) custom-call(bf16[1024,768]{1,0:T(8,128)(2,1)} %get-tuple-element.66.refs_0_.q, bf16[2560,768]{1,0:T(8,128)(2,1)} %get-tuple-element.67.refs_1_.k, bf16[2560,768]{1,0:T(8,128)(2,1)} %get-tuple-element.68.refs_2_.v, ...), custom_call_target="tpu_custom_call", output_to_operand_aliasing={{0}: (7, {}), {1}: (8, {})} | custom-call | flops 14000000000 | bytes 6000000 | tf_op jit(solution)/shard_map/pallas_call | solution.py:470
  188.5 1.2 broadcast_in_dim.98.keep
  190.0 47.1 %shard_map.336 = (bf16[1024,768]{1,0:T(8,128)(2,1)}, bf16[1024,768]{1,0:T(8,128)(2,1)}, bf16[1024,3072]{1,0:T(8,128)(2,1)}, bf16[1024,768]{1,0:T(8,128)(2,1)}, b...) custom-call(s32[16]{0:T(128)} %fusion.2.order, ...), custom_call_target="tpu_custom_call" | custom-call | flops 32600000512 | bytes 30000000 | tf_op jit(solution)/shard_map/pallas_call | solution.py:1102
  237.1 11.4 %shard_map.338 = (bf16[8,208,768]{2,1,0:T(8,128)(2,1)}, bf16[8,208,768]{2,1,0:T(8,128)(2,1)}) custom-call(s32[16]{0:T(128)} %fusion.2.order, bf16[1024,3072]{1,0:T(8,128)(2,1)} %get-tuple-element.88.act, bf16[1024,768]{1,0:T(8,128)(2,1)} %get-tuple-element.89.ddel, f32[16,768]{1,0:T(8,128)} %get-tuple-element.90.sums), custom_call_target="tpu_custom_call" | custom-call | flops 5000000000 | bytes 20000000 | tf_op jit(solution)/shard_map/pallas_call | solution.py:1193
  248.5 12.9 %shard_map.337 = (bf16[8,48,3840]{2,1,0:T(8,128)(2,1)}, bf16[8,48,3840]{2,1,0:T(8,128)(2,1)}) custom-call(s32[16]{0:T(128)} %fusion.2.order, bf16[1024,768]{1,0:T(8,128)(2,1)} %get-tuple-element.76.mixed.o, bf16[1024,768]{1,0:T(8,128)(2,1)} %get-tuple-element.83.adel, bf16[1024,768]{1,0:T(8,128)(2,1)} %get-tuple-element.84.hid, ...), custom_call_target="tpu_custom_call" | custom-call | flops 6000000000 | bytes 20000000 | tf_op jit(solution)/shard_map/pallas_call | solution.py:1160
  261.9 4.8 %add_convert_fusion.1.xb = bf16[8,208,768]{2,1,0:T(8,128)(2,1)} fusion(bf16[8,208,768]{2,1,0:T(8,128)(2,1)} %collective-permute-done.13, bf16[8,208,768]{2,1,0:T(8,128)(2,1)} %get-tuple-element.91), kind=kLoop, calls=%fused_computation.1 | loop fusion | flops 5111808 | bytes 7667712 | tf_op jit(solution)/shard_map/convert_element_type | solution.py:1338
  267.2 2.3 add_convert_fusion.xa
  269.4 151.3 %shard_map.339 = (bf16[1024,768]{1,0:T(8,128)(2,1)}, bf16[512,1536]{1,0:T(8,128)(2,1)}, bf16[512,1536]{1,0:T(8,128)(2,1)}, bf16[96,768]{1,0:T(8,128)(2,1)}, bf16...) custom-call(bf16[1024,768]{1,0:T(8,128)(2,1)} %get-tuple-element.66., ...), custom_call_target="tpu_custom_call" | custom-call | flops 99999997952 | bytes 40000000 | tf_op jit(solution)/shard_map/pallas_call | solution.py:944
  420.7 0.8 slice_convert_fusion
  421.5 1.1 slice.100
  422.7 1.1 slice.114
  423.8 0.7 slice.110
  424.5 0.6 fusion.18
  425.1 1.1 bitcast_convert_fusion
  426.3 0.7 convert_element_type.101
  427.0 0.7 convert_element_type.102
  427.7 0.7 convert_element_type.99
  429.1 0.7 slice.92
  432.8 0.7 dynamic_slice.63
  433.4 8.9 %shard_map.340 = bf16[1024,768]{1,0:T(8,128)(2,1)} custom-call(bf16[1024,768]{1,0:T(8,128)(2,1)} %get-tuple-element.83.adel, bf16[1024,768]{1,0:T(8,128)(2,1)} %get-tuple-element.94.dq, bf16[512,1536]{1,0:T(8,128)(2,1)} %get-tuple-element.95.own, bf16[512,1536]{1,0:T(8,128)(2,1)} %get-tuple-element.96.cont, bf16[768,768]{1,0:T(8,128)(2,1)} %bitcast.83, ...), custom_call_target="tpu_custom_call" | custom-call | flops 3600000000 | bytes 12000000 | tf_op jit(solution)/shard_map/pallas_call | solution.py:1225
  (85 shorter events, 7.8 us)
Async XLA Ops:
  0.7 37.1 %copy-start = (bf16[384,768]{1,0:T(8,128)(2,1)S(1)}, bf16[384,768]{1,0:T(8,128)(2,1)}, u32[]{:S(2)}) copy-start(bf16[384,768]{1,0:T(8,128)(2,1)} %param.36) | copy-start | bytes 1769476
  0.7 3.6 copy-start.3
  0.7 3.6 copy-start.4
  0.7 3.6 copy-start.5
  4.3 1.4 copy-start.2
  33.3 1.4 copy-start.6
  34.7 1.0 copy-start.7
  35.7 1.0 copy-start.8
  36.8 1.0 copy-start.9
  37.8 59.5 %collective-permute-start = (bf16[48,3840]{1,0:T(8,128)(2,1)S(1)}, bf16[48,3840]{1,0:T(8,128)(2,1)S(1)}, u32[]{:S(2)}, u32[]{:S(2)}) collective-permute-start(bf16[48,3840]{1,0:T(8,128)(2,1)S(1)} %fusion.21), channel_id=1, source_target_pairs={{0,2},{1,3},{2,0},{3,1},{4,6},{5,7},{6,4},{7,5},{8,10},{9,11},{10,... | collective-permute-start | bytes 1105928 | tf_op jit(solution)/shard_map/ppermute | solution.py:1238
  39.5 58.2 %collective-permute-start.1 = (bf16[48,3840]{1,0:T(8,128)(2,1)S(1)}, bf16[48,3840]{1,0:T(8,128)(2,1)S(1)}, u32[]{:S(2)}, u32[]{:S(2)}) collective-permute-start(bf16[48,3840]{1,0:T(8,128)(2,1)S(1)} %fusion.21), channel_id=1, source_target_pairs={{0,4},{1,5},{2,6},{3,7},{4,0},{5,1},{6,2},{7,3},{8,12},{9,13},{10,... | collective-permute-start | bytes 1105928 | tf_op jit(solution)/shard_map/ppermute | solution.py:1238
  42.0 55.7 %collective-permute-start.2 = (bf16[48,3840]{1,0:T(8,128)(2,1)S(1)}, bf16[48,3840]{1,0:T(8,128)(2,1)S(1)}, u32[]{:S(2)}, u32[]{:S(2)}) collective-permute-start(bf16[48,3840]{1,0:T(8,128)(2,1)S(1)} %fusion.21), channel_id=1, source_target_pairs={{0,6},{1,7},{2,4},{3,5},{4,2},{5,3},{6,0},{7,1},{8,14},{9,15},{10,... | collective-permute-start | bytes 1105928 | tf_op jit(solution)/shard_map/ppermute | solution.py:1238
  43.0 55.4 %collective-permute-start.6 = (bf16[192,768]{1,0:T(8,128)(2,1)}, bf16[192,768]{1,0:T(8,128)(2,1)S(1)}, u32[]{:S(2)}, u32[]{:S(2)}) collective-permute-start(bf16[192,768]{1,0:T(8,128)(2,1)} %fusion.20), channel_id=1, source_target_pairs={{0,2},{1,3},{2,0},{3,1},{4,6},{5,7},{6,4},{7,5},{8,10},{9,11},{10,... | collective-permute-start | bytes 884744 | tf_op jit(solution)/shard_map/ppermute | solution.py:1238
  43.7 54.8 %collective-permute-start.7 = (bf16[192,768]{1,0:T(8,128)(2,1)}, bf16[192,768]{1,0:T(8,128)(2,1)}, u32[]{:S(2)}, u32[]{:S(2)}) collective-permute-start(bf16[192,768]{1,0:T(8,128)(2,1)} %fusion.20), channel_id=1, source_target_pairs={{0,4},{1,5},{2,6},{3,7},{4,0},{5,1},{6,2},{7,3},{8,12},{9,13},{10,... | collective-permute-start | bytes 884744 | tf_op jit(solution)/shard_map/ppermute | solution.py:1238
  47.1 1.5 copy-start.17
  97.3 8.9 %collective-permute-start.8 = (bf16[192,768]{1,0:T(8,128)(2,1)}, bf16[192,768]{1,0:T(8,128)(2,1)S(1)}, u32[]{:S(2)}, u32[]{:S(2)}) collective-permute-start(bf16[192,768]{1,0:T(8,128)(2,1)} %fusion.20), channel_id=1, source_target_pairs={{0,6},{1,7},{2,4},{3,5},{4,2},{5,3},{6,0},{7,1},{8,14},{9,15},{10,... | collective-permute-start | bytes 884744 | tf_op jit(solution)/shard_map/ppermute | solution.py:1238
  97.9 43.3 %copy-start.12 = (bf16[4,48,3840]{2,1,0:T(8,128)(2,1)}, bf16[4,48,3840]{2,1,0:T(8,128)(2,1)S(1)}, u32[]{:S(2)}) copy-start(bf16[4,48,3840]{2,1,0:T(8,128)(2,1)S(1)} %pad_maximum_fusion.ua) | copy-start | bytes 4423684
  97.9 43.4 %collective-permute-start.3 = (bf16[4,48,3840]{2,1,0:T(8,128)(2,1)S(1)}, bf16[4,48,3840]{2,1,0:T(8,128)(2,1)}, u32[]{:S(2)}, u32[]{:S(2)}) collective-permute-start(bf16[4,48,3840]{2,1,0:T(8,128)(2,1)S(1)} %pad_maximum_fusion.ua), channel_id=1, source_target_pairs={{0,1},{1,0},{2,3},{3,2},{4,5},{5,4},{6,7},{7,6},{8,9},{9,8},{10,11... | collective-permute-start | bytes 4423688 | tf_op jit(solution)/shard_map/ppermute | solution.py:1238
  107.3 37.6 %copy-start.13 = (bf16[4,192,768]{2,1,0:T(8,128)(2,1)}, bf16[4,192,768]{2,1,0:T(8,128)(2,1)S(1)}, u32[]{:S(2)}) copy-start(bf16[4,192,768]{2,1,0:T(8,128)(2,1)S(1)} %pad_maximum_fusion.1.da) | copy-start | bytes 3538948
  107.3 48.9 %collective-permute-start.9 = (bf16[4,192,768]{2,1,0:T(8,128)(2,1)S(1)}, bf16[4,192,768]{2,1,0:T(8,128)(2,1)}, u32[]{:S(2)}, u32[]{:S(2)}) collective-permute-start(bf16[4,192,768]{2,1,0:T(8,128)(2,1)S(1)} %pad_maximum_fusion.1.da), channel_id=1, source_target_pairs={{0,1},{1,0},{2,3},{3,2},{4,5},{5,4},{6,7},{7,6},{8,9},{9,8},{10,11... | collective-permute-start | bytes 3538952 | tf_op jit(solution)/shard_map/ppermute | solution.py:1238
  109.1 34.0 %copy-start.18 = (s32[1,1,1024]{2,1,0:T(1,128)S(1)}, s32[1,1,1024]{2,1,0:T(1,128)}, u32[]{:S(2)}) copy-start(s32[1,1,1024]{2,1,0:T(1,128)} %param.23) | copy-start | bytes 12292
  141.2 47.3 %collective-permute-start.4 = (bf16[4,48,3840]{2,1,0:T(8,128)(2,1)S(1)}, bf16[4,48,3840]{2,1,0:T(8,128)(2,1)}, u32[]{:S(2)}, u32[]{:S(2)}) collective-permute-start(bf16[4,48,3840]{2,1,0:T(8,128)(2,1)S(1)} %pad_maximum_fusion.ua), channel_id=1, source_target_pairs={{0,8},{8,0},{16,24},{24,16},{1,9},{9,1},{17,25},{25,17},{2,10},{10... | collective-permute-start | bytes 4423688 | tf_op jit(solution)/shard_map/ppermute | solution.py:1238
  141.3 47.2 %collective-permute-start.5 = (bf16[4,48,3840]{2,1,0:T(8,128)(2,1)}, bf16[4,48,3840]{2,1,0:T(8,128)(2,1)}, u32[]{:S(2)}, u32[]{:S(2)}) collective-permute-start(bf16[4,48,3840]{2,1,0:T(8,128)(2,1)} %collective-permute-done.3.ub), channel_id=1, source_target_pairs={{0,8},{8,0},{16,24},{24,16},{1,9},{9,1},{17,25},{25,17},{2,10},{10... | collective-permute-start | bytes 4423688 | tf_op jit(solution)/shard_map/ppermute | solution.py:1238
  145.0 43.4 %collective-permute-start.10 = (bf16[4,192,768]{2,1,0:T(8,128)(2,1)S(1)}, bf16[4,192,768]{2,1,0:T(8,128)(2,1)S(1)}, u32[]{:S(2)}, u32[]{:S(2)}) collective-permute-start(bf16[4,192,768]{2,1,0:T(8,128)(2,1)S(1)} %pad_maximum_fusion.1.da), channel_id=1, source_target_pairs={{0,8},{8,0},{16,24},{24,16},{1,9},{9,1},{17,25},{25,17},{2,10},{10... | collective-permute-start | bytes 3538952 | tf_op jit(solution)/shard_map/ppermute | solution.py:1238
  156.2 32.2 %collective-permute-start.11 = (bf16[4,192,768]{2,1,0:T(8,128)(2,1)}, bf16[4,192,768]{2,1,0:T(8,128)(2,1)S(1)}, u32[]{:S(2)}, u32[]{:S(2)}) collective-permute-start(bf16[4,192,768]{2,1,0:T(8,128)(2,1)} %collective-permute-done.9.db), channel_id=1, source_target_pairs={{0,8},{8,0},{16,24},{24,16},{1,9},{9,1},{17,25},{25,17},{2,10},{10... | collective-permute-start | bytes 3538952 | tf_op jit(solution)/shard_map/ppermute | solution.py:1238
  188.4 1.3 copy-start.19
  188.4 1.6 copy-start.20
  248.5 13.4 %collective-permute-start.13 = (bf16[8,208,768]{2,1,0:T(8,128)(2,1)}, bf16[8,208,768]{2,1,0:T(8,128)(2,1)}, u32[]{:S(2)}, u32[]{:S(2)}) collective-permute-start(bf16[8,208,768]{2,1,0:T(8,128)(2,1)} %get-tuple-element.92), channel_id=1, source_target_pairs={{0,8},{8,0},{16,24},{24,16},{1,9},{9,1},{17,25},{25,17},{2,10},{10... | collective-permute-start | bytes 7667720 | tf_op jit(solution)/shard_map/ppermute | solution.py:1238
  261.4 5.7 %collective-permute-start.12 = (bf16[8,48,3840]{2,1,0:T(8,128)(2,1)}, bf16[8,48,3840]{2,1,0:T(8,128)(2,1)S(1)}, u32[]{:S(2)}, u32[]{:S(2)}) collective-permute-start(bf16[8,48,3840]{2,1,0:T(8,128)(2,1)} %get-tuple-element.87), channel_id=1, source_target_pairs={{0,8},{8,0},{16,24},{24,16},{1,9},{9,1},{17,25},{25,17},{2,10},{10... | collective-permute-start | bytes 8847368 | tf_op jit(solution)/shard_map/ppermute | solution.py:1238
  261.9 5.2 %copy-start.10 = (bf16[8,48,3840]{2,1,0:T(8,128)(2,1)S(1)}, bf16[8,48,3840]{2,1,0:T(8,128)(2,1)}, u32[]{:S(2)}) copy-start(bf16[8,48,3840]{2,1,0:T(8,128)(2,1)} %get-tuple-element.86) | copy-start | bytes 8847364
  420.7 1.9 copy-start.11
  423.8 2.5 copy-start.16
  423.8 3.2 copy-start.15
  423.8 4.0 copy-start.14
  433.4 8.9 %copy-start.1 = (bf16[384,768]{1,0:T(8,128)(2,1)S(1)}, bf16[384,768]{1,0:T(8,128)(2,1)}, u32[]{:S(2)}) copy-start(bf16[384,768]{1,0:T(8,128)(2,1)} %param.36) | copy-start | bytes 1769476
